TPU v7x, 128 devices: a whole 4x4x4 slice. The times are simulated.
128 devices in a mesh: section: 4 (over z), table: 32 (over x, y, core).
Axes of the slice: x: 4, y: 4, z: 4, core: 2. Of those that a mesh axis runs over, the one named last changes fastest.
Arguments:
- saved_inputs: bfloat16 [4, 4, 2048, 4096], P('section', None, 'table'), may hold values from -6 to 6
- memory: bfloat16 [4, 4, 2048, 8, 1024], P('section', None, 'table'), may hold values from -6 to 6
- value_weight: bfloat16 [4, 8, 1024, 512], P('section'), may hold values from -0.1875 to 0.1875
- conv_weight: float32 [4, 4, 4, 4096], P('section'), may hold values from -3 to 3
- norm_gain: float32 [4, 4, 4096], P('section'), may hold values from 0.25 to 1.75
- layer_counts: int32 [4], P('section'), may hold values from 1 to 4
- row_ids: int32 [4, 4, 2048, 8], P('section', None, 'table'), may hold values from 0 to 32767, as said below
- out_grad: bfloat16 [4, 2048, 4096], P(None, 'table'), may hold values from -6 to 6
Outputs:
- section_grads: bfloat16 [4, 4, 2048, 4096], P('section', None, 'table')
- table_grad: float32 [4, 32768, 1024], P('section', 'table')
Inputs may be any that keep to these rules, and one draw needn't show every extreme that they name: `row_ids`: the owner of a row id is id // 1024. In every section and micro-batch, at most 24 of the ids of the 64 tokens of one index of table fall to one owner.
All inputs are finite; a program needn't handle non-finite values.
Results may differ from a plain program's by a relative error of at most 0.0062.
Values may be sent and summed in bfloat16 or wider, within the bound.
No kernel may reach another device: no remote copies, remote signals or barrier semaphores. Data moves between devices by JAX's collectives and lax.ppermute only.
A program may use at most 256 MiB of HBM per device.

v0:
```python
import math

import jax
import jax.numpy as jnp
from jax import lax
from jax.sharding import PartitionSpec as P

TABLE_DEV = 1024


epsilon = 1e-06


def shifted(block, axis, distance):
    devices = range(lax.axis_size(axis))
    route = [(i - distance, i) for i in devices if i - distance in devices]
    return lax.ppermute(block, axis, route)


def rms_unit(values):
    return values * lax.rsqrt(jnp.mean(values * values, -1, keepdims=True) + epsilon)


def gate_mix(inputs, values):
    score = jnp.sum(rms_unit(inputs) * rms_unit(values), -1, keepdims=True) / math.sqrt(
        inputs.shape[-1]
    )
    return inputs + jax.nn.sigmoid(score) * values


def forward_taps(before, normed, kernel_taps):
    width = kernel_taps.shape[0]
    length = normed.shape[0]
    padded = jnp.concatenate([before, normed], 0)
    mixed = kernel_taps[0] * padded[width - 1 : width - 1 + length]
    for offset in range(1, width):
        mixed = (
            mixed + kernel_taps[offset] * padded[width - 1 - offset : width - 1 - offset + length]
        )
    return mixed


def backward_taps(grad_mix, after, kernel_taps):
    width = kernel_taps.shape[0]
    length = grad_mix.shape[0]
    padded = jnp.concatenate([grad_mix, after], 0)
    result = kernel_taps[0] * padded[0:length]
    for offset in range(1, width):
        result = result + kernel_taps[offset] * padded[offset : offset + length]
    return result


def section_backward(inputs_b, memory_b, grad_out, weight, convs, gains, live_layers):
    length = inputs_b.shape[0]
    width = convs.shape[1]
    values = jnp.einsum(
        "thr,hrc->thc", memory_b, weight, preferred_element_type=jnp.float32
    ).reshape(length, -1)
    inputs = inputs_b.astype(jnp.float32)
    hidden = gate_mix(inputs, values)
    saved = []
    for layer in range(convs.shape[0]):
        normed = rms_unit(hidden) * gains[layer]
        before = shifted(normed[length - (width - 1) :], "table", 1)
        mixed = forward_taps(before, normed, convs[layer])
        saved.append((hidden, mixed))
        hidden = jnp.where(layer < live_layers, hidden + jax.nn.silu(mixed), hidden)
    grad_now = grad_out
    for layer in reversed(range(convs.shape[0])):
        hidden, mixed = saved[layer]
        sigma = jax.nn.sigmoid(mixed)
        grad_mix = grad_now * sigma * (1.0 + mixed * (1.0 - sigma))
        after = shifted(grad_mix[: width - 1], "table", -1)
        grad_norm = backward_taps(grad_mix, after, convs[layer])
        gain = gains[layer]
        pull = jax.vjp(lambda state: rms_unit(state) * gain, hidden)[1]
        grad_now = jnp.where(layer < live_layers, grad_now + pull(grad_norm)[0], grad_now)
    pull = jax.vjp(gate_mix, inputs, values)[1]
    grad_in, grad_values = pull(grad_now)
    heads = memory_b.shape[1]
    grad_values = grad_values.astype(jnp.bfloat16).reshape(length, heads, -1)
    return (grad_in, grad_values)


def pack_rows(payload, ids_batch, active, owners, capacity, heads):
    feature = payload.shape[-1]
    flat_ids = ids_batch.reshape(-1)
    owner_of = flat_ids // TABLE_DEV
    local_row = flat_ids - owner_of * TABLE_DEV
    head_of = jnp.arange(flat_ids.shape[0], dtype=jnp.int32) % heads
    member = (owner_of[:, None] == jnp.arange(owners, dtype=jnp.int32)[None, :]).astype(jnp.int32)
    slot_of = jnp.sum((jnp.cumsum(member, 0) - member) * member, 1)
    send_rows = (
        jnp.zeros((owners, capacity, feature), payload.dtype).at[owner_of, slot_of].set(payload)
    )
    send_index = (
        jnp.full((owners, capacity), TABLE_DEV, jnp.int32)
        .at[owner_of, slot_of]
        .set(jnp.where(active, local_row, TABLE_DEV))
    )
    send_head = jnp.zeros((owners, capacity), jnp.int32).at[owner_of, slot_of].set(head_of)
    return (send_rows, send_index, send_head)


def owner_add(table_sum, got_rows, got_index):
    row_width = got_rows.shape[-1]
    flat_index = got_index.reshape(-1)
    flat_rows = got_rows.reshape(-1, row_width)
    return table_sum.at[flat_index].add(flat_rows, mode="drop")


def owner_receive(table_sum, received):
    got_rows, got_index = received
    return owner_add(table_sum, got_rows, got_index)


def shards(
    saved_inputs, memory, value_weight, conv_weight, norm_gain, layer_counts, row_ids, out_grad
):
    section_now = lax.axis_index("section")
    sections = lax.axis_size("section")
    owners = lax.axis_size("table")
    batches, length, width_model = out_grad.shape
    heads = memory.shape[3]
    row_width = memory.shape[4]
    capacity = 3 * length * heads // (2 * owners)
    weight = value_weight[0]
    convs = conv_weight[0]
    gains = norm_gain[0]
    live_layers = layer_counts[0]
    is_top = section_now == sections - 1
    arriving = jnp.zeros((length, width_model), jnp.bfloat16)
    grads_all = jnp.zeros((batches, length, width_model), jnp.bfloat16)
    table_sum = jnp.zeros((TABLE_DEV, row_width), jnp.float32)
    last_tick = batches + sections - 2
    for timestep in range(batches + sections - 1):
        position = timestep - (sections - 1 - section_now)
        active = (position >= 0) & (position < batches)
        which = jnp.clip(position, 0, batches - 1)
        inputs_b = lax.dynamic_index_in_dim(saved_inputs[0], which, 0, keepdims=False)
        memory_b = lax.dynamic_index_in_dim(memory[0], which, 0, keepdims=False)
        top_grad = lax.dynamic_index_in_dim(out_grad, which, 0, keepdims=False)
        grad_out = jnp.where(is_top, top_grad, arriving).astype(jnp.float32)
        grad_in, grad_values = section_backward(
            inputs_b, memory_b, grad_out, weight, convs, gains, live_layers
        )
        grad_send = grad_in.astype(jnp.bfloat16)
        previous = lax.dynamic_index_in_dim(grads_all, which, 0, keepdims=False)
        grads_all = lax.dynamic_update_index_in_dim(
            grads_all, jnp.where(active, grad_send, previous), which, 0
        )
        ids_batch = lax.dynamic_index_in_dim(row_ids[0], which, 0, keepdims=False)
        row_grads = jnp.einsum(
            "thc,hrc->thr", grad_values, weight, preferred_element_type=jnp.float32
        )
        send_rows, send_index, send_head = pack_rows(
            row_grads.reshape(length * heads, row_width), ids_batch, active, owners, capacity, heads
        )
        outgoing = (send_rows, send_index)
        received = (
            lax.all_to_all(outgoing[0], "table", split_axis=0, concat_axis=0, tiled=True),
            lax.all_to_all(outgoing[1], "table", split_axis=0, concat_axis=0, tiled=True),
        )
        table_sum = owner_receive(table_sum, received)
        if timestep < last_tick:
            arriving = shifted(grad_send, "section", -1)
    return (grads_all[None], table_sum[None])


def solution(mesh):
    placed = (
        P("section", None, "table", None),
        P("section", None, "table", None, None),
        P("section", None, None, None),
        P("section", None, None, None),
        P("section", None, None),
        P("section"),
        P("section", None, "table", None),
        P(None, "table", None),
    )
    return jax.shard_map(
        shards,
        mesh=mesh,
        in_specs=placed,
        out_specs=(P("section", None, "table", None), P("section", "table", None)),
        check_vma=False,
    )
```

profile of v0, /device:TPU:1, one launch (start us, length us, event | category | flops | bytes accessed | tf_op | source)
XLA Modules:
  0.0 1855.2 jit_solution(1582499416080707142)
XLA Ops:
  39.1 25.2 %scatter_fusion = s32[32,24]{0,1:T(8,128)S(1)} fusion(s32[32,24]{0,1:T(8,128)S(1)} %broadcast.2166.clone, s32[512]{0:T(512)S(1)} %bitcast.765, s32[512]{0:T(512)S(1)} %get-tuple-element.307), kind=kCustom, calls=%fused_computation | custom fusion | bytes 10240 | tf_op jit(solution)/shard_map/scatter | solution.py:99
  64.9 7.3 all-to-all-start
  76.1 6.9 fusion.569
  97.4 7.0 multiply_reduce_fusion.52
  115.2 7.2 multiply_reduce_fusion.51
  282.5 7.1 collective-permute-start.21
  331.5 7.6 collective-permute-done.24
  382.2 7.4 collective-permute-start.30
  432.2 6.3 collective-permute-done.33
  489.4 7.1 collective-permute-start.39
  566.3 6.4 collective-permute-start.45
  595.3 7.5 collective-permute-start.48
  604.5 25.2 %scatter_fusion.2 = s32[32,24]{0,1:T(8,128)S(1)} fusion(s32[32,24]{0,1:T(8,128)S(1)} %broadcast.2166.clone.1, s32[512]{0:T(512)S(1)} %bitcast.769, s32[512]{0:T(512)S(1)} %get-tuple-element.305), kind=kCustom, calls=%fused_computation.3 | custom fusion | bytes 10240 | tf_op jit(solution)/shard_map/scatter | solution.py:99
  630.3 25.2 %scatter_fusion.5 = s32[32,24]{0,1:T(8,128)S(1)} fusion(s32[32,24]{0,1:T(8,128)S(1)} %broadcast.2166.clone.2, s32[512]{0:T(512)S(1)} %bitcast.767, s32[512]{0:T(512)S(1)} %get-tuple-element.303), kind=kCustom, calls=%fused_computation.6 | custom fusion | bytes 10240 | tf_op jit(solution)/shard_map/scatter | solution.py:99
  656.2 25.2 %scatter_fusion.8 = s32[32,24]{0,1:T(8,128)S(1)} fusion(s32[32,24]{0,1:T(8,128)S(1)} %broadcast.2166.clone.3, s32[512]{0:T(512)S(1)} %bitcast.773, s32[512]{0:T(512)S(1)} %copy-done.194), kind=kCustom, calls=%fused_computation.9 | custom fusion | bytes 10240 | tf_op jit(solution)/shard_map/scatter | solution.py:99
  682.1 25.2 %scatter_fusion.11 = s32[32,24]{0,1:T(8,128)S(1)} fusion(s32[32,24]{0,1:T(8,128)S(1)} %broadcast.2166.clone.4, s32[512]{0:T(512)S(1)} %bitcast.771, s32[512]{0:T(512)S(1)} %copy-done.193), kind=kCustom, calls=%fused_computation.12 | custom fusion | bytes 10240 | tf_op jit(solution)/shard_map/scatter | solution.py:99
  707.9 25.2 %scatter_fusion.14 = s32[32,24]{0,1:T(8,128)S(1)} fusion(s32[32,24]{0,1:T(8,128)S(1)} %broadcast.2166.clone.5, s32[512]{0:T(512)S(1)} %bitcast.777, s32[512]{0:T(512)S(1)} %copy-done.196), kind=kCustom, calls=%fused_computation.15 | custom fusion | bytes 10240 | tf_op jit(solution)/shard_map/scatter | solution.py:99
  733.8 25.2 %scatter_fusion.17 = s32[32,24]{0,1:T(8,128)S(1)} fusion(s32[32,24]{0,1:T(8,128)S(1)} %broadcast.2166.clone.6, s32[512]{0:T(512)S(1)} %bitcast.775, s32[512]{0:T(512)S(1)} %copy-done.195), kind=kCustom, calls=%fused_computation.18 | custom fusion | bytes 10240 | tf_op jit(solution)/shard_map/scatter | solution.py:99
  776.7 74.6 %scatter_fusion.1 = f32[32,24,1024]{2,1,0:T(8,128)} fusion(f32[32,24,1024]{2,1,0:T(8,128)} %broadcast.2179.clone, s32[512]{0:T(512)S(1)} %bitcast.766, f32[512,1024]{1,0:T(8,128)} %bitcast.822), kind=kCustom, calls=%fused_computation.1 | custom fusion | bytes 6295552 | tf_op jit(solution)/shard_map/scatter | solution.py:94
  871.5 75.0 %scatter_fusion.3 = f32[32,24,1024]{2,1,0:T(8,128)} fusion(f32[32,24,1024]{2,1,0:T(8,128)} %broadcast.2179.clone.1, s32[512]{0:T(512)S(1)} %bitcast.770, f32[512,1024]{1,0:T(8,128)} %bitcast.823), kind=kCustom, calls=%fused_computation.4 | custom fusion | bytes 6295552 | tf_op jit(solution)/shard_map/scatter | solution.py:94
  946.5 24.8 %all-to-all-start.2 = ((s32[32,1,24]{2,1,0:T(1,128)}), s32[32,1,24]{2,1,0:T(1,128)S(1)}, u32[]{:S(2)}, u32[]{:S(2)}) async-start(s32[32,1,24]{2,1,0:T(1,128)} %copy.120), calls=%async_computation.2 | async-start | bytes 32768 | tf_op jit(solution)/shard_map/all_to_all | solution.py:162
  983.2 6.9 all-to-all-done.4
  1001.8 7.5 all-to-all-start.8
  1020.2 74.8 %scatter_fusion.6 = f32[32,24,1024]{2,1,0:T(8,128)} fusion(f32[32,24,1024]{2,1,0:T(8,128)} %broadcast.2179.clone.2, s32[512]{0:T(512)S(1)} %bitcast.768, f32[512,1024]{1,0:T(8,128)} %bitcast.824), kind=kCustom, calls=%fused_computation.7 | custom fusion | bytes 6295552 | tf_op jit(solution)/shard_map/scatter | solution.py:94
  1095.0 7.5 all-to-all-start.10
  1114.6 7.0 all-to-all-done.12
  1144.0 74.9 %scatter_fusion.9 = f32[32,24,1024]{2,1,0:T(8,128)} fusion(f32[32,24,1024]{2,1,0:T(8,128)} %broadcast.2179.clone.3, s32[512]{0:T(512)S(1)} %bitcast.774, f32[512,1024]{1,0:T(8,128)} %bitcast.825), kind=kCustom, calls=%fused_computation.10 | custom fusion | bytes 6295552 | tf_op jit(solution)/shard_map/scatter | solution.py:94
  1227.9 7.5 all-to-all-start.3
  1243.0 27.1 %collective-permute-done.54 = f32[3,4096]{1,0:T(4,128)S(1)} collective-permute-done((f32[3,4096]{1,0:T(4,128)S(1)}, f32[3,4096]{1,0:T(4,128)S(1)}, u32[]{:S(2)}, u32[]{:S(2)}) %collective-permute-start.54) | collective-permute-done | bytes 49184 | tf_op jit(solution)/shard_map/ppermute | solution.py:17
  1279.1 9.6 all-to-all-start.5
  1302.1 21.3 %collective-permute-done.56 = f32[3,4096]{1,0:T(4,128)S(1)} collective-permute-done((f32[3,4096]{1,0:T(4,128)S(1)}, f32[3,4096]{1,0:T(4,128)S(1)}, u32[]{:S(2)}, u32[]{:S(2)}) %collective-permute-start.56) | collective-permute-done | bytes 49184 | tf_op jit(solution)/shard_map/ppermute | solution.py:17
  1328.6 6.2 all-to-all-start.7
  1339.9 29.6 %collective-permute-done.57 = f32[3,4096]{1,0:T(4,128)S(1)} collective-permute-done((f32[3,4096]{1,0:T(4,128)S(1)}, f32[3,4096]{1,0:T(4,128)S(1)}, u32[]{:S(2)}, u32[]{:S(2)}) %collective-permute-start.57) | collective-permute-done | bytes 49184 | tf_op jit(solution)/shard_map/ppermute | solution.py:17
  1384.8 74.7 %scatter_fusion.12 = f32[32,24,1024]{2,1,0:T(8,128)} fusion(f32[32,24,1024]{2,1,0:T(8,128)} %broadcast.2179.clone.4, s32[512]{0:T(512)S(1)} %bitcast.772, f32[512,1024]{1,0:T(8,128)} %bitcast.826), kind=kCustom, calls=%fused_computation.13 | custom fusion | bytes 6295552 | tf_op jit(solution)/shard_map/scatter | solution.py:94
  1463.9 9.7 all-to-all-start.9
  1479.1 33.0 %collective-permute-done.59 = f32[3,4096]{1,0:T(4,128)S(1)} collective-permute-done((f32[3,4096]{1,0:T(4,128)S(1)}, f32[3,4096]{1,0:T(4,128)S(1)}, u32[]{:S(2)}, u32[]{:S(2)}) %collective-permute-start.59) | collective-permute-done | bytes 49184 | tf_op jit(solution)/shard_map/ppermute | solution.py:17
  1524.1 74.9 %scatter_fusion.15 = f32[32,24,1024]{2,1,0:T(8,128)} fusion(f32[32,24,1024]{2,1,0:T(8,128)} %broadcast.2179.clone.5, s32[512]{0:T(512)S(1)} %bitcast.778, f32[512,1024]{1,0:T(8,128)} %bitcast.827), kind=kCustom, calls=%fused_computation.16 | custom fusion | bytes 6295552 | tf_op jit(solution)/shard_map/scatter | solution.py:94
  1603.7 6.4 all-to-all-start.11
  1616.0 31.5 %collective-permute-done.61 = f32[3,4096]{1,0:T(4,128)S(1)} collective-permute-done((f32[3,4096]{1,0:T(4,128)S(1)}, f32[3,4096]{1,0:T(4,128)S(1)}, u32[]{:S(2)}, u32[]{:S(2)}) %collective-permute-start.61) | collective-permute-done | bytes 49184 | tf_op jit(solution)/shard_map/ppermute | solution.py:17
  1658.3 74.9 %scatter_fusion.18 = f32[32,24,1024]{2,1,0:T(8,128)} fusion(f32[32,24,1024]{2,1,0:T(8,128)} %broadcast.2179.clone.6, s32[512]{0:T(512)S(1)} %bitcast.776, f32[512,1024]{1,0:T(8,128)} %bitcast.828), kind=kCustom, calls=%fused_computation.19 | custom fusion | bytes 6295552 | tf_op jit(solution)/shard_map/scatter | solution.py:94
  1733.2 6.7 all-to-all-start.13
  1749.0 12.5 scatter_custom_fusion.2
  1764.7 14.6 scatter_fusion.4
  1781.9 14.5 scatter_fusion.7
  1796.4 14.7 scatter_fusion.10
  1811.1 14.5 scatter_fusion.13
  1825.5 14.7 scatter_fusion.16
  1840.3 14.5 scatter_fusion.19
  (1307 shorter events, 726.9 us)
Async XLA Ops:
  29.3 68.0 %collective-permute-start.9 = (f32[3,4096]{1,0:T(4,128)}, f32[3,4096]{1,0:T(4,128)}, u32[]{:S(2)}, u32[]{:S(2)}) collective-permute-start(f32[3,4096]{1,0:T(4,128)} %slice.1456), channel_id=1, source_target_pairs={{0,1},{1,2},{2,3},{3,4},{4,5},{5,6},{6,7},{7,8},{8,9},{9,10},{10,1... | collective-permute-start | bytes 147464 | tf_op jit(solution)/shard_map/ppermute | solution.py:17
  34.5 62.8 %collective-permute-start = (f32[3,4096]{1,0:T(4,128)}, f32[3,4096]{1,0:T(4,128)}, u32[]{:S(2)}, u32[]{:S(2)}) collective-permute-start(f32[3,4096]{1,0:T(4,128)} %slice.1416), channel_id=1, source_target_pairs={{0,1},{1,2},{2,3},{3,4},{4,5},{5,6},{6,7},{7,8},{8,9},{9,10},{10,1... | collective-permute-start | bytes 147464 | tf_op jit(solution)/shard_map/ppermute | solution.py:17
  64.9 881.6 %all-to-all-start = ((s32[32,1,24]{2,1,0:T(1,128)}), s32[32,1,24]{2,1,0:T(1,128)}, u32[]{:S(2)}, u32[]{:S(2)}) async-start(s32[32,1,24]{2,1,0:T(1,128)} %copy.112), calls=%async_computation | async-start | bytes 32768 | tf_op jit(solution)/shard_map/all_to_all | solution.py:162
  182.8 14.0 collective-permute-start.8
  271.5 8.0 collective-permute-start.20
  278.2 14.4 collective-permute-start.17
  282.5 8.8 collective-permute-start.21
  298.0 9.0 collective-permute-start.22
  327.7 11.4 collective-permute-start.24
  370.3 8.0 collective-permute-start.29
  377.1 16.4 collective-permute-start.26
  382.2 11.3 collective-permute-start.30
  415.1 8.5 collective-permute-start.32
  430.1 8.4 collective-permute-start.33
  483.5 16.9 collective-permute-start.35
  489.4 11.0 collective-permute-start.39
  505.8 7.8 collective-permute-start.40
  522.3 8.2 collective-permute-start.41
  538.0 8.0 collective-permute-start.42
  584.3 8.3 collective-permute-start.47
  591.3 168.4 %collective-permute-start.44 = (bf16[64,4096]{1,0:T(8,128)(2,1)}, bf16[64,4096]{1,0:T(8,128)(2,1)}, u32[]{:S(2)}, u32[]{:S(2)}) collective-permute-start(bf16[64,4096]{1,0:T(8,128)(2,1)} %get-tuple-element.73), channel_id=1, source_target_pairs={{32,0},{64,32},{96,64},{33,1},{65,33},{97,65},{34,2},{66,34},{98,6... | collective-permute-start | bytes 1572872 | tf_op jit(solution)/shard_map/ppermute | solution.py:17
  595.3 164.3 %collective-permute-start.48 = (f32[3,4096]{1,0:T(4,128)}, f32[3,4096]{1,0:T(4,128)}, u32[]{:S(2)}, u32[]{:S(2)}) collective-permute-start(f32[3,4096]{1,0:T(4,128)} %slice.1631), channel_id=1, source_target_pairs={{0,1},{1,2},{2,3},{3,4},{4,5},{5,6},{6,7},{7,8},{8,9},{9,10},{10,1... | collective-permute-start | bytes 147464 | tf_op jit(solution)/shard_map/ppermute | solution.py:17
  764.1 87.2 %collective-permute-start.49 = (f32[3,4096]{1,0:T(4,128)}, f32[3,4096]{1,0:T(4,128)}, u32[]{:S(2)}, u32[]{:S(2)}) collective-permute-start(f32[3,4096]{1,0:T(4,128)} %slice.1636), channel_id=1, source_target_pairs={{1,0},{2,1},{3,2},{4,3},{5,4},{6,5},{7,6},{8,7},{9,8},{10,9},{11,1... | collective-permute-start | bytes 147464 | tf_op jit(solution)/shard_map/ppermute | solution.py:17
  858.5 112.9 %collective-permute-start.50 = (f32[3,4096]{1,0:T(4,128)}, f32[3,4096]{1,0:T(4,128)}, u32[]{:S(2)}, u32[]{:S(2)}) collective-permute-start(f32[3,4096]{1,0:T(4,128)} %slice.1641), channel_id=1, source_target_pairs={{1,0},{2,1},{3,2},{4,3},{5,4},{6,5},{7,6},{8,7},{9,8},{10,9},{11,1... | collective-permute-start | bytes 147464 | tf_op jit(solution)/shard_map/ppermute | solution.py:17
  946.5 31.8 %all-to-all-start.2 = ((s32[32,1,24]{2,1,0:T(1,128)}), s32[32,1,24]{2,1,0:T(1,128)S(1)}, u32[]{:S(2)}, u32[]{:S(2)}) async-start(s32[32,1,24]{2,1,0:T(1,128)} %copy.120), calls=%async_computation.2 | async-start | bytes 32768 | tf_op jit(solution)/shard_map/all_to_all | solution.py:162
  978.3 11.8 all-to-all-start.4
  990.1 11.7 all-to-all-start.6
  999.5 103.1 %collective-permute-start.51 = (f32[3,4096]{1,0:T(4,128)}, f32[3,4096]{1,0:T(4,128)}, u32[]{:S(2)}, u32[]{:S(2)}) collective-permute-start(f32[3,4096]{1,0:T(4,128)} %slice.1646), channel_id=1, source_target_pairs={{1,0},{2,1},{3,2},{4,3},{5,4},{6,5},{7,6},{8,7},{9,8},{10,9},{11,1... | collective-permute-start | bytes 147464 | tf_op jit(solution)/shard_map/ppermute | solution.py:17
  1001.8 93.2 %all-to-all-start.8 = ((s32[32,1,24]{2,1,0:T(1,128)}), s32[32,1,24]{2,1,0:T(1,128)}, u32[]{:S(2)}, u32[]{:S(2)}) async-start(s32[32,1,24]{2,1,0:T(1,128)} %copy.144), calls=%async_computation.8 | async-start | bytes 32768 | tf_op jit(solution)/shard_map/all_to_all | solution.py:162
  1095.0 14.5 all-to-all-start.10
  1109.6 12.0 all-to-all-start.12
  1121.6 106.3 %all-to-all-start.1 = ((f32[32,24,1024]{2,1,0:T(8,128)}), f32[32,24,1024]{2,1,0:T(8,128)}, u32[]{:S(2)}, u32[]{:S(2)}) async-start(f32[32,24,1024]{2,1,0:T(8,128)} %scatter_fusion.1), calls=%async_computation.1 | async-start | bytes 6291456 | tf_op jit(solution)/shard_map/all_to_all | solution.py:161
  1131.1 87.8 %collective-permute-start.52 = (f32[3,4096]{1,0:T(4,128)}, f32[3,4096]{1,0:T(4,128)}, u32[]{:S(2)}, u32[]{:S(2)}) collective-permute-start(f32[3,4096]{1,0:T(4,128)} %slice.1651), channel_id=1, source_target_pairs={{1,0},{2,1},{3,2},{4,3},{5,4},{6,5},{7,6},{8,7},{9,8},{10,9},{11,1... | collective-permute-start | bytes 147464 | tf_op jit(solution)/shard_map/ppermute | solution.py:17
  1227.9 51.2 %all-to-all-start.3 = ((f32[32,24,1024]{2,1,0:T(8,128)}), f32[32,24,1024]{2,1,0:T(8,128)}, u32[]{:S(2)}, u32[]{:S(2)}) async-start(f32[32,24,1024]{2,1,0:T(8,128)} %scatter_fusion.3), calls=%async_computation.3 | async-start | bytes 6291456 | tf_op jit(solution)/shard_map/all_to_all | solution.py:161
  1237.5 32.6 %collective-permute-start.54 = (f32[3,4096]{1,0:T(4,128)S(1)}, f32[3,4096]{1,0:T(4,128)S(1)}, u32[]{:S(2)}, u32[]{:S(2)}) collective-permute-start(f32[3,4096]{1,0:T(4,128)S(1)} %slice.1656), channel_id=1, source_target_pairs={{0,1},{1,2},{2,3},{3,4},{4,5},{5,6},{6,7},{7,8},{8,9},{9,10},{10,1... | collective-permute-start | bytes 147464 | tf_op jit(solution)/shard_map/ppermute | solution.py:17
  1274.7 14.7 collective-permute-start.55
  1279.1 49.4 %all-to-all-start.5 = ((f32[32,24,1024]{2,1,0:T(8,128)}), f32[32,24,1024]{2,1,0:T(8,128)}, u32[]{:S(2)}, u32[]{:S(2)}) async-start(f32[32,24,1024]{2,1,0:T(8,128)} %scatter_fusion.6), calls=%async_computation.5 | async-start | bytes 6291456 | tf_op jit(solution)/shard_map/all_to_all | solution.py:161
  1295.6 27.9 %collective-permute-start.56 = (f32[3,4096]{1,0:T(4,128)S(1)}, f32[3,4096]{1,0:T(4,128)S(1)}, u32[]{:S(2)}, u32[]{:S(2)}) collective-permute-start(f32[3,4096]{1,0:T(4,128)S(1)} %slice.1666), channel_id=1, source_target_pairs={{0,1},{1,2},{2,3},{3,4},{4,5},{5,6},{6,7},{7,8},{8,9},{9,10},{10,1... | collective-permute-start | bytes 147464 | tf_op jit(solution)/shard_map/ppermute | solution.py:17
  1300.6 68.9 %collective-permute-start.53 = (bf16[64,4096]{1,0:T(8,128)(2,1)}, bf16[64,4096]{1,0:T(8,128)(2,1)}, u32[]{:S(2)}, u32[]{:S(2)}) collective-permute-start(bf16[64,4096]{1,0:T(8,128)(2,1)} %get-tuple-element.44), channel_id=1, source_target_pairs={{32,0},{64,32},{96,64},{33,1},{65,33},{97,65},{34,2},{66,34},{98,6... | collective-permute-start | bytes 1572872 | tf_op jit(solution)/shard_map/ppermute | solution.py:17
  1328.6 135.3 %all-to-all-start.7 = ((f32[32,24,1024]{2,1,0:T(8,128)}), f32[32,24,1024]{2,1,0:T(8,128)}, u32[]{:S(2)}, u32[]{:S(2)}) async-start(f32[32,24,1024]{2,1,0:T(8,128)} %scatter_fusion.9), calls=%async_computation.7 | async-start | bytes 6291456 | tf_op jit(solution)/shard_map/all_to_all | solution.py:161
  1336.2 33.3 %collective-permute-start.57 = (f32[3,4096]{1,0:T(4,128)S(1)}, f32[3,4096]{1,0:T(4,128)S(1)}, u32[]{:S(2)}, u32[]{:S(2)}) collective-permute-start(f32[3,4096]{1,0:T(4,128)S(1)} %slice.1671), channel_id=1, source_target_pairs={{0,1},{1,2},{2,3},{3,4},{4,5},{5,6},{6,7},{7,8},{8,9},{9,10},{10,1... | collective-permute-start | bytes 147464 | tf_op jit(solution)/shard_map/ppermute | solution.py:17
  1372.3 87.2 %collective-permute-start.58 = (f32[3,4096]{1,0:T(4,128)}, f32[3,4096]{1,0:T(4,128)}, u32[]{:S(2)}, u32[]{:S(2)}) collective-permute-start(f32[3,4096]{1,0:T(4,128)} %slice.1676), channel_id=1, source_target_pairs={{1,0},{2,1},{3,2},{4,3},{5,4},{6,5},{7,6},{8,7},{9,8},{10,9},{11,1... | collective-permute-start | bytes 147464 | tf_op jit(solution)/shard_map/ppermute | solution.py:17
  1463.9 139.8 %all-to-all-start.9 = ((f32[32,24,1024]{2,1,0:T(8,128)}), f32[32,24,1024]{2,1,0:T(8,128)}, u32[]{:S(2)}, u32[]{:S(2)}) async-start(f32[32,24,1024]{2,1,0:T(8,128)} %scatter_fusion.12), calls=%async_computation.9 | async-start | bytes 6291456 | tf_op jit(solution)/shard_map/all_to_all | solution.py:161
  1476.6 35.5 %collective-permute-start.59 = (f32[3,4096]{1,0:T(4,128)S(1)}, f32[3,4096]{1,0:T(4,128)S(1)}, u32[]{:S(2)}, u32[]{:S(2)}) collective-permute-start(f32[3,4096]{1,0:T(4,128)S(1)} %slice.1681), channel_id=1, source_target_pairs={{1,0},{2,1},{3,2},{4,3},{5,4},{6,5},{7,6},{8,7},{9,8},{10,9},{11,1... | collective-permute-start | bytes 147464 | tf_op jit(solution)/shard_map/ppermute | solution.py:17
  1514.5 84.6 %collective-permute-start.60 = (f32[3,4096]{1,0:T(4,128)S(1)}, f32[3,4096]{1,0:T(4,128)S(1)}, u32[]{:S(2)}, u32[]{:S(2)}) collective-permute-start(f32[3,4096]{1,0:T(4,128)S(1)} %slice.1686), channel_id=1, source_target_pairs={{1,0},{2,1},{3,2},{4,3},{5,4},{6,5},{7,6},{8,7},{9,8},{10,9},{11,1... | collective-permute-start | bytes 147464 | tf_op jit(solution)/shard_map/ppermute | solution.py:17
  1603.7 129.5 %all-to-all-start.11 = ((f32[32,24,1024]{2,1,0:T(8,128)}), f32[32,24,1024]{2,1,0:T(8,128)}, u32[]{:S(2)}, u32[]{:S(2)}) async-start(f32[32,24,1024]{2,1,0:T(8,128)} %scatter_fusion.15), calls=%async_computation.11 | async-start | bytes 6291456 | tf_op jit(solution)/shard_map/all_to_all | solution.py:161
  1613.0 34.5 %collective-permute-start.61 = (f32[3,4096]{1,0:T(4,128)S(1)}, f32[3,4096]{1,0:T(4,128)S(1)}, u32[]{:S(2)}, u32[]{:S(2)}) collective-permute-start(f32[3,4096]{1,0:T(4,128)S(1)} %slice.1691), channel_id=1, source_target_pairs={{1,0},{2,1},{3,2},{4,3},{5,4},{6,5},{7,6},{8,7},{9,8},{10,9},{11,1... | collective-permute-start | bytes 147464 | tf_op jit(solution)/shard_map/ppermute | solution.py:17
  1733.2 107.1 %all-to-all-start.13 = ((f32[32,24,1024]{2,1,0:T(8,128)}), f32[32,24,1024]{2,1,0:T(8,128)}, u32[]{:S(2)}, u32[]{:S(2)}) async-start(f32[32,24,1024]{2,1,0:T(8,128)} %scatter_fusion.18), calls=%async_computation.13 | async-start | bytes 6291456 | tf_op jit(solution)/shard_map/all_to_all | solution.py:161
  (388 other events, 2598.0 us)
where the time goes:
time: 1880 us; the launch traced here: 1860 us
  local copies, waits for them, and re-layouts  848 us (45%)
  other arithmetic  390 us (21%)
  starting transfers between devices  308 us (16%)
  waiting for transfers between devices  245 us (13%)
  matrix products  55.8 us (3%)
    scatter x7, local copies, waits for them, and re-layouts, pack_rows(): jnp.zeros((owners, capacity, feature), payload.dtype).at[owner_of, slot_of]  524 us
    ppermute x62, waiting for transfers between devices, shifted(): return lax.ppermute(block, axis, route)  223 us
    ppermute x62, starting transfers between devices, shifted(): return lax.ppermute(block, axis, route)  195 us
    scatter x7, local copies, waits for them, and re-layouts, pack_rows(): send_index = jnp.full((owners, capacity), TABLE_DEV, jnp.int32).at[owner_...  176 us
    scatter-add x7, other arithmetic, owner_add(): return table_sum.at[flat_index].add(flat_rows, mode='drop')  100 us
    reduce_sum x34, other arithmetic, rms_unit(): values * lax.rsqrt(jnp.mean(values * values, -1, keepdims=True) + epsilon)  84.3 us
    mul x28, other arithmetic, section_backward(): grad_mix = grad_now * sigma * (1.0 + mixed * (1.0 - sigma))  69.6 us
    all_to_all x7, starting transfers between devices, shards(): lax.all_to_all(outgoing[1], 'table', split_axis=0, concat_axis=0, tiled=T...  61.3 us
  transfers between devices with their start and end apart: 76, of which 41 were waited for; matrix products, arithmetic and copies ran while one was open for 65% of the time, Pallas kernels for 0%

commit v1 on v0

v1 whole, which is shorter than its diff:
```python
import functools
import math

import jax
import jax.numpy as jnp
from jax import lax
from jax.experimental import pallas as pl
from jax.experimental.pallas import tpu as pltpu
from jax.sharding import PartitionSpec as P

TABLE_DEV = 1024
HALO = 16
EPS = 1e-06
LANES = 128
MIB = 1 << 20

f32 = jnp.float32
bf16 = jnp.bfloat16


def row_total(partial):
    return jnp.broadcast_to(jnp.sum(partial, -1, keepdims=True), partial.shape)


def columns(chunk):
    return pl.ds(pl.multiple_of(chunk * LANES, LANES), LANES)


def forward_kernel(
    live_ref, xb, xm, xa, vb, vm, va, taps, hid_out, der_out, scal_out,
    x_win, v_win, hid, der, scal, rms_now, sems,
):
    width = xm.shape[-1]
    rows = x_win.shape[0]
    keep = rows - HALO
    chunks = width // LANES
    live = live_ref[0]
    length = xm.shape[-2]

    def load(chunk, sums):
        cols = columns(chunk)
        for ref, at, size in ((xb, 0, HALO), (xm, HALO, length), (xa, HALO + length, HALO)):
            x_win[at : at + size, cols] = ref[0, :, cols].astype(f32)
        for ref, at, size in ((vb, 0, HALO), (vm, HALO, length), (va, HALO + length, HALO)):
            v_win[at : at + size, cols] = ref[0, :, cols]
        x = x_win[:, cols]
        v = v_win[:, cols]
        return sums[0] + x * x, sums[1] + v * v, sums[2] + x * v

    zero = jnp.zeros((rows, LANES), f32)
    xx, vv, xv = lax.fori_loop(0, chunks, load, (zero, zero, zero))
    xv = row_total(xv)
    rx = lax.rsqrt(row_total(xx) / width + EPS)
    rv = lax.rsqrt(row_total(vv) / width + EPS)
    gate = jax.nn.sigmoid(rx * rv * xv / math.sqrt(width))
    scal[4] = rx[HALO:]
    scal[5] = rv[HALO:]
    scal[6] = xv[HALO:]
    scal[7] = gate[HALO:]
    rms_now[...] = gate

    def mix(chunk, total):
        cols = columns(chunk)
        hidden = x_win[:, cols] + rms_now[...] * v_win[:, cols]
        hid[0, :, cols] = hidden
        return total + hidden * hidden

    total = lax.fori_loop(0, chunks, mix, zero)

    def hidden_copy(layer):
        return pltpu.make_async_copy(
            hid.at[layer, pl.ds(HALO, keep)], hid_out.at[layer], sems.at[0, layer]
        )

    def slope_copy(layer):
        return pltpu.make_async_copy(der.at[layer], der_out.at[layer], sems.at[1, layer])

    def layer_step(layer, total):
        hidden_copy(layer).start()
        rms = lax.rsqrt(row_total(total) / width + EPS)
        scal[layer] = rms[HALO:]
        rms_now[...] = rms

        def one(chunk, total):
            cols = columns(chunk)
            hidden = hid[layer, :, cols]
            unit = hidden * rms_now[...]
            mixed = taps[layer, 0:1, cols] * unit
            for k in range(1, 4):
                mixed = mixed + taps[layer, k : k + 1, cols] * pltpu.roll(unit, k, 0)
            sigma = 0.5 * jnp.tanh(0.5 * mixed) + 0.5
            silu = mixed * sigma
            der[layer, :, cols] = (sigma + silu * (1.0 - sigma))[HALO:]
            after = hidden + silu
            hid[layer + 1, :, cols] = after
            return total + after * after

        total = lax.fori_loop(0, chunks, one, zero)
        slope_copy(layer).start()
        return total

    lax.fori_loop(0, live, layer_step, total)
    out = pltpu.make_async_copy(scal, scal_out, sems.at[0, 4])
    out.start()

    def finish(layer, carry):
        hidden_copy(layer).wait()
        slope_copy(layer).wait()
        return carry

    lax.fori_loop(0, live, finish, 0)
    out.wait()


def forward_map(batch, live, x, x_before, x_after, v, v_before, v_after, taps):
    length, width = x.shape[1:]
    keep = length + HALO
    rows = keep + HALO
    layers = taps.shape[0]

    def part(size):
        return pl.BlockSpec((1, size, width), lambda i, *_: (batch, 0, 0))

    return pl.pallas_call(
        forward_kernel,
        out_shape=(
            jax.ShapeDtypeStruct((layers, keep, width), f32),
            jax.ShapeDtypeStruct((layers, keep, width), f32),
            jax.ShapeDtypeStruct((8, keep, LANES), f32),
        ),
        grid_spec=pltpu.PrefetchScalarGridSpec(
            num_scalar_prefetch=1,
            grid=(1,),
            in_specs=[
                part(HALO), part(length), part(HALO),
                part(HALO), part(length), part(HALO),
                pl.BlockSpec(taps.shape, lambda i, *_: (0, 0, 0)),
            ],
            out_specs=[pl.BlockSpec(memory_space=pl.ANY)] * 3,
            scratch_shapes=[
                pltpu.VMEM((rows, width), f32),
                pltpu.VMEM((rows, width), f32),
                pltpu.VMEM((layers + 1, rows, width), f32),
                pltpu.VMEM((layers, keep, width), f32),
                pltpu.VMEM((8, keep, LANES), f32),
                pltpu.VMEM((rows, LANES), f32),
                pltpu.SemaphoreType.DMA((2, layers + 1)),
            ],
        ),
        compiler_params=pltpu.CompilerParams(vmem_limit_bytes=44 * MIB),
        cost_estimate=pl.CostEstimate(flops=30 * layers * rows * width, bytes_accessed=16 * MIB, transcendentals=layers * rows * width),
        name="forward_map",
    )(live, x_before, x, x_after, v_before, v, v_after, taps)


def backward_kernel(
    held, info, near, near_halo, top, top_halo, x_all, xa_all, v_all, va_all, taps, *refs,
):
    saved = [refs[3 * i : 3 * i + 3] for i in range(held[1])]
    refs = refs[3 * held[1] :]
    if held[2]:
        refs = refs[2:]
    (
        grad_send, halo_send, grads_all, gv_all,
        hid, der, scal, x_win, v_win, g, u, coef, x_in, xa_in, g_in, ga_in, gv, sems,
    ) = refs
    which = info[0]
    active = info[1]
    is_top = info[2]
    live = info[3]
    length, width = grad_send.shape
    rows = g.shape[0]
    chunks = width // LANES
    first, count = held[0], held[1]

    def scal_copy(i):
        return pltpu.make_async_copy(saved[i][2], scal, sems.at[2, 0])

    def hidden_copy(i, layer):
        return pltpu.make_async_copy(saved[i][0].at[layer], hid.at[layer], sems.at[0, layer])

    def slope_copy(i, layer):
        return pltpu.make_async_copy(saved[i][1].at[layer], der.at[layer], sems.at[1, layer])

    def input_copies():
        return (
            pltpu.make_async_copy(x_all.at[which], x_in, sems.at[2, 1]),
            pltpu.make_async_copy(xa_all.at[which], xa_in, sems.at[2, 2]),
            pltpu.make_async_copy(v_all.at[which], v_win.at[pl.ds(0, length)], sems.at[2, 3]),
            pltpu.make_async_copy(va_all.at[which], v_win.at[pl.ds(length, HALO)], sems.at[2, 4]),
        )

    def grad_copies(source, source_halo):
        return (
            pltpu.make_async_copy(source, g_in, sems.at[3, 0]),
            pltpu.make_async_copy(source_halo, ga_in, sems.at[3, 1]),
        )

    @pl.when(active == 1)
    def _():
        @pl.when(is_top == 1)
        def _():
            for copy in grad_copies(top.at[which], top_halo.at[which]):
                copy.start()

        @pl.when(is_top == 0)
        def _():
            for copy in grad_copies(near, near_halo):
                copy.start()

        for i in range(count):
            @pl.when(which == first + i)
            def _():
                scal_copy(i).start()

                def begin(step, carry):
                    layer = live - 1 - step
                    slope_copy(i, layer).start()
                    hidden_copy(i, layer).start()
                    return carry

                lax.fori_loop(0, live, begin, 0)

        for copy in input_copies():
            copy.start()

        zero = jnp.zeros((rows, LANES), f32)
        for copy in grad_copies(near, near_halo):
            copy.wait()
        scal_copy(0).wait()

        def into_taps(layer, cols, grad):
            slope = grad * der[layer, :, cols]
            out = taps[layer, 0:1, cols] * slope
            for k in range(1, 4):
                out = out + taps[layer, k : k + 1, cols] * pltpu.roll(slope, rows - k, 0)
            u[:, cols] = out
            return out * hid[layer, :, cols]

        last = live - 1
        slope_copy(0, last).wait()
        hidden_copy(0, last).wait()

        def begin(chunk, total):
            cols = columns(chunk)
            g[0:length, cols] = g_in[:, cols].astype(f32)
            g[length:rows, cols] = ga_in[:, cols].astype(f32)
            return total + into_taps(last, cols, g[:, cols])

        total = lax.fori_loop(0, chunks, begin, zero)

        def coefficients(layer, total):
            rms = scal[layer]
            coef[0] = rms
            coef[1] = -rms * rms * rms * (row_total(total) / width)

        def through_rms(layer, cols):
            return g[:, cols] + (coef[0] * u[:, cols] + coef[1] * hid[layer, :, cols])

        def layer_step(step, total):
            layer = live - 1 - step
            coefficients(layer, total)
            slope_copy(0, layer - 1).wait()
            hidden_copy(0, layer - 1).wait()

            def one(chunk, total):
                cols = columns(chunk)
                grad = through_rms(layer, cols)
                g[:, cols] = grad
                return total + into_taps(layer - 1, cols, grad)

            return lax.fori_loop(0, chunks, one, zero)

        total = lax.fori_loop(0, live - 1, layer_step, total)
        coefficients(0, total)
        for copy in input_copies():
            copy.wait()

        def to_gate(chunk, total):
            cols = columns(chunk)
            grad = through_rms(0, cols)
            g[:, cols] = grad
            return total + grad * v_win[:, cols]

        total = row_total(lax.fori_loop(0, chunks, to_gate, zero))
        rx, rv, xv, gate = scal[4], scal[5], scal[6], scal[7]
        both = total * gate * (1.0 - gate) * (1.0 / math.sqrt(width)) * rx * rv
        mean = xv / width
        coef[0] = both
        coef[1] = -both * rx * rx * mean
        coef[2] = -both * rv * rv * mean
        coef[3] = gate

        def finish(chunk, carry):
            cols = columns(chunk)
            grad = g[0:length, cols]
            x = x_in[:, cols].astype(f32)
            v = v_win[0:length, cols]
            grad_x = grad + coef[0, 0:length] * v + coef[1, 0:length] * x
            grad_v = coef[3, 0:length] * grad + coef[0, 0:length] * x + coef[2, 0:length] * v
            grad_x = grad_x.astype(bf16)
            grad_send[:, cols] = grad_x
            halo_send[:, cols] = grad_x[0:HALO]
            gv[:, cols] = grad_v.astype(bf16)
            return carry

        lax.fori_loop(0, chunks, finish, 0)
        outs = (
            pltpu.make_async_copy(grad_send, grads_all.at[which], sems.at[3, 2]),
            pltpu.make_async_copy(gv, gv_all.at[which], sems.at[3, 3]),
        )
        for copy in outs:
            copy.start()
        for copy in outs:
            copy.wait()


def backward_map(info, near, near_halo, top, top_halo, x, x_after, v, v_after, taps, first, saved, previous):
    batches, length, width = x.shape
    rows = length + HALO
    layers = taps.shape[0]
    flat = [array for group in saved for array in group]
    some = pl.BlockSpec(memory_space=pl.ANY)
    extra = () if previous is None else previous
    operands = (info, near, near_halo, top, top_halo, x, x_after, v, v_after, taps, *flat, *extra)
    aliases = {} if previous is None else {len(operands) - 2: 2, len(operands) - 1: 3}
    return pl.pallas_call(
        functools.partial(backward_kernel, (first, len(saved), previous is not None)),
        out_shape=(
            jax.ShapeDtypeStruct((length, width), bf16),
            jax.ShapeDtypeStruct((HALO, width), bf16),
            jax.ShapeDtypeStruct((batches, length, width), bf16),
            jax.ShapeDtypeStruct((batches, length, width), bf16),
        ),
        in_specs=[pl.BlockSpec(memory_space=pltpu.SMEM)]
        + [some] * 8
        + [pl.BlockSpec(memory_space=pltpu.VMEM)]
        + [some] * (len(flat) + len(extra)),
        out_specs=[pl.BlockSpec(memory_space=pltpu.VMEM)] * 2 + [some] * 2,
        scratch_shapes=[
            pltpu.VMEM((layers, rows, width), f32),
            pltpu.VMEM((layers, rows, width), f32),
            pltpu.VMEM((8, rows, LANES), f32),
            pltpu.VMEM((rows, width), f32),
            pltpu.VMEM((rows, width), f32),
            pltpu.VMEM((rows, width), f32),
            pltpu.VMEM((rows, width), f32),
            pltpu.VMEM((4, rows, LANES), f32),
            pltpu.VMEM((length, width), bf16),
            pltpu.VMEM((HALO, width), bf16),
            pltpu.VMEM((length, width), bf16),
            pltpu.VMEM((HALO, width), bf16),
            pltpu.VMEM((length, width), bf16),
            pltpu.SemaphoreType.DMA((4, 5)),
        ],
        input_output_aliases=aliases,
        compiler_params=pltpu.CompilerParams(vmem_limit_bytes=44 * MIB),
        cost_estimate=pl.CostEstimate(flops=25 * layers * rows * width, bytes_accessed=14 * MIB, transcendentals=0),
        name="backward_map",
    )(*operands)


def pack_kernel(dest, gv_all, out, stacked):
    heads, width = 8, out.shape[-1]
    length = gv_all.shape[1]
    for head in range(heads):
        stacked[head * length : (head + 1) * length, :] = gv_all[0, :, head * width : (head + 1) * width]
    slots = out.shape[0]
    step = 256

    def one(tile, carry):
        at = pl.multiple_of(tile * step, step)
        slot = lax.broadcasted_iota(jnp.int32, (step, heads * length), 0) + at
        place = jnp.where(slot == dest[...], 1.0, 0.0).astype(bf16)
        out[pl.ds(at, step), :] = jnp.dot(
            place, stacked[...], preferred_element_type=f32
        ).astype(bf16)
        return carry

    lax.fori_loop(0, slots // step, one, 0)


def pack_values(batch, dest, gv_all, slots):
    batches, length, model = gv_all.shape
    feature = model // 8
    return pl.pallas_call(
        pack_kernel,
        out_shape=jax.ShapeDtypeStruct((slots, feature), bf16),
        grid=(1,),
        in_specs=[
            pl.BlockSpec(dest.shape, lambda i: (0, 0)),
            pl.BlockSpec((1, length, model), lambda i: (batch, 0, 0)),
        ],
        out_specs=pl.BlockSpec((slots, feature), lambda i: (0, 0)),
        scratch_shapes=[pltpu.VMEM((8 * length, feature), bf16)],
        compiler_params=pltpu.CompilerParams(vmem_limit_bytes=24 * MIB),
        cost_estimate=pl.CostEstimate(flops=2 * slots * 8 * length * feature, bytes_accessed=2 * MIB, transcendentals=0),
        name="pack_values",
    )(dest, gv_all)


def owner_kernel(has_table, got, head_of, row_of, weight, *refs):
    if has_table:
        table_in, refs = refs[0], refs[1:]
    table, spread, flat, place, sems = refs
    heads, row_width, feature = weight.shape
    slots = got.shape[0]
    copies = [
        pltpu.make_async_copy(
            weight.at[h], flat.at[:, pl.ds(h * feature, feature)], sems.at[h]
        )
        for h in range(heads)
    ]
    for copy in copies:
        copy.start()
    step = 128

    def expand(tile, carry):
        at = pl.ds(pl.multiple_of(tile * step, step), step)
        own = head_of[at, :]
        block = got[at, :]
        for h in range(heads):
            mask = jnp.broadcast_to(own == h, block.shape)
            spread[at, h * feature : (h + 1) * feature] = jnp.where(mask, block, jnp.zeros_like(block))
        return carry

    lax.fori_loop(0, slots // step, expand, 0)
    table_rows = table.shape[0]

    def mark(tile, carry):
        at = pl.multiple_of(tile * step, step)
        row = lax.broadcasted_iota(jnp.int32, (step, slots), 0) + at
        place[pl.ds(at, step), :] = jnp.where(row == row_of[...], 1.0, 0.0).astype(bf16)
        return carry

    lax.fori_loop(0, table_rows // step, mark, 0)
    for copy in copies:
        copy.wait()
    tile = 256

    def add(block, carry):
        at = pl.ds(pl.multiple_of(block * tile, tile), tile)
        rows = lax.dot_general(
            spread[...], flat[at, :], (((1,), (1,)), ((), ())), preferred_element_type=f32
        )
        total = jnp.dot(place[...], rows.astype(bf16), preferred_element_type=f32)
        if has_table:
            total = total + table_in[:, at]
        table[:, at] = total
        return carry

    lax.fori_loop(0, row_width // tile, add, 0)


def owner_add(table, got, head_of, row_of, weight):
    heads, row_width, feature = weight.shape
    slots = got.shape[0]
    vmem = pl.BlockSpec(memory_space=pltpu.VMEM)
    operands = [got, head_of, row_of, weight]
    specs = [vmem, vmem, vmem, pl.BlockSpec(memory_space=pl.ANY)]
    if table is not None:
        operands.append(table)
        specs.append(vmem)
    return pl.pallas_call(
        functools.partial(owner_kernel, table is not None),
        out_shape=jax.ShapeDtypeStruct((TABLE_DEV, row_width), f32),
        in_specs=specs,
        out_specs=vmem,
        scratch_shapes=[
            pltpu.VMEM((slots, heads * feature), bf16),
            pltpu.VMEM((row_width, heads * feature), bf16),
            pltpu.VMEM((TABLE_DEV, slots), bf16),
            pltpu.SemaphoreType.DMA((heads,)),
        ],
        compiler_params=pltpu.CompilerParams(vmem_limit_bytes=48 * MIB),
        cost_estimate=pl.CostEstimate(flops=2 * slots * row_width * (heads * feature + TABLE_DEV), bytes_accessed=18 * MIB, transcendentals=0),
        name="owner_add",
    )(*operands)


def slots_of(row_ids, owners, capacity):
    batches, length, heads = row_ids.shape
    ids = row_ids.transpose(0, 2, 1).reshape(batches, heads * length)
    owner = ids // TABLE_DEV
    local = ids - owner * TABLE_DEV
    head = jnp.arange(heads * length, dtype=jnp.int32) // length
    order = jnp.arange(heads * length, dtype=jnp.int32)
    ahead = (owner[:, None, :] == owner[:, :, None]) & (order[None, :] < order[:, None])
    rank = jnp.sum(ahead.astype(jnp.int32), -1)
    dest = owner * capacity + rank
    code = local * heads + head
    slot = jnp.arange(owners * capacity, dtype=jnp.int32)
    hit = dest[:, None, :] == slot[:, None]
    holds = jnp.sum(jnp.where(hit, code[:, None, :] + 1, 0), -1) - 1
    return dest, holds


def after(value, *others):
    return lax.optimization_barrier((value, *others))[0]


def shards(
    saved_inputs, memory, value_weight, conv_weight, norm_gain, layer_counts, row_ids, out_grad
):
    section = lax.axis_index("section")
    sections = lax.axis_size("section")
    owners = lax.axis_size("table")
    batches, length, width = out_grad.shape
    heads = memory.shape[3]
    capacity = 3 * length * heads // (2 * owners)
    slots = owners * capacity
    weight = value_weight[0]
    live = layer_counts[0]
    taps = conv_weight[0] * norm_gain[0][:, None, :]
    x = saved_inputs[0]
    is_top = section == sections - 1

    to_next = [(i, i + 1) for i in range(owners - 1)]
    to_last = [(i + 1, i) for i in range(owners - 1)]
    down = [(i + 1, i) for i in range(sections - 1)]
    down_halo = [
        ((i + 1) * owners + t + 1, i * owners + t)
        for i in range(sections - 1)
        for t in range(owners - 1)
    ]
    x_before = lax.ppermute(x[:, length - HALO :], "table", to_next)
    x_after = lax.ppermute(x[:, :HALO], "table", to_last)
    top_halo = lax.ppermute(out_grad[:, :HALO], "table", to_last)
    v = jnp.einsum("bthr,hrc->bthc", memory[0], weight, preferred_element_type=f32)
    v = v.reshape(batches, length, width)
    v_before = lax.ppermute(v[:, length - HALO :], "table", to_next)
    v_after = lax.ppermute(v[:, :HALO], "table", to_last)

    saved = []
    near = jnp.zeros((length, width), bf16)
    near_halo = jnp.zeros((HALO, width), bf16)
    outputs = None
    table = None
    head_of = row_of = dest = None
    ticks = batches + sections - 1
    grad_send = None
    for tick in range(ticks):
        if tick < batches:
            number = live.reshape(1)
            if tick > 0:
                number = after(number, grad_send)
            saved.append(
                forward_map(tick, number, x, x_before, x_after, v, v_before, v_after, taps)
            )
        if tick == 2:
            ids = after(row_ids[0], grad_send)
            dest, holds = slots_of(ids, owners, capacity)
            holds = holds.reshape(batches, owners, capacity).transpose(1, 0, 2)
            holds = lax.all_to_all(
                holds.reshape(owners, batches * capacity), "table", 0, 0, tiled=True
            )
            holds = holds.reshape(owners, batches, capacity).transpose(1, 0, 2)
            holds = holds.reshape(batches, slots)
            row_of = jnp.where(holds < 0, -1, holds // heads)
            head_of = jnp.where(holds < 0, -1, holds % heads)
        position = tick - (sections - 1 - section)
        which = jnp.clip(position, 0, batches - 1)
        active = (position >= 0) & (position < batches)
        info = jnp.stack([which, active, is_top, live]).astype(jnp.int32)
        first = max(0, tick - (sections - 1))
        grad_send, halo_send, *outputs = backward_map(
            info, near, near_halo, out_grad, top_halo, x, x_after, v, v_after, taps,
            first, saved[first : tick + 1], outputs,
        )
        if tick < ticks - 1:
            near = lax.ppermute(grad_send, "section", down)
            near_halo = lax.ppermute(halo_send, ("section", "table"), down_halo)
        batch = tick - (sections - 1)
        if batch >= 0:
            packed = pack_values(batch, dest[batch][None, :], outputs[1], slots)
            got = lax.all_to_all(packed, "table", 0, 0, tiled=True)
            table = owner_add(
                table, got, head_of[batch][:, None], row_of[batch][None, :], weight
            )
    return (outputs[0][None], table[None])


def solution(mesh):
    placed = (
        P("section", None, "table", None),
        P("section", None, "table", None, None),
        P("section", None, None, None),
        P("section", None, None, None),
        P("section", None, None),
        P("section"),
        P("section", None, "table", None),
        P(None, "table", None),
    )
    return jax.shard_map(
        shards,
        mesh=mesh,
        in_specs=placed,
        out_specs=(P("section", None, "table", None), P("section", "table", None)),
        check_vma=False,
    )
```

time: 1880 us -> 388 us (0.21); the launches traced: 1860 us -> 384 us
  local copies, waits for them, and re-layouts: 848 us -> 65.4 us
  other arithmetic: 390 us -> 8.42 us
  starting transfers between devices: 308 us -> 79.6 us
  waiting for transfers between devices: 245 us -> 54.1 us
  Pallas kernels: 0 us -> 172 us
  matrix products: 55.8 us -> 2.33 us
    scatter x14 -> x0, local copies, waits for them, and re-layouts: 700 us -> none  [the longest x7 524 us: pack_rows(): jnp.zeros((owners, capacity, feature), payload.dtype).at[owner_of, slot_of]]
    pallas_call x0 -> x19, Pallas kernels: none -> 172 us  [the longest x4 70.7 us: owner_add(): pl.pallas_call(functools.partial(owner_kernel, table is not None), out_sh...]
    ppermute x62 -> x17, waiting for transfers between devices: 223 us -> 54.1 us  [the longest x6 40.6 us: shards(): near_halo = lax.ppermute(halo_send, ('section', 'table'), down_halo)]
    ppermute x62 -> x17, starting transfers between devices: 195 us -> 29.4 us  [the longest x6 7.73 us: shards(): near_halo = lax.ppermute(halo_send, ('section', 'table'), down_halo)]
    reduce_sum x72 -> x2, other arithmetic: 146 us -> 2.94 us  [the longest x1 2.1 us: slots_of(): rank = jnp.sum(ahead.astype(jnp.int32), -1)]
    scatter-add x7 -> x0, other arithmetic: 100 us -> none  [owner_add(): return table_sum.at[flat_index].add(flat_rows, mode='drop')]
    mul x53 -> x1, other arithmetic: 77.7 us -> 1.02 us  [shards(): taps = conv_weight[0] * norm_gain[0][:, None, :]]
    all_to_all x14 -> x5, starting transfers between devices: 112 us -> 50.1 us  [the longest x4 33.7 us: shards(): got = lax.all_to_all(packed, 'table', 0, 0, tiled=True)]
  transfers between devices with their start and end apart: 76 -> 22, of which waited for: 41 -> 9; matrix products, arithmetic and copies ran while one was open for 65% -> 5% of each run, Pallas kernels for 0% -> 39%
where the time goes in v1:
time: 388 us; the launch traced here: 384 us
  Pallas kernels  172 us (44%)
  starting transfers between devices  79.6 us (21%)
  local copies, waits for them, and re-layouts  65.4 us (17%)
  waiting for transfers between devices  54.1 us (14%)
  other arithmetic  8.42 us (2%)
    pallas_call x4, Pallas kernels, owner_add(): pl.pallas_call(functools.partial(owner_kernel, table is not None), out_sh...  70.7 us
    pallas_call x7, Pallas kernels, backward_map(): pl.pallas_call(functools.partial(backward_kernel, (first, len(saved), pre...  52.1 us
    unnamed x128, local copies, waits for them, and re-layouts  46.7 us
    pallas_call x4, Pallas kernels, forward_map(): pl.pallas_call(forward_kernel, out_shape=(jax.ShapeDtypeStruct((layers, k...  44.5 us
    ppermute x6, waiting for transfers between devices, shards(): near_halo = lax.ppermute(halo_send, ('section', 'table'), down_halo)  40.6 us
    all_to_all x4, starting transfers between devices, shards(): got = lax.all_to_all(packed, 'table', 0, 0, tiled=True)  33.7 us
    all_to_all x1, starting transfers between devices, shards(): lax.all_to_all(holds.reshape(owners, batches * capacity), 'table', 0, 0,...  16.4 us
    ppermute x6, waiting for transfers between devices, shards(): near = lax.ppermute(grad_send, 'section', down)  8.08 us
  transfers between devices with their start and end apart: 22, of which 9 were waited for; matrix products, arithmetic and copies ran while one was open for 5% of the time, Pallas kernels for 39%

profile of v1, /device:TPU:1, one launch (start us, length us, event | category | flops | bytes accessed | tf_op | source)
XLA Modules:
  0.0 384.0 jit_solution(14417765343262538473)
XLA Ops:
  0.6 4.7 %copy.41 = bf16[4,64,8,1024]{3,1,0,2:T(8,128)(2,1)S(1)} copy(bf16[4,64,8,1024]{3,2,1,0:T(8,128)(2,1)} %bitcast.90) | data formatting | bytes 8388608 | tf_op jit(solution)/shard_map/squeeze | solution.py:529
  5.3 2.3 fusion.9
  8.1 1.4 fusion.11
  9.6 2.0 copy-done
  11.6 3.3 collective-permute-start.2
  14.9 3.2 collective-permute-start.4
  19.2 2.1 collective-permute-start.1
  21.3 3.5 collective-permute-start.3
  24.7 1.9 slice.51
  26.6 1.9 collective-permute-start
  30.3 4.2 %collective-permute-done.1.xa.xa_all = bf16[4,16,4096]{2,1,0:T(8,128)(2,1)} collective-permute-done((bf16[4,16,4096]{2,1,0:T(8,128)(2,1)}, bf16[4,16,4096]{2,1,0:T(8,128)(2,1)}, u32[]{:S(2)}, u32[]{:S(2)}) %collective-permute-start.1) | collective-permute-done | bytes 524320 | tf_op jit(solution)/shard_map/ppermute | solution.py:527
  35.8 2.2 copy-done.1
  38.0 11.1 %forward_map.4 = (f32[4,80,4096]{2,1,0:T(8,128)}, f32[4,80,4096]{2,1,0:T(8,128)}, f32[8,80,128]{2,1,0:T(8,128)S(1)}) custom-call(s32[1]{0:T(128)S(6)} %copy.63.live_ref, bf16[4,16,4096]{2,1,0:T(8,128)(2,1)} %collective-permute-done.3.xb, bf16[4,64,4096]{2,1,0:T(8,128)(2,1)S(1)} %bitcast.73, bf16[4,16,4096]{2,1,0:T(8,128)(2,1)} %collective-permute-done.1.xa.xa_all, ...), custom_call_target="tpu_custom_call" | custom-call | flops 47185920 | bytes 16777216 | tf_op jit(solution)/shard_map/forward_map/pallas_call | solution.py:124
  49.2 1.6 backward_map.7
  56.9 2.2 copy-done.2
  59.1 11.0 %forward_map.5 = (f32[4,80,4096]{2,1,0:T(8,128)}, f32[4,80,4096]{2,1,0:T(8,128)}, f32[8,80,128]{2,1,0:T(8,128)S(1)}) custom-call(s32[1]{0:T(128)S(6)} %copy.63.live_ref, bf16[4,16,4096]{2,1,0:T(8,128)(2,1)} %collective-permute-done.3.xb, bf16[4,64,4096]{2,1,0:T(8,128)(2,1)S(1)} %bitcast.75, bf16[4,16,4096]{2,1,0:T(8,128)(2,1)} %collective-permute-done.1.xa.xa_all, ...), custom_call_target="tpu_custom_call" | custom-call | flops 47185920 | bytes 16777216 | tf_op jit(solution)/shard_map/forward_map/pallas_call | solution.py:124
  70.1 11.2 %forward_map.6 = (f32[4,80,4096]{2,1,0:T(8,128)}, f32[4,80,4096]{2,1,0:T(8,128)}, f32[8,80,128]{2,1,0:T(8,128)S(1)}) custom-call(s32[1]{0:T(128)S(6)} %copy.63.live_ref, bf16[4,16,4096]{2,1,0:T(8,128)(2,1)} %collective-permute-done.3.xb, bf16[4,64,4096]{2,1,0:T(8,128)(2,1)S(1)} %bitcast.76, bf16[4,16,4096]{2,1,0:T(8,128)(2,1)} %collective-permute-done.1.xa.xa_all, ...), custom_call_target="tpu_custom_call" | custom-call | flops 47185920 | bytes 16777216 | tf_op jit(solution)/shard_map/forward_map/pallas_call | solution.py:124
  81.3 11.2 %forward_map.7 = (f32[4,80,4096]{2,1,0:T(8,128)}, f32[4,80,4096]{2,1,0:T(8,128)}, f32[8,80,128]{2,1,0:T(8,128)S(1)}) custom-call(s32[1]{0:T(128)S(6)} %copy.63.live_ref, bf16[4,16,4096]{2,1,0:T(8,128)(2,1)} %collective-permute-done.3.xb, bf16[4,64,4096]{2,1,0:T(8,128)(2,1)S(1)} %bitcast.77, bf16[4,16,4096]{2,1,0:T(8,128)(2,1)} %collective-permute-done.1.xa.xa_all, ...), custom_call_target="tpu_custom_call" | custom-call | flops 47185920 | bytes 16777216 | tf_op jit(solution)/shard_map/forward_map/pallas_call | solution.py:124
  92.6 1.6 backward_map.8
  99.5 2.1 convert_reduce_fusion
  101.6 4.5 %collective-permute-done.8.near_halo = bf16[16,4096]{1,0:T(8,128)(2,1)S(1)} collective-permute-done((bf16[16,4096]{1,0:T(8,128)(2,1)}, bf16[16,4096]{1,0:T(8,128)(2,1)S(1)}, u32[]{:S(2)}, u32[]{:S(2)}) %collective-permute-start.8) | collective-permute-done | bytes 131104 | tf_op jit(solution)/shard_map/ppermute | solution.py:572
  107.1 1.6 copy-done.8
  111.6 1.5 backward_map.9
  118.1 16.4 %all-to-all-start.1 = ((s32[32,1,96]{2,1,0:T(1,128)}), s32[32,1,96]{2,1,0:T(1,128)S(1)}, u32[]{:S(2)}, u32[]{:S(2)}) async-start(s32[32,1,96]{2,1,0:T(1,128)} %bitcast.30), calls=%async_computation.1 | async-start | bytes 32768 | tf_op jit(solution)/shard_map/all_to_all | solution.py:554
  136.7 10.9 %collective-permute-done.10.near_halo = bf16[16,4096]{1,0:T(8,128)(2,1)S(1)} collective-permute-done((bf16[16,4096]{1,0:T(8,128)(2,1)}, bf16[16,4096]{1,0:T(8,128)(2,1)S(1)}, u32[]{:S(2)}, u32[]{:S(2)}) %collective-permute-start.10) | collective-permute-done | bytes 131104 | tf_op jit(solution)/shard_map/ppermute | solution.py:572
  147.6 1.6 copy-done.10
  153.1 11.3 %backward_map.10 = (bf16[64,4096]{1,0:T(8,128)(2,1)S(1)}, bf16[16,4096]{1,0:T(8,128)(2,1)S(1)}, bf16[4,64,4096]{2,1,0:T(8,128)(2,1)}, bf16[4,64,4096]{2,1,0:T(8,128)(2,1)S(1)}) custom-call(s32[4]{0:T(128)S(1)} %add_add_fusion.4.info, bf16[64,4096]{1,0:T(8,128)(2,1)} %collective-permute-done.9.near, ...), custom_call_target="tpu_custom_call", output_to_operand_aliasing={{2}: (22, {}), {3}: (23, {})} | custom-call | flops 32768000 | bytes 14680064 | tf_op jit(solution)/shard_map/backward_map/pallas_call | solution.py:327
  168.9 7.5 %all-to-all-start.4 = ((bf16[32,24,512]{2,1,0:T(8,128)(2,1)}), bf16[32,24,512]{2,1,0:T(8,128)(2,1)}, u32[]{:S(2)}, u32[]{:S(2)}) async-start(bf16[32,24,512]{2,1,0:T(8,128)(2,1)} %bitcast.80), calls=%async_computation.4 | async-start | bytes 1572864 | tf_op jit(solution)/shard_map/all_to_all | solution.py:576
  179.7 18.5 %collective-permute-done.12.near_halo = bf16[16,4096]{1,0:T(8,128)(2,1)S(1)} collective-permute-done((bf16[16,4096]{1,0:T(8,128)(2,1)}, bf16[16,4096]{1,0:T(8,128)(2,1)S(1)}, u32[]{:S(2)}, u32[]{:S(2)}) %collective-permute-start.12) | collective-permute-done | bytes 131104 | tf_op jit(solution)/shard_map/ppermute | solution.py:572
  198.2 4.0 %collective-permute-done.11.near = bf16[64,4096]{1,0:T(8,128)(2,1)} collective-permute-done((bf16[64,4096]{1,0:T(8,128)(2,1)}, bf16[64,4096]{1,0:T(8,128)(2,1)}, u32[]{:S(2)}, u32[]{:S(2)}) %collective-permute-start.11) | collective-permute-done | bytes 524320 | tf_op jit(solution)/shard_map/ppermute | solution.py:571
  202.2 1.6 copy-done.12
  206.8 11.3 %backward_map.11 = (bf16[64,4096]{1,0:T(8,128)(2,1)S(1)}, bf16[16,4096]{1,0:T(8,128)(2,1)S(1)}, bf16[4,64,4096]{2,1,0:T(8,128)(2,1)}, bf16[4,64,4096]{2,1,0:T(8,128)(2,1)S(1)}) custom-call(s32[4]{0:T(128)S(1)} %add_add_fusion.3.info, bf16[64,4096]{1,0:T(8,128)(2,1)} %collective-permute-done.11.near, ...), custom_call_target="tpu_custom_call", output_to_operand_aliasing={{2}: (19, {}), {3}: (20, {})} | custom-call | flops 32768000 | bytes 14680064 | tf_op jit(solution)/shard_map/backward_map/pallas_call | solution.py:327
  222.7 9.3 %all-to-all-start.3 = ((bf16[32,24,512]{2,1,0:T(8,128)(2,1)}), bf16[32,24,512]{2,1,0:T(8,128)(2,1)}, u32[]{:S(2)}, u32[]{:S(2)}) async-start(bf16[32,24,512]{2,1,0:T(8,128)(2,1)} %bitcast.79), calls=%async_computation.3 | async-start | bytes 1572864 | tf_op jit(solution)/shard_map/all_to_all | solution.py:576
  242.6 6.7 %collective-permute-done.14.near_halo = bf16[16,4096]{1,0:T(8,128)(2,1)S(1)} collective-permute-done((bf16[16,4096]{1,0:T(8,128)(2,1)}, bf16[16,4096]{1,0:T(8,128)(2,1)S(1)}, u32[]{:S(2)}, u32[]{:S(2)}) %collective-permute-start.14) | collective-permute-done | bytes 131104 | tf_op jit(solution)/shard_map/ppermute | solution.py:572
  249.3 3.1 collective-permute-done.13.near
  252.4 1.6 copy-done.18
  256.0 12.1 %backward_map.12 = (bf16[64,4096]{1,0:T(8,128)(2,1)}, bf16[16,4096]{1,0:T(8,128)(2,1)}, bf16[4,64,4096]{2,1,0:T(8,128)(2,1)}, bf16[4,64,4096]{2,1,0:T(8,128)(2,1)S(1)}) custom-call(s32[4]{0:T(128)S(1)} %copy-done.48, bf16[64,4096]{1,0:T(8,128)(2,1)} %collective-permute-done.13.near, ...), custom_call_target="tpu_custom_call", output_to_operand_aliasing={{2}: (16, {}), {3}: (17, {})} | custom-call | flops 32768000 | bytes 14680064 | tf_op jit(solution)/shard_map/backward_map/pallas_call | solution.py:327
  272.5 9.5 %all-to-all-start.2 = ((bf16[32,24,512]{2,1,0:T(8,128)(2,1)}), bf16[32,24,512]{2,1,0:T(8,128)(2,1)}, u32[]{:S(2)}, u32[]{:S(2)}) async-start(bf16[32,24,512]{2,1,0:T(8,128)(2,1)} %bitcast.81), calls=%async_computation.2 | async-start | bytes 1572864 | tf_op jit(solution)/shard_map/all_to_all | solution.py:576
  283.7 17.1 %owner_add.4.refs_0_ = f32[1024,1024]{1,0:T(8,128)S(1)} custom-call(bf16[768,512]{1,0:T(8,128)(2,1)} %bitcast.40.got, s32[768,1]{1,0:T(8,128)S(1)} %copy-done.44, s32[1,768]{1,0:T(1,128)S(1)} %copy-done.46, bf16[8,1024,512]{2,1,0:T(8,128)(2,1)} %bitcast.86), custom_call_target="tpu_custom_call" | custom-call | flops 8053063680 | bytes 18874368 | tf_op jit(solution)/shard_map/owner_add/pallas_call | solution.py:464
  300.9 12.8 %backward_map.13 = (bf16[64,4096]{1,0:T(8,128)(2,1)}, bf16[16,4096]{1,0:T(8,128)(2,1)}, bf16[4,64,4096]{2,1,0:T(8,128)(2,1)}, bf16[4,64,4096]{2,1,0:T(8,128)(2,1)S(1)}) custom-call(s32[4]{0:T(128)S(1)} %copy-done.47, bf16[64,4096]{1,0:T(8,128)(2,1)} %collective-permute-done.15.near, ...), custom_call_target="tpu_custom_call", output_to_operand_aliasing={{2}: (13, {}), {3}: (14, {})} | custom-call | flops 32768000 | bytes 14680064 | tf_op jit(solution)/shard_map/backward_map/pallas_call | solution.py:327
  313.7 1.9 pack_values.4
  315.6 7.4 %all-to-all-start = ((bf16[32,24,512]{2,1,0:T(8,128)(2,1)}), bf16[32,24,512]{2,1,0:T(8,128)(2,1)S(1)}, u32[]{:S(2)}, u32[]{:S(2)}) async-start(bf16[32,24,512]{2,1,0:T(8,128)(2,1)} %bitcast.27), calls=%async_computation | async-start | bytes 1572864 | tf_op jit(solution)/shard_map/all_to_all | solution.py:576
  324.0 18.0 %owner_add.5.refs_0_ = f32[1024,1024]{1,0:T(8,128)S(1)} custom-call(bf16[768,512]{1,0:T(8,128)(2,1)} %bitcast.37.got, s32[768,1]{1,0:T(8,128)S(1)} %copy-done.43, s32[1,768]{1,0:T(1,128)S(1)} %copy-done.45, bf16[8,1024,512]{2,1,0:T(8,128)(2,1)} %bitcast.87, f32[1024,1024]{1,0:T(8,128)} %copy-done.55), custom_call_target="tpu_custom_call" | custom-call | flops 8053063680 | bytes 18874368 | tf_op jit(solution)/shard_map/owner_add/pallas_call | solution.py:464
  342.1 2.0 copy-done.58
  344.1 18.0 %owner_add.6.refs_0_ = f32[1024,1024]{1,0:T(8,128)S(1)} custom-call(bf16[768,512]{1,0:T(8,128)(2,1)} %bitcast.34.got, s32[768,1]{1,0:T(8,128)S(1)} %copy-done.42, s32[1,768]{1,0:T(1,128)S(1)} %get-tuple-element.94.row_of, bf16[8,1024,512]{2,1,0:T(8,128)(2,1)} %bitcast.88, f32[1024,1024]{1,0:T(8,128)} %copy-done.58), custom_call_target="tpu_custom_call" | custom-call | flops 8053063680 | bytes 18874368 | tf_op jit(solution)/shard_map/owner_add/pallas_call | solution.py:464
  362.1 2.0 copy-done.56
  364.1 2.2 copy-done.57
  366.3 17.6 %owner_add.7 = f32[1024,1024]{1,0:T(8,128)} custom-call(bf16[768,512]{1,0:T(8,128)(2,1)S(1)} %bitcast.82, s32[768,1]{1,0:T(8,128)S(1)} %copy-done.41, s32[1,768]{1,0:T(1,128)S(1)} %get-tuple-element.95.row_of, bf16[8,1024,512]{2,1,0:T(8,128)(2,1)} %bitcast.89, f32[1024,1024]{1,0:T(8,128)S(1)} %copy-done.57), custom_call_target="tpu_custom_call" | custom-call | flops 8053063680 | bytes 18874368 | tf_op jit(solution)/shard_map/owner_add/pallas_call | solution.py:464
  (183 shorter events, 65.1 us)
Async XLA Ops:
  0.6 4.7 %copy-start.59 = (bf16[1,8,1024,512]{3,2,1,0:T(8,128)(2,1)S(1)}, bf16[1,8,1024,512]{3,2,1,0:T(8,128)(2,1)}, u32[]{:S(2)}) copy-start(bf16[1,8,1024,512]{3,2,1,0:T(8,128)(2,1)} %param.10) | copy-start | bytes 25165828
  8.1 10.0 %copy-start.3 = (bf16[1,4,64,4096]{3,2,1,0:T(8,128)(2,1)S(1)}, bf16[1,4,64,4096]{3,2,1,0:T(8,128)(2,1)}, u32[]{:S(2)}) copy-start(bf16[1,4,64,4096]{3,2,1,0:T(8,128)(2,1)} %param.8) | copy-start | bytes 6291460
  8.1 21.2 %copy-start.61 = (f32[1,4,4096]{2,1,0:T(4,128)S(1)}, f32[1,4,4096]{2,1,0:T(4,128)}, u32[]{:S(2)}) copy-start(f32[1,4,4096]{2,1,0:T(4,128)} %param.12) | copy-start | bytes 196612
  11.6 24.2 %collective-permute-start.2 = (f32[4,16,4096]{2,1,0:T(8,128)}, f32[4,16,4096]{2,1,0:T(8,128)S(1)}, u32[]{:S(2)}, u32[]{:S(2)}) collective-permute-start(f32[4,16,4096]{2,1,0:T(8,128)} %get-tuple-element.89), channel_id=1, source_target_pairs={{1,0},{2,1},{3,2},{4,3},{5,4},{6,5},{7,6},{8,7},{9,8},{10,9},{11,1... | collective-permute-start | bytes 3145736 | tf_op jit(solution)/shard_map/ppermute | solution.py:532
  14.9 20.9 %collective-permute-start.4 = (f32[4,16,4096]{2,1,0:T(8,128)}, f32[4,16,4096]{2,1,0:T(8,128)}, u32[]{:S(2)}, u32[]{:S(2)}) collective-permute-start(f32[4,16,4096]{2,1,0:T(8,128)} %get-tuple-element.88), channel_id=1, source_target_pairs={{0,1},{1,2},{2,3},{3,4},{4,5},{5,6},{6,7},{7,8},{8,9},{9,10},{10,1... | collective-permute-start | bytes 3145736 | tf_op jit(solution)/shard_map/ppermute | solution.py:531
  19.2 15.4 %collective-permute-start.1 = (bf16[4,16,4096]{2,1,0:T(8,128)(2,1)}, bf16[4,16,4096]{2,1,0:T(8,128)(2,1)}, u32[]{:S(2)}, u32[]{:S(2)}) collective-permute-start(bf16[4,16,4096]{2,1,0:T(8,128)(2,1)} %get-tuple-element.91), channel_id=1, source_target_pairs={{1,0},{2,1},{3,2},{4,3},{5,4},{6,5},{7,6},{8,7},{9,8},{10,9},{11,1... | collective-permute-start | bytes 1572872 | tf_op jit(solution)/shard_map/ppermute | solution.py:527
  21.3 14.5 %collective-permute-start.3 = (bf16[4,16,4096]{2,1,0:T(8,128)(2,1)}, bf16[4,16,4096]{2,1,0:T(8,128)(2,1)}, u32[]{:S(2)}, u32[]{:S(2)}) collective-permute-start(bf16[4,16,4096]{2,1,0:T(8,128)(2,1)} %get-tuple-element.90), channel_id=1, source_target_pairs={{0,1},{1,2},{2,3},{3,4},{4,5},{5,6},{6,7},{7,8},{8,9},{9,10},{10,1... | collective-permute-start | bytes 1572872 | tf_op jit(solution)/shard_map/ppermute | solution.py:526
  26.6 22.5 %collective-permute-start = (bf16[4,16,4096]{2,1,0:T(8,128)(2,1)}, bf16[4,16,4096]{2,1,0:T(8,128)(2,1)}, u32[]{:S(2)}, u32[]{:S(2)}) collective-permute-start(bf16[4,16,4096]{2,1,0:T(8,128)(2,1)} %slice.51), channel_id=1, source_target_pairs={{1,0},{2,1},{3,2},{4,3},{5,4},{6,5},{7,6},{8,7},{9,8},{10,9},{11,1... | collective-permute-start | bytes 1572872 | tf_op jit(solution)/shard_map/ppermute | solution.py:528
  35.8 2.2 copy-start.1
  38.0 11.2 %copy-start.15 = (bf16[4,64,4096]{2,1,0:T(8,128)(2,1)S(1)}, bf16[4,64,4096]{2,1,0:T(8,128)(2,1)}, u32[]{:S(2)}) copy-start(bf16[4,64,4096]{2,1,0:T(8,128)(2,1)} %top.13) | copy-start | bytes 6291460
  52.7 39.8 %collective-permute-start.5 = (bf16[64,4096]{1,0:T(8,128)(2,1)}, bf16[64,4096]{1,0:T(8,128)(2,1)}, u32[]{:S(2)}, u32[]{:S(2)}) collective-permute-start(bf16[64,4096]{1,0:T(8,128)(2,1)} %get-tuple-element.47), channel_id=1, source_target_pairs={{32,0},{64,32},{96,64},{33,1},{65,33},{97,65},{34,2},{66,34},{98,6... | collective-permute-start | bytes 1572872 | tf_op jit(solution)/shard_map/ppermute | solution.py:571
  54.8 37.7 %collective-permute-start.6 = (bf16[16,4096]{1,0:T(8,128)(2,1)}, bf16[16,4096]{1,0:T(8,128)(2,1)S(1)}, u32[]{:S(2)}, u32[]{:S(2)}) collective-permute-start(bf16[16,4096]{1,0:T(8,128)(2,1)} %copy-done.53), channel_id=1, source_target_pairs={{33,0},{34,1},{35,2},{36,3},{37,4},{38,5},{39,6},{40,7},{41,8},{42... | collective-permute-start | bytes 393224 | tf_op jit(solution)/shard_map/ppermute | solution.py:572
  56.9 2.2 copy-start.2
  70.1 22.4 %copy-start.25 = (f32[8,80,128]{2,1,0:T(8,128)}, f32[8,80,128]{2,1,0:T(8,128)S(1)}, u32[]{:S(2)}) copy-start(f32[8,80,128]{2,1,0:T(8,128)S(1)} %get-tuple-element.52.refs_5_.refs_2_) | copy-start | bytes 983044
  81.3 11.2 %copy-start.20 = (f32[8,80,128]{2,1,0:T(8,128)}, f32[8,80,128]{2,1,0:T(8,128)S(1)}, u32[]{:S(2)}) copy-start(f32[8,80,128]{2,1,0:T(8,128)S(1)} %get-tuple-element.60.refs_8_.refs_5_.refs_2_) | copy-start | bytes 983044
  81.3 11.2 %copy-start.6 = (bf16[4,64,4096]{2,1,0:T(8,128)(2,1)S(1)}, bf16[4,64,4096]{2,1,0:T(8,128)(2,1)}, u32[]{:S(2)}) copy-start(bf16[4,64,4096]{2,1,0:T(8,128)(2,1)} %copy-done.5) | copy-start | bytes 6291460
  81.3 11.2 %copy-start.16 = (bf16[4,64,4096]{2,1,0:T(8,128)(2,1)S(1)}, bf16[4,64,4096]{2,1,0:T(8,128)(2,1)}, u32[]{:S(2)}) copy-start(bf16[4,64,4096]{2,1,0:T(8,128)(2,1)} %top.13) | copy-start | bytes 6291460
  81.3 11.2 %copy-start.35 = (f32[8,80,128]{2,1,0:T(8,128)S(1)}, f32[8,80,128]{2,1,0:T(8,128)}, u32[]{:S(2)}) copy-start(f32[8,80,128]{2,1,0:T(8,128)} %copy-done.34) | copy-start | bytes 983044
  92.6 14.5 %copy-start.17 = (bf16[4,64,4096]{2,1,0:T(8,128)(2,1)S(1)}, bf16[4,64,4096]{2,1,0:T(8,128)(2,1)}, u32[]{:S(2)}) copy-start(bf16[4,64,4096]{2,1,0:T(8,128)(2,1)} %top.13) | copy-start | bytes 6291460
  95.4 11.6 %collective-permute-start.7 = (bf16[64,4096]{1,0:T(8,128)(2,1)}, bf16[64,4096]{1,0:T(8,128)(2,1)}, u32[]{:S(2)}, u32[]{:S(2)}) collective-permute-start(bf16[64,4096]{1,0:T(8,128)(2,1)} %get-tuple-element.55), channel_id=1, source_target_pairs={{32,0},{64,32},{96,64},{33,1},{65,33},{97,65},{34,2},{66,34},{98,6... | collective-permute-start | bytes 1572872 | tf_op jit(solution)/shard_map/ppermute | solution.py:571
  96.7 9.4 %collective-permute-start.8 = (bf16[16,4096]{1,0:T(8,128)(2,1)}, bf16[16,4096]{1,0:T(8,128)(2,1)S(1)}, u32[]{:S(2)}, u32[]{:S(2)}) collective-permute-start(bf16[16,4096]{1,0:T(8,128)(2,1)} %get-tuple-element.56), channel_id=1, source_target_pairs={{33,0},{34,1},{35,2},{36,3},{37,4},{38,5},{39,6},{40,7},{41,8},{42... | collective-permute-start | bytes 393224 | tf_op jit(solution)/shard_map/ppermute | solution.py:572
  101.6 14.7 %copy-start.60 = (s32[4,512]{1,0:T(4,128)}, s32[4,512]{1,0:T(4,128)S(1)}, u32[]{:S(2)}) copy-start(s32[4,512]{1,0:T(4,128)S(1)} %multiply_add_fusion) | copy-start | bytes 24580
  115.1 32.5 %collective-permute-start.9 = (bf16[64,4096]{1,0:T(8,128)(2,1)}, bf16[64,4096]{1,0:T(8,128)(2,1)}, u32[]{:S(2)}, u32[]{:S(2)}) collective-permute-start(bf16[64,4096]{1,0:T(8,128)(2,1)} %get-tuple-element.63), channel_id=1, source_target_pairs={{32,0},{64,32},{96,64},{33,1},{65,33},{97,65},{34,2},{66,34},{98,6... | collective-permute-start | bytes 1572872 | tf_op jit(solution)/shard_map/ppermute | solution.py:571
  118.1 50.8 %all-to-all-start.1 = ((s32[32,1,96]{2,1,0:T(1,128)}), s32[32,1,96]{2,1,0:T(1,128)S(1)}, u32[]{:S(2)}, u32[]{:S(2)}) async-start(s32[32,1,96]{2,1,0:T(1,128)} %bitcast.30), calls=%async_computation.1 | async-start | bytes 32768 | tf_op jit(solution)/shard_map/all_to_all | solution.py:554
  134.5 13.1 %collective-permute-start.10 = (bf16[16,4096]{1,0:T(8,128)(2,1)}, bf16[16,4096]{1,0:T(8,128)(2,1)S(1)}, u32[]{:S(2)}, u32[]{:S(2)}) collective-permute-start(bf16[16,4096]{1,0:T(8,128)(2,1)} %copy-done.54), channel_id=1, source_target_pairs={{33,0},{34,1},{35,2},{36,3},{37,4},{38,5},{39,6},{40,7},{41,8},{42... | collective-permute-start | bytes 393224 | tf_op jit(solution)/shard_map/ppermute | solution.py:572
  168.9 8.8 %copy-start.62 = (s32[32,1,96]{2,1,0:T(1,128)}, s32[32,1,96]{2,1,0:T(1,128)S(1)}, u32[]{:S(2)}) copy-start(s32[32,1,96]{2,1,0:T(1,128)S(1)} %all-to-all-done.1) | copy-start | bytes 36868
  168.9 53.8 %all-to-all-start.4 = ((bf16[32,24,512]{2,1,0:T(8,128)(2,1)}), bf16[32,24,512]{2,1,0:T(8,128)(2,1)}, u32[]{:S(2)}, u32[]{:S(2)}) async-start(bf16[32,24,512]{2,1,0:T(8,128)(2,1)} %bitcast.80), calls=%async_computation.4 | async-start | bytes 1572864 | tf_op jit(solution)/shard_map/all_to_all | solution.py:576
  176.4 25.9 %collective-permute-start.11 = (bf16[64,4096]{1,0:T(8,128)(2,1)}, bf16[64,4096]{1,0:T(8,128)(2,1)}, u32[]{:S(2)}, u32[]{:S(2)}) collective-permute-start(bf16[64,4096]{1,0:T(8,128)(2,1)} %copy-done.49), channel_id=1, source_target_pairs={{32,0},{64,32},{96,64},{33,1},{65,33},{97,65},{34,2},{66,34},{98,6... | collective-permute-start | bytes 1572872 | tf_op jit(solution)/shard_map/ppermute | solution.py:571
  177.7 20.5 %collective-permute-start.12 = (bf16[16,4096]{1,0:T(8,128)(2,1)}, bf16[16,4096]{1,0:T(8,128)(2,1)S(1)}, u32[]{:S(2)}, u32[]{:S(2)}) collective-permute-start(bf16[16,4096]{1,0:T(8,128)(2,1)} %copy-done.51), channel_id=1, source_target_pairs={{33,0},{34,1},{35,2},{36,3},{37,4},{38,5},{39,6},{40,7},{41,8},{42... | collective-permute-start | bytes 393224 | tf_op jit(solution)/shard_map/ppermute | solution.py:572
  219.5 13.7 %copy-start.63 = (s32[32,1,96]{2,1,0:T(1,128)S(1)}, s32[32,1,96]{2,1,0:T(1,128)}, u32[]{:S(2)}) copy-start(s32[32,1,96]{2,1,0:T(1,128)} %copy-done.62) | copy-start | bytes 36868
  219.5 33.0 %copy-start.48 = (s32[4]{0:T(128)S(1)}, s32[4]{0:T(128)}, u32[]{:S(2)}) copy-start(s32[4]{0:T(128)} %add_add_fusion.2.info) | copy-start | bytes 52
  222.7 29.7 %copy-start.14 = (bf16[4,64,4096]{2,1,0:T(8,128)(2,1)S(1)}, bf16[4,64,4096]{2,1,0:T(8,128)(2,1)}, u32[]{:S(2)}) copy-start(bf16[4,64,4096]{2,1,0:T(8,128)(2,1)} %copy-done.13) | copy-start | bytes 6291460
  222.7 49.8 %all-to-all-start.3 = ((bf16[32,24,512]{2,1,0:T(8,128)(2,1)}), bf16[32,24,512]{2,1,0:T(8,128)(2,1)}, u32[]{:S(2)}, u32[]{:S(2)}) async-start(bf16[32,24,512]{2,1,0:T(8,128)(2,1)} %bitcast.79), calls=%async_computation.3 | async-start | bytes 1572864 | tf_op jit(solution)/shard_map/all_to_all | solution.py:576
  235.6 16.8 %collective-permute-start.13 = (bf16[64,4096]{1,0:T(8,128)(2,1)}, bf16[64,4096]{1,0:T(8,128)(2,1)}, u32[]{:S(2)}, u32[]{:S(2)}) collective-permute-start(bf16[64,4096]{1,0:T(8,128)(2,1)} %copy-done.50), channel_id=1, source_target_pairs={{32,0},{64,32},{96,64},{33,1},{65,33},{97,65},{34,2},{66,34},{98,6... | collective-permute-start | bytes 1572872 | tf_op jit(solution)/shard_map/ppermute | solution.py:571
  240.7 8.6 %collective-permute-start.14 = (bf16[16,4096]{1,0:T(8,128)(2,1)}, bf16[16,4096]{1,0:T(8,128)(2,1)S(1)}, u32[]{:S(2)}, u32[]{:S(2)}) collective-permute-start(bf16[16,4096]{1,0:T(8,128)(2,1)} %copy-done.52), channel_id=1, source_target_pairs={{33,0},{34,1},{35,2},{36,3},{37,4},{38,5},{39,6},{40,7},{41,8},{42... | collective-permute-start | bytes 393224 | tf_op jit(solution)/shard_map/ppermute | solution.py:572
  268.1 32.8 %collective-permute-start.15 = (bf16[64,4096]{1,0:T(8,128)(2,1)}, bf16[64,4096]{1,0:T(8,128)(2,1)}, u32[]{:S(2)}, u32[]{:S(2)}) collective-permute-start(bf16[64,4096]{1,0:T(8,128)(2,1)} %get-tuple-element.79), channel_id=1, source_target_pairs={{32,0},{64,32},{96,64},{33,1},{65,33},{97,65},{34,2},{66,34},{98,6... | collective-permute-start | bytes 1572872 | tf_op jit(solution)/shard_map/ppermute | solution.py:571
  269.4 31.4 %collective-permute-start.16 = (bf16[16,4096]{1,0:T(8,128)(2,1)}, bf16[16,4096]{1,0:T(8,128)(2,1)S(1)}, u32[]{:S(2)}, u32[]{:S(2)}) collective-permute-start(bf16[16,4096]{1,0:T(8,128)(2,1)} %get-tuple-element.80), channel_id=1, source_target_pairs={{33,0},{34,1},{35,2},{36,3},{37,4},{38,5},{39,6},{40,7},{41,8},{42... | collective-permute-start | bytes 393224 | tf_op jit(solution)/shard_map/ppermute | solution.py:572
  272.5 43.0 %all-to-all-start.2 = ((bf16[32,24,512]{2,1,0:T(8,128)(2,1)}), bf16[32,24,512]{2,1,0:T(8,128)(2,1)}, u32[]{:S(2)}, u32[]{:S(2)}) async-start(bf16[32,24,512]{2,1,0:T(8,128)(2,1)} %bitcast.81), calls=%async_computation.2 | async-start | bytes 1572864 | tf_op jit(solution)/shard_map/all_to_all | solution.py:576
  283.7 17.2 %copy-start.4 = (bf16[1,4,64,4096]{3,2,1,0:T(8,128)(2,1)S(1)}, bf16[1,4,64,4096]{3,2,1,0:T(8,128)(2,1)}, u32[]{:S(2)}) copy-start(bf16[1,4,64,4096]{3,2,1,0:T(8,128)(2,1)} %param.8) | copy-start | bytes 6291460
  283.7 17.2 %copy-start.19 = (bf16[4,64,4096]{2,1,0:T(8,128)(2,1)S(1)}, bf16[4,64,4096]{2,1,0:T(8,128)(2,1)}, u32[]{:S(2)}) copy-start(bf16[4,64,4096]{2,1,0:T(8,128)(2,1)} %top.13) | copy-start | bytes 6291460
  283.7 17.2 %copy-start.33 = (f32[8,80,128]{2,1,0:T(8,128)S(1)}, f32[8,80,128]{2,1,0:T(8,128)}, u32[]{:S(2)}) copy-start(f32[8,80,128]{2,1,0:T(8,128)} %copy-done.29) | copy-start | bytes 983044
  283.7 17.2 %copy-start.47 = (s32[4]{0:T(128)S(1)}, s32[4]{0:T(128)}, u32[]{:S(2)}) copy-start(s32[4]{0:T(128)} %add_add_fusion.1.info) | copy-start | bytes 52
  300.8 12.8 %copy-start.55 = (f32[1024,1024]{1,0:T(8,128)}, f32[1024,1024]{1,0:T(8,128)S(1)}, u32[]{:S(2)}) copy-start(f32[1024,1024]{1,0:T(8,128)S(1)} %owner_add.4.refs_0_) | copy-start | bytes 12582916
  313.7 9.3 %copy-start.45 = (s32[1,768]{1,0:T(1,128)S(1)}, s32[1,768]{1,0:T(1,128)}, u32[]{:S(2)}) copy-start(s32[1,768]{1,0:T(1,128)} %get-tuple-element.93.row_of) | copy-start | bytes 9220
  315.6 48.5 %all-to-all-start = ((bf16[32,24,512]{2,1,0:T(8,128)(2,1)}), bf16[32,24,512]{2,1,0:T(8,128)(2,1)S(1)}, u32[]{:S(2)}, u32[]{:S(2)}) async-start(bf16[32,24,512]{2,1,0:T(8,128)(2,1)} %bitcast.27), calls=%async_computation | async-start | bytes 1572864 | tf_op jit(solution)/shard_map/all_to_all | solution.py:576
  324.0 20.1 %copy-start.42 = (s32[768,1]{1,0:T(8,128)S(1)}, s32[768,1]{1,0:T(8,128)}, u32[]{:S(2)}) copy-start(s32[768,1]{1,0:T(8,128)} %copy.48.head_of) | copy-start | bytes 9220
  344.1 20.0 %copy-start.41 = (s32[768,1]{1,0:T(8,128)S(1)}, s32[768,1]{1,0:T(8,128)}, u32[]{:S(2)}) copy-start(s32[768,1]{1,0:T(8,128)} %copy.49.head_of) | copy-start | bytes 9220
  364.1 2.2 copy-start.57
  (38 other events, 43.4 us)

commit v2 on v1

--- a/solution.py
+++ b/solution.py
@@ -13,6 +13,8 @@
 EPS = 1e-06
 LANES = 128
 MIB = 1 << 20
+UNROLL = (1, 2, 2, 2)
+VMEM_LIMIT = 60 * MIB
 
 f32 = jnp.float32
 bf16 = jnp.bfloat16
@@ -27,7 +29,7 @@
 
 
 def forward_kernel(
-    live_ref, xb, xm, xa, vb, vm, va, taps, hid_out, der_out, scal_out,
+    batch, live_ref, xb, xm, xa, vb, vm, va, taps, order, hid_out, der_out, scal_out,
     x_win, v_win, hid, der, scal, rms_now, sems,
 ):
     width = xm.shape[-1]
@@ -36,19 +38,28 @@
     chunks = width // LANES
     live = live_ref[0]
     length = xm.shape[-2]
+    parts = ((xb, vb, 0, HALO), (xm, vm, HALO, length), (xa, va, HALO + length, HALO))
+    loads = []
+    for i, (x_part, v_part, at, size) in enumerate(parts):
+        for j, (part, window) in enumerate(((x_part, x_win), (v_part, v_win))):
+            loads.append(
+                pltpu.make_async_copy(
+                    part.at[batch], window.at[pl.ds(at, size)], sems.at[2 + j, i]
+                )
+            )
+    for copy in loads:
+        copy.start()
+    for copy in loads:
+        copy.wait()
 
     def load(chunk, sums):
         cols = columns(chunk)
-        for ref, at, size in ((xb, 0, HALO), (xm, HALO, length), (xa, HALO + length, HALO)):
-            x_win[at : at + size, cols] = ref[0, :, cols].astype(f32)
-        for ref, at, size in ((vb, 0, HALO), (vm, HALO, length), (va, HALO + length, HALO)):
-            v_win[at : at + size, cols] = ref[0, :, cols]
-        x = x_win[:, cols]
+        x = x_win[:, cols].astype(f32)
         v = v_win[:, cols]
         return sums[0] + x * x, sums[1] + v * v, sums[2] + x * v
 
     zero = jnp.zeros((rows, LANES), f32)
-    xx, vv, xv = lax.fori_loop(0, chunks, load, (zero, zero, zero))
+    xx, vv, xv = lax.fori_loop(0, chunks, load, (zero, zero, zero), unroll=UNROLL[0])
     xv = row_total(xv)
     rx = lax.rsqrt(row_total(xx) / width + EPS)
     rv = lax.rsqrt(row_total(vv) / width + EPS)
@@ -61,11 +72,11 @@
 
     def mix(chunk, total):
         cols = columns(chunk)
-        hidden = x_win[:, cols] + rms_now[...] * v_win[:, cols]
+        hidden = x_win[:, cols].astype(f32) + rms_now[...] * v_win[:, cols]
         hid[0, :, cols] = hidden
         return total + hidden * hidden
 
-    total = lax.fori_loop(0, chunks, mix, zero)
+    total = lax.fori_loop(0, chunks, mix, zero, unroll=UNROLL[0])
 
     def hidden_copy(layer):
         return pltpu.make_async_copy(
@@ -95,7 +106,7 @@
             hid[layer + 1, :, cols] = after
             return total + after * after
 
-        total = lax.fori_loop(0, chunks, one, zero)
+        total = lax.fori_loop(0, chunks, one, zero, unroll=UNROLL[1])
         slope_copy(layer).start()
         return total
 
@@ -112,45 +123,40 @@
     out.wait()
 
 
-def forward_map(batch, live, x, x_before, x_after, v, v_before, v_after, taps):
+def forward_map(batch, live, x, x_before, x_after, v, v_before, v_after, taps, order):
     length, width = x.shape[1:]
     keep = length + HALO
     rows = keep + HALO
     layers = taps.shape[0]
-
-    def part(size):
-        return pl.BlockSpec((1, size, width), lambda i, *_: (batch, 0, 0))
-
+    hbm = pl.BlockSpec(memory_space=pltpu.HBM)
     return pl.pallas_call(
-        forward_kernel,
+        functools.partial(forward_kernel, batch),
         out_shape=(
             jax.ShapeDtypeStruct((layers, keep, width), f32),
             jax.ShapeDtypeStruct((layers, keep, width), f32),
             jax.ShapeDtypeStruct((8, keep, LANES), f32),
         ),
-        grid_spec=pltpu.PrefetchScalarGridSpec(
-            num_scalar_prefetch=1,
-            grid=(1,),
-            in_specs=[
-                part(HALO), part(length), part(HALO),
-                part(HALO), part(length), part(HALO),
-                pl.BlockSpec(taps.shape, lambda i, *_: (0, 0, 0)),
-            ],
-            out_specs=[pl.BlockSpec(memory_space=pl.ANY)] * 3,
-            scratch_shapes=[
-                pltpu.VMEM((rows, width), f32),
-                pltpu.VMEM((rows, width), f32),
-                pltpu.VMEM((layers + 1, rows, width), f32),
-                pltpu.VMEM((layers, keep, width), f32),
-                pltpu.VMEM((8, keep, LANES), f32),
-                pltpu.VMEM((rows, LANES), f32),
-                pltpu.SemaphoreType.DMA((2, layers + 1)),
-            ],
+        in_specs=[pl.BlockSpec(memory_space=pltpu.SMEM)]
+        + [hbm] * 6
+        + [pl.BlockSpec(memory_space=pltpu.VMEM), pl.BlockSpec(memory_space=pltpu.SMEM)],
+        out_specs=[hbm] * 3,
+        scratch_shapes=[
+            pltpu.VMEM((rows, width), bf16),
+            pltpu.VMEM((rows, width), f32),
+            pltpu.VMEM((layers + 1, rows, width), f32),
+            pltpu.VMEM((layers, keep, width), f32),
+            pltpu.VMEM((8, keep, LANES), f32),
+            pltpu.VMEM((rows, LANES), f32),
+            pltpu.SemaphoreType.DMA((4, layers + 1)),
+        ],
+        compiler_params=pltpu.CompilerParams(vmem_limit_bytes=VMEM_LIMIT),
+        cost_estimate=pl.CostEstimate(
+            flops=30 * layers * rows * width,
+            bytes_accessed=16 * MIB,
+            transcendentals=layers * rows * width,
         ),
-        compiler_params=pltpu.CompilerParams(vmem_limit_bytes=44 * MIB),
-        cost_estimate=pl.CostEstimate(flops=30 * layers * rows * width, bytes_accessed=16 * MIB, transcendentals=layers * rows * width),
         name="forward_map",
-    )(live, x_before, x, x_after, v_before, v, v_after, taps)
+    )(live, x_before, x, x_after, v_before, v, v_after, taps, order)
 
 
 def backward_kernel(
@@ -161,7 +167,7 @@
     if held[2]:
         refs = refs[2:]
     (
-        grad_send, halo_send, grads_all, gv_all,
+        grad_send, halo_send, grads_all, gv_all, order_out,
         hid, der, scal, x_win, v_win, g, u, coef, x_in, xa_in, g_in, ga_in, gv, sems,
     ) = refs
     which = info[0]
@@ -172,6 +178,7 @@
     rows = g.shape[0]
     chunks = width // LANES
     first, count = held[0], held[1]
+    order_out[0] = 0
 
     def scal_copy(i):
         return pltpu.make_async_copy(saved[i][2], scal, sems.at[2, 0])
@@ -247,7 +254,7 @@
             g[length:rows, cols] = ga_in[:, cols].astype(f32)
             return total + into_taps(last, cols, g[:, cols])
 
-        total = lax.fori_loop(0, chunks, begin, zero)
+        total = lax.fori_loop(0, chunks, begin, zero, unroll=UNROLL[2])
 
         def coefficients(layer, total):
             rms = scal[layer]
@@ -269,7 +276,7 @@
                 g[:, cols] = grad
                 return total + into_taps(layer - 1, cols, grad)
 
-            return lax.fori_loop(0, chunks, one, zero)
+            return lax.fori_loop(0, chunks, one, zero, unroll=UNROLL[2])
 
         total = lax.fori_loop(0, live - 1, layer_step, total)
         coefficients(0, total)
@@ -282,7 +289,7 @@
             g[:, cols] = grad
             return total + grad * v_win[:, cols]
 
-        total = row_total(lax.fori_loop(0, chunks, to_gate, zero))
+        total = row_total(lax.fori_loop(0, chunks, to_gate, zero, unroll=UNROLL[3]))
         rx, rv, xv, gate = scal[4], scal[5], scal[6], scal[7]
         both = total * gate * (1.0 - gate) * (1.0 / math.sqrt(width)) * rx * rv
         mean = xv / width
@@ -304,7 +311,7 @@
             gv[:, cols] = grad_v.astype(bf16)
             return carry
 
-        lax.fori_loop(0, chunks, finish, 0)
+        lax.fori_loop(0, chunks, finish, 0, unroll=UNROLL[3])
         outs = (
             pltpu.make_async_copy(grad_send, grads_all.at[which], sems.at[3, 2]),
             pltpu.make_async_copy(gv, gv_all.at[which], sems.at[3, 3]),
@@ -321,6 +328,7 @@
     layers = taps.shape[0]
     flat = [array for group in saved for array in group]
     some = pl.BlockSpec(memory_space=pl.ANY)
+    hbm = pl.BlockSpec(memory_space=pltpu.HBM)
     extra = () if previous is None else previous
     operands = (info, near, near_halo, top, top_halo, x, x_after, v, v_after, taps, *flat, *extra)
     aliases = {} if previous is None else {len(operands) - 2: 2, len(operands) - 1: 3}
@@ -331,12 +339,16 @@
             jax.ShapeDtypeStruct((HALO, width), bf16),
             jax.ShapeDtypeStruct((batches, length, width), bf16),
             jax.ShapeDtypeStruct((batches, length, width), bf16),
+            jax.ShapeDtypeStruct((1,), jnp.int32),
         ),
         in_specs=[pl.BlockSpec(memory_space=pltpu.SMEM)]
-        + [some] * 8
+        + [some] * 2
+        + [hbm] * 6
         + [pl.BlockSpec(memory_space=pltpu.VMEM)]
-        + [some] * (len(flat) + len(extra)),
-        out_specs=[pl.BlockSpec(memory_space=pltpu.VMEM)] * 2 + [some] * 2,
+        + [hbm] * (len(flat) + len(extra)),
+        out_specs=[pl.BlockSpec(memory_space=pltpu.VMEM)] * 2
+        + [hbm] * 2
+        + [pl.BlockSpec(memory_space=pltpu.SMEM)],
         scratch_shapes=[
             pltpu.VMEM((layers, rows, width), f32),
             pltpu.VMEM((layers, rows, width), f32),
@@ -354,13 +366,13 @@
             pltpu.SemaphoreType.DMA((4, 5)),
         ],
         input_output_aliases=aliases,
-        compiler_params=pltpu.CompilerParams(vmem_limit_bytes=44 * MIB),
+        compiler_params=pltpu.CompilerParams(vmem_limit_bytes=VMEM_LIMIT),
         cost_estimate=pl.CostEstimate(flops=25 * layers * rows * width, bytes_accessed=14 * MIB, transcendentals=0),
         name="backward_map",
     )(*operands)
 
 
-def pack_kernel(dest, gv_all, out, stacked):
+def pack_kernel(dest, gv_all, order, arrived, out, stacked):
     heads, width = 8, out.shape[-1]
     length = gv_all.shape[1]
     for head in range(heads):
@@ -380,7 +392,7 @@
     lax.fori_loop(0, slots // step, one, 0)
 
 
-def pack_values(batch, dest, gv_all, slots):
+def pack_values(batch, dest, gv_all, slots, order, arrived):
     batches, length, model = gv_all.shape
     feature = model // 8
     return pl.pallas_call(
@@ -390,90 +402,119 @@
         in_specs=[
             pl.BlockSpec(dest.shape, lambda i: (0, 0)),
             pl.BlockSpec((1, length, model), lambda i: (batch, 0, 0)),
+            pl.BlockSpec(memory_space=pltpu.SMEM),
+            pl.BlockSpec(memory_space=pl.ANY),
         ],
         out_specs=pl.BlockSpec((slots, feature), lambda i: (0, 0)),
         scratch_shapes=[pltpu.VMEM((8 * length, feature), bf16)],
-        compiler_params=pltpu.CompilerParams(vmem_limit_bytes=24 * MIB),
+        compiler_params=pltpu.CompilerParams(vmem_limit_bytes=VMEM_LIMIT),
         cost_estimate=pl.CostEstimate(flops=2 * slots * 8 * length * feature, bytes_accessed=2 * MIB, transcendentals=0),
         name="pack_values",
-    )(dest, gv_all)
-
-
-def owner_kernel(has_table, got, head_of, row_of, weight, *refs):
+    )(dest, gv_all, order, arrived)
+
+
+def owner_kernel(batch, has_table, got, place_of, row_of, groups, order, weight, *refs):
     if has_table:
         table_in, refs = refs[0], refs[1:]
-    table, spread, flat, place, sems = refs
+    table, order_out, sorted_in, rows, place, flat, total, sems = refs
+    heads, row_width, feature = weight.shape
+    table_rows = table.shape[0]
+    slots = got.shape[0]
+    room = place.shape[1]
+    order_out[0] = 0
+    copies = [pltpu.make_async_copy(weight.at[h], flat.at[h], sems.at[h]) for h in range(heads)]
+    for copy in copies:
+        copy.start()
+    if has_table:
+        table_copy = pltpu.make_async_copy(table_in, total, sems.at[heads])
+        table_copy.start()
+    step = 128
+
+    def sort(tile, carry):
+        at = pl.multiple_of(tile * step, step)
+        slot = lax.broadcasted_iota(jnp.int32, (step, slots), 0) + at
+        pick = jnp.where(slot == place_of[batch : batch + 1, :], 1.0, 0.0).astype(bf16)
+        sorted_in[pl.ds(at, step), :] = jnp.dot(
+            pick, got[...], preferred_element_type=f32
+        ).astype(bf16)
+        rows[pl.ds(at, step), :] = jnp.zeros((step, row_width), bf16)
+        return carry
+
+    lax.fori_loop(0, room // step, sort, 0)
+
+    def mark(tile, carry):
+        at = pl.multiple_of(tile * step, step)
+        row = lax.broadcasted_iota(jnp.int32, (step, room), 0) + at
+        place[pl.ds(at, step), :] = jnp.where(
+            row == row_of[batch : batch + 1, :], 1.0, 0.0
+        ).astype(bf16)
+        return carry
+
+    lax.fori_loop(0, table_rows // step, mark, 0)
+
+    for h in range(heads):
+        copies[h].wait()
+
+        def multiply(tile, carry):
+            at = pl.ds(pl.multiple_of(groups[batch, h] + tile * step, 16), step)
+            rows[at, :] = lax.dot_general(
+                sorted_in[at, :], flat[h], (((1,), (1,)), ((), ())), preferred_element_type=f32
+            ).astype(bf16)
+            return carry
+
+        lax.fori_loop(0, groups[batch, heads + h], multiply, 0)
+    if has_table:
+        table_copy.wait()
+    tile = 256
+    outs = []
+    for block in range(row_width // tile):
+        cols = pl.ds(block * tile, tile)
+        part = jnp.dot(place[...], rows[0:room, cols], preferred_element_type=f32)
+        if has_table:
+            part = part + total[:, cols]
+        total[:, cols] = part
+        outs.append(
+            pltpu.make_async_copy(
+                total.at[:, cols], table.at[:, cols], sems.at[heads + 1 + block]
+            )
+        )
+        outs[-1].start()
+    for copy in outs:
+        copy.wait()
+
+
+def owner_add(batch, table, got, place_of, row_of, groups, weight, order):
     heads, row_width, feature = weight.shape
     slots = got.shape[0]
-    copies = [
-        pltpu.make_async_copy(
-            weight.at[h], flat.at[:, pl.ds(h * feature, feature)], sems.at[h]
-        )
-        for h in range(heads)
-    ]
-    for copy in copies:
-        copy.start()
-    step = 128
-
-    def expand(tile, carry):
-        at = pl.ds(pl.multiple_of(tile * step, step), step)
-        own = head_of[at, :]
-        block = got[at, :]
-        for h in range(heads):
-            mask = jnp.broadcast_to(own == h, block.shape)
-            spread[at, h * feature : (h + 1) * feature] = jnp.where(mask, block, jnp.zeros_like(block))
-        return carry
-
-    lax.fori_loop(0, slots // step, expand, 0)
-    table_rows = table.shape[0]
-
-    def mark(tile, carry):
-        at = pl.multiple_of(tile * step, step)
-        row = lax.broadcasted_iota(jnp.int32, (step, slots), 0) + at
-        place[pl.ds(at, step), :] = jnp.where(row == row_of[...], 1.0, 0.0).astype(bf16)
-        return carry
-
-    lax.fori_loop(0, table_rows // step, mark, 0)
-    for copy in copies:
-        copy.wait()
-    tile = 256
-
-    def add(block, carry):
-        at = pl.ds(pl.multiple_of(block * tile, tile), tile)
-        rows = lax.dot_general(
-            spread[...], flat[at, :], (((1,), (1,)), ((), ())), preferred_element_type=f32
-        )
-        total = jnp.dot(place[...], rows.astype(bf16), preferred_element_type=f32)
-        if has_table:
-            total = total + table_in[:, at]
-        table[:, at] = total
-        return carry
-
-    lax.fori_loop(0, row_width // tile, add, 0)
-
-
-def owner_add(table, got, head_of, row_of, weight):
-    heads, row_width, feature = weight.shape
-    slots = got.shape[0]
+    room = row_of.shape[1]
     vmem = pl.BlockSpec(memory_space=pltpu.VMEM)
-    operands = [got, head_of, row_of, weight]
-    specs = [vmem, vmem, vmem, pl.BlockSpec(memory_space=pl.ANY)]
+    hbm = pl.BlockSpec(memory_space=pltpu.HBM)
+    smem = pl.BlockSpec(memory_space=pltpu.SMEM)
+    operands = [got, place_of, row_of, groups, order, weight]
+    specs = [vmem, vmem, vmem, smem, smem, hbm]
     if table is not None:
         operands.append(table)
-        specs.append(vmem)
+        specs.append(hbm)
     return pl.pallas_call(
-        functools.partial(owner_kernel, table is not None),
-        out_shape=jax.ShapeDtypeStruct((TABLE_DEV, row_width), f32),
+        functools.partial(owner_kernel, batch, table is not None),
+        out_shape=(
+            jax.ShapeDtypeStruct((TABLE_DEV, row_width), f32),
+            jax.ShapeDtypeStruct((1,), jnp.int32),
+        ),
         in_specs=specs,
-        out_specs=vmem,
+        out_specs=(hbm, smem),
         scratch_shapes=[
-            pltpu.VMEM((slots, heads * feature), bf16),
-            pltpu.VMEM((row_width, heads * feature), bf16),
-            pltpu.VMEM((TABLE_DEV, slots), bf16),
-            pltpu.SemaphoreType.DMA((heads,)),
+            pltpu.VMEM((room + 128, feature), bf16),
+            pltpu.VMEM((room + 128, row_width), bf16),
+            pltpu.VMEM((TABLE_DEV, room), bf16),
+            pltpu.VMEM((heads, row_width, feature), bf16),
+            pltpu.VMEM((TABLE_DEV, row_width), f32),
+            pltpu.SemaphoreType.DMA((heads + 5,)),
         ],
-        compiler_params=pltpu.CompilerParams(vmem_limit_bytes=48 * MIB),
-        cost_estimate=pl.CostEstimate(flops=2 * slots * row_width * (heads * feature + TABLE_DEV), bytes_accessed=18 * MIB, transcendentals=0),
+        compiler_params=pltpu.CompilerParams(vmem_limit_bytes=VMEM_LIMIT),
+        cost_estimate=pl.CostEstimate(
+            flops=6 * slots * row_width * TABLE_DEV, bytes_accessed=18 * MIB, transcendentals=0
+        ),
         name="owner_add",
     )(*operands)
 
@@ -495,8 +536,25 @@
     return dest, holds
 
 
-def after(value, *others):
-    return lax.optimization_barrier((value, *others))[0]
+def groups_of(holds, heads):
+    batches, slots = holds.shape
+    room = -(-(slots + 15 * heads) // 128) * 128
+    valid = holds >= 0
+    head = jnp.where(valid, holds % heads, -1)
+    member = head[..., None] == jnp.arange(heads, dtype=jnp.int32)
+    order = jnp.arange(slots, dtype=jnp.int32)
+    below = (order[None, :] < order[:, None]).astype(bf16)
+    rank = jnp.einsum("ij,bjh->bih", below, member.astype(bf16), preferred_element_type=f32)
+    counts = jnp.sum(member.astype(jnp.int32), 1)
+    padded = (counts + 15) // 16 * 16
+    number = jnp.arange(heads, dtype=jnp.int32)
+    starts = jnp.sum(jnp.where(number[None, :] < number[:, None], padded[:, None, :], 0), -1)
+    place = jnp.sum(jnp.where(member, rank.astype(jnp.int32) + starts[:, None, :] + 1, 0), -1) - 1
+    spot = jnp.arange(room, dtype=jnp.int32)
+    hit = place[:, None, :] == spot[:, None]
+    row = jnp.sum(jnp.where(hit, (holds // heads)[:, None, :] + 1, 0), -1) - 1
+    groups = jnp.concatenate([starts, (counts + 127) // 128], 1)
+    return place, row, groups
 
 
 def shards(
@@ -534,49 +592,50 @@
     saved = []
     near = jnp.zeros((length, width), bf16)
     near_halo = jnp.zeros((HALO, width), bf16)
-    outputs = None
-    table = None
-    head_of = row_of = dest = None
+    outputs = table = dest = holds = place_of = row_of = groups = got = None
+    order = jnp.zeros((1,), jnp.int32)
     ticks = batches + sections - 1
-    grad_send = None
     for tick in range(ticks):
         if tick < batches:
-            number = live.reshape(1)
-            if tick > 0:
-                number = after(number, grad_send)
             saved.append(
-                forward_map(tick, number, x, x_before, x_after, v, v_before, v_after, taps)
+                forward_map(
+                    tick, live.reshape(1), x, x_before, x_after, v, v_before, v_after, taps, order
+                )
             )
-        if tick == 2:
-            ids = after(row_ids[0], grad_send)
-            dest, holds = slots_of(ids, owners, capacity)
-            holds = holds.reshape(batches, owners, capacity).transpose(1, 0, 2)
-            holds = lax.all_to_all(
-                holds.reshape(owners, batches * capacity), "table", 0, 0, tiled=True
-            )
-            holds = holds.reshape(owners, batches, capacity).transpose(1, 0, 2)
-            holds = holds.reshape(batches, slots)
-            row_of = jnp.where(holds < 0, -1, holds // heads)
-            head_of = jnp.where(holds < 0, -1, holds % heads)
         position = tick - (sections - 1 - section)
         which = jnp.clip(position, 0, batches - 1)
         active = (position >= 0) & (position < batches)
         info = jnp.stack([which, active, is_top, live]).astype(jnp.int32)
         first = max(0, tick - (sections - 1))
-        grad_send, halo_send, *outputs = backward_map(
+        grad_send, halo_send, *outputs, order = backward_map(
             info, near, near_halo, out_grad, top_halo, x, x_after, v, v_after, taps,
             first, saved[first : tick + 1], outputs,
         )
         if tick < ticks - 1:
             near = lax.ppermute(grad_send, "section", down)
             near_halo = lax.ppermute(halo_send, ("section", "table"), down_halo)
+        if tick == 0:
+            dest, holds = slots_of(row_ids[0] + order, owners, capacity)
+            holds = holds.reshape(batches, owners, capacity).transpose(1, 0, 2)
+            holds = holds.reshape(owners, batches * capacity)
+        if tick == 1:
+            holds = lax.all_to_all(holds + order, "table", 0, 0, tiled=True)
+            holds = holds.reshape(owners, batches, capacity).transpose(1, 0, 2)
+            holds = holds.reshape(batches, slots)
+        if tick == 2:
+            place_of, row_of, groups = groups_of(holds + order, heads)
         batch = tick - (sections - 1)
         if batch >= 0:
-            packed = pack_values(batch, dest[batch][None, :], outputs[1], slots)
+            token = order
+            if got is not None:
+                table, token = owner_add(
+                    batch - 1, table, got, place_of, row_of, groups, weight, order
+                )
+            packed = pack_values(
+                batch, dest[batch][None, :], outputs[1], slots, token, near_halo
+            )
             got = lax.all_to_all(packed, "table", 0, 0, tiled=True)
-            table = owner_add(
-                table, got, head_of[batch][:, None], row_of[batch][None, :], weight
-            )
+    table, _ = owner_add(batches - 1, table, got, place_of, row_of, groups, weight, order)
     return (outputs[0][None], table[None])
 
 

time: 388 us -> 380 us (0.979); the launches traced: 384 us -> 382 us
  waiting for transfers between devices: 54.1 us -> 103 us
  local copies, waits for them, and re-layouts: 65.4 us -> 26.5 us
  Pallas kernels: 172 us -> 145 us
  blocking collectives: 0 us -> 22.3 us
  starting transfers between devices: 79.6 us -> 67.1 us
  other arithmetic: 8.42 us -> 13.2 us
    ppermute x6, waiting for transfers between devices: 8.08 us -> 58.4 us  [shards(): near = lax.ppermute(grad_send, 'section', down)]
    unnamed x128 -> x54, local copies, waits for them, and re-layouts: 46.7 us -> 12.4 us
    pallas_call x8, Pallas kernels: 115 us -> 88.2 us  [the longest x4 49.6 us: owner_add(): pl.pallas_call(functools.partial(owner_kernel, batch, table is not None),...]
    all_to_all x0 -> x1, blocking collectives: none -> 22.3 us  [shards(): got = lax.all_to_all(packed, 'table', 0, 0, tiled=True)]
    all_to_all x4 -> x3, starting transfers between devices: 33.7 us -> 22.2 us  [shards(): got = lax.all_to_all(packed, 'table', 0, 0, tiled=True)]
    pallas_call x4, Pallas kernels: 4.67 us -> 14 us  [pack_values(): pl.pallas_call(pack_kernel, out_shape=jax.ShapeDtypeStruct((slots, featur...]
    pallas_call x7, Pallas kernels: 52.1 us -> 43.3 us  [backward_map(): pl.pallas_call(functools.partial(backward_kernel, (first, len(saved), pre...]
    ppermute x1, waiting for transfers between devices: 0.01 us -> 6.9 us  [shards(): v_before = lax.ppermute(v[:, length - HALO:], 'table', to_next)]
  transfers between devices with their start and end apart: 22 -> 21, of which waited for: 9 -> 8; matrix products, arithmetic and copies ran while one was open for 5% -> 7% of each run, Pallas kernels for 39% -> 24%
where the time goes in v2:
time: 380 us; the launch traced here: 382 us
  Pallas kernels  145 us (38%)
  waiting for transfers between devices  103 us (27%)
  starting transfers between devices  67.1 us (18%)
  local copies, waits for them, and re-layouts  26.5 us (7%)
  blocking collectives  22.3 us (6%)
  other arithmetic  13.2 us (3%)
    ppermute x6, waiting for transfers between devices, shards(): near = lax.ppermute(grad_send, 'section', down)  58.4 us
    pallas_call x4, Pallas kernels, owner_add(): pl.pallas_call(functools.partial(owner_kernel, batch, table is not None),...  49.6 us
    pallas_call x7, Pallas kernels, backward_map(): pl.pallas_call(functools.partial(backward_kernel, (first, len(saved), pre...  43.3 us
    pallas_call x4, Pallas kernels, forward_map(): pl.pallas_call(functools.partial(forward_kernel, batch), out_shape=(jax.S...  38.6 us
    ppermute x6, waiting for transfers between devices, shards(): near_halo = lax.ppermute(halo_send, ('section', 'table'), down_halo)  34.7 us
    all_to_all x1, blocking collectives, shards(): got = lax.all_to_all(packed, 'table', 0, 0, tiled=True)  22.3 us
    all_to_all x3, starting transfers between devices, shards(): got = lax.all_to_all(packed, 'table', 0, 0, tiled=True)  22.2 us
    all_to_all x1, starting transfers between devices, shards(): holds = lax.all_to_all(holds + order, 'table', 0, 0, tiled=True)  16.2 us
  transfers between devices with their start and end apart: 21, of which 8 were waited for; matrix products, arithmetic and copies ran while one was open for 7% of the time, Pallas kernels for 24%

profile of v2, /device:TPU:1, one launch (start us, length us, event | category | flops | bytes accessed | tf_op | source)
XLA Modules:
  0.0 382.3 jit_solution(11206337381024463811)
XLA Ops:
  0.6 1.9 slice.27
  2.5 3.3 collective-permute-start
  5.8 2.3 fusion.39
  8.1 1.9 collective-permute-start.1
  10.1 4.7 %copy.33 = bf16[4,64,8,1024]{3,1,0,2:T(8,128)(2,1)S(1)} copy(bf16[4,64,8,1024]{3,2,1,0:T(8,128)(2,1)} %bitcast.104) | data formatting | bytes 8388608 | tf_op jit(solution)/shard_map/squeeze | solution.py:587
  14.7 2.3 fusion.36
  17.5 2.0 copy-done
  19.5 1.5 fusion.38
  21.0 1.9 collective-permute-start.2
  22.9 3.6 collective-permute-start.3
  26.6 2.4 collective-permute-start.4
  32.9 1.7 bitcast_multiply_fusion.taps
  34.7 2.7 collective-permute-done.2.va.va_all
  37.3 6.9 %collective-permute-done.4.vb = f32[4,16,4096]{2,1,0:T(8,128)S(1)} collective-permute-done((f32[4,16,4096]{2,1,0:T(8,128)}, f32[4,16,4096]{2,1,0:T(8,128)S(1)}, u32[]{:S(2)}, u32[]{:S(2)}) %collective-permute-start.4) | collective-permute-done | bytes 1048608 | tf_op jit(solution)/shard_map/ppermute | solution.py:589
  45.2 9.2 %forward_map.4 = (f32[4,80,4096]{2,1,0:T(8,128)}, f32[4,80,4096]{2,1,0:T(8,128)}, f32[8,80,128]{2,1,0:T(8,128)}) custom-call(s32[1]{0:T(128)S(6)} %copy.51.live_ref, bf16[4,16,4096]{2,1,0:T(8,128)(2,1)} %collective-permute-done.3.xb, bf16[4,64,4096]{2,1,0:T(8,128)(2,1)} %bitcast.86, bf16[4,16,4096]{2,1,0:T(8,128)(2,1)} %copy-done.2, ...), custom_call_target="tpu_custom_call" | custom-call | flops 47185920 | bytes 16777216 | tf_op jit(solution)/shard_map/forward_map/pallas_call | solution.py:132
  56.0 2.0 backward_map.7
  60.0 1.3 collective-permute-start.6
  61.4 9.8 %forward_map.5 = (f32[4,80,4096]{2,1,0:T(8,128)}, f32[4,80,4096]{2,1,0:T(8,128)}, f32[8,80,128]{2,1,0:T(8,128)}) custom-call(s32[1]{0:T(128)S(6)} %copy.51.live_ref, bf16[4,16,4096]{2,1,0:T(8,128)(2,1)} %collective-permute-done.3.xb, bf16[4,64,4096]{2,1,0:T(8,128)(2,1)} %bitcast.88, bf16[4,16,4096]{2,1,0:T(8,128)(2,1)} %copy-done.2, ...), custom_call_target="tpu_custom_call" | custom-call | flops 47185920 | bytes 16777216 | tf_op jit(solution)/shard_map/forward_map/pallas_call | solution.py:132
  73.3 2.0 backward_map.8
  80.1 16.2 %all-to-all-start.1 = ((s32[32,1,96]{2,1,0:T(1,128)}), s32[32,1,96]{2,1,0:T(1,128)S(1)}, u32[]{:S(2)}, u32[]{:S(2)}) async-start(s32[32,1,96]{2,1,0:T(1,128)} %bitcast.32), calls=%async_computation.1 | async-start | bytes 32768 | tf_op jit(solution)/shard_map/all_to_all | solution.py:622
  96.9 9.7 %forward_map.6 = (f32[4,80,4096]{2,1,0:T(8,128)}, f32[4,80,4096]{2,1,0:T(8,128)}, f32[8,80,128]{2,1,0:T(8,128)}) custom-call(s32[1]{0:T(128)S(6)} %copy.51.live_ref, bf16[4,16,4096]{2,1,0:T(8,128)(2,1)} %collective-permute-done.3.xb, bf16[4,64,4096]{2,1,0:T(8,128)(2,1)} %bitcast.90, bf16[4,16,4096]{2,1,0:T(8,128)(2,1)} %copy-done.2, ...), custom_call_target="tpu_custom_call" | custom-call | flops 47185920 | bytes 16777216 | tf_op jit(solution)/shard_map/forward_map/pallas_call | solution.py:132
  107.5 2.0 backward_map.9
  109.5 1.3 collective-permute-start.9
  110.8 1.3 collective-permute-start.10
  113.3 9.9 %forward_map.7 = (f32[4,80,4096]{2,1,0:T(8,128)}, f32[4,80,4096]{2,1,0:T(8,128)}, f32[8,80,128]{2,1,0:T(8,128)}) custom-call(s32[1]{0:T(128)S(6)} %copy.51.live_ref, bf16[4,16,4096]{2,1,0:T(8,128)(2,1)} %collective-permute-done.3.xb, bf16[4,64,4096]{2,1,0:T(8,128)(2,1)} %bitcast.92, bf16[4,16,4096]{2,1,0:T(8,128)(2,1)} %copy-done.2, ...), custom_call_target="tpu_custom_call" | custom-call | flops 47185920 | bytes 16777216 | tf_op jit(solution)/shard_map/forward_map/pallas_call | solution.py:132
  123.3 13.8 %collective-permute-done.10.near_halo = bf16[16,4096]{1,0:T(8,128)(2,1)S(1)} collective-permute-done((bf16[16,4096]{1,0:T(8,128)(2,1)}, bf16[16,4096]{1,0:T(8,128)(2,1)S(1)}, u32[]{:S(2)}, u32[]{:S(2)}) %collective-permute-start.10) | collective-permute-done | bytes 131104 | tf_op jit(solution)/shard_map/ppermute | solution.py:616
  138.5 9.3 %backward_map.10 = (bf16[64,4096]{1,0:T(8,128)(2,1)}, bf16[16,4096]{1,0:T(8,128)(2,1)}, bf16[4,64,4096]{2,1,0:T(8,128)(2,1)}, bf16[4,64,4096]{2,1,0:T(8,128)(2,1)}, s32[1]{0:T(128)}) custom-call(s32[4]{0:T(128)} %add_add_fusion.5.info, bf16[64,4096]{1,0:T(8,128)(2,1)} %copy-done.10, ...), custom_call_target="tpu_custom_call", output_to_operand_aliasing={{2}: (22, {}), {3}: (23, {})} | custom-call | flops 32768000 | bytes 14680064 | tf_op jit(solution)/shard_map/backward_map/pallas_call | solution.py:335
  147.8 1.4 collective-permute-start.12
  149.7 20.8 %collective-permute-done.12.near_halo.arrived = bf16[16,4096]{1,0:T(8,128)(2,1)S(1)} collective-permute-done((bf16[16,4096]{1,0:T(8,128)(2,1)}, bf16[16,4096]{1,0:T(8,128)(2,1)S(1)}, u32[]{:S(2)}, u32[]{:S(2)}) %collective-permute-start.12) | collective-permute-done | bytes 131104 | tf_op jit(solution)/shard_map/ppermute | solution.py:616
  171.1 3.6 pack_values.4
  174.7 6.7 %all-to-all-start = ((bf16[32,24,512]{2,1,0:T(8,128)(2,1)}), bf16[32,24,512]{2,1,0:T(8,128)(2,1)S(1)}, u32[]{:S(2)}, u32[]{:S(2)}) async-start(bf16[32,24,512]{2,1,0:T(8,128)(2,1)} %bitcast.107), calls=%async_computation | async-start | bytes 1572864 | tf_op jit(solution)/shard_map/all_to_all | solution.py:637
  183.3 1.4 select_reduce_fusion
  185.3 22.7 %collective-permute-done.11.near = bf16[64,4096]{1,0:T(8,128)(2,1)S(1)} collective-permute-done((bf16[64,4096]{1,0:T(8,128)(2,1)S(1)}, bf16[64,4096]{1,0:T(8,128)(2,1)S(1)}, u32[]{:S(2)}, u32[]{:S(2)}) %collective-permute-start.11) | collective-permute-done | bytes 524320 | tf_op jit(solution)/shard_map/ppermute | solution.py:615
  208.8 9.3 %backward_map.11 = (bf16[64,4096]{1,0:T(8,128)(2,1)}, bf16[16,4096]{1,0:T(8,128)(2,1)}, bf16[4,64,4096]{2,1,0:T(8,128)(2,1)}, bf16[4,64,4096]{2,1,0:T(8,128)(2,1)}, s32[1]{0:T(128)}) custom-call(s32[4]{0:T(128)} %add_add_fusion.4.info, bf16[64,4096]{1,0:T(8,128)(2,1)} %copy-done.14, ...), custom_call_target="tpu_custom_call", output_to_operand_aliasing={{2}: (19, {}), {3}: (20, {})} | custom-call | flops 32768000 | bytes 14680064 | tf_op jit(solution)/shard_map/backward_map/pallas_call | solution.py:335
  220.3 12.4 %owner_add.4 = (f32[1024,1024]{1,0:T(8,128)}, s32[1]{0:T(128)}) custom-call(bf16[768,512]{1,0:T(8,128)(2,1)} %bitcast.111, s32[4,768]{1,0:T(4,128)} %copy-done.22, s32[4,896]{1,0:T(4,128)} %broadcast_add_fusion.row_of, s32[4,16]{1,0:T(4,128)} %pad_add_fusion.groups, s32[1]{0:T(128)} %get-tuple-element.96.order, bf16[8,1024,512]{2,1,0:T(8,128)(2,1)} %bitcast.100), custom_call_target="tpu_custom_call" | custom-call | flops 4831838208 | bytes 18874368 | tf_op jit(solution)/shard_map/owner_add/pallas_call | solution.py:498
  233.4 3.5 pack_values.5
  236.9 7.8 %all-to-all-start.2 = ((bf16[32,24,512]{2,1,0:T(8,128)(2,1)}), bf16[32,24,512]{2,1,0:T(8,128)(2,1)S(1)}, u32[]{:S(2)}, u32[]{:S(2)}) async-start(bf16[32,24,512]{2,1,0:T(8,128)(2,1)} %bitcast.106), calls=%async_computation.2 | async-start | bytes 1572864 | tf_op jit(solution)/shard_map/all_to_all | solution.py:637
  246.6 19.8 %collective-permute-done.13.near = bf16[64,4096]{1,0:T(8,128)(2,1)S(1)} collective-permute-done((bf16[64,4096]{1,0:T(8,128)(2,1)S(1)}, bf16[64,4096]{1,0:T(8,128)(2,1)S(1)}, u32[]{:S(2)}, u32[]{:S(2)}) %collective-permute-start.13) | collective-permute-done | bytes 524320 | tf_op jit(solution)/shard_map/ppermute | solution.py:615
  267.1 9.3 %backward_map.12 = (bf16[64,4096]{1,0:T(8,128)(2,1)}, bf16[16,4096]{1,0:T(8,128)(2,1)}, bf16[4,64,4096]{2,1,0:T(8,128)(2,1)}, bf16[4,64,4096]{2,1,0:T(8,128)(2,1)}, s32[1]{0:T(128)}) custom-call(s32[4]{0:T(128)} %add_add_fusion.3.info, bf16[64,4096]{1,0:T(8,128)(2,1)} %copy-done.13, ...), custom_call_target="tpu_custom_call", output_to_operand_aliasing={{2}: (16, {}), {3}: (17, {})} | custom-call | flops 32768000 | bytes 14680064 | tf_op jit(solution)/shard_map/backward_map/pallas_call | solution.py:335
  278.7 12.4 %owner_add.5 = (f32[1024,1024]{1,0:T(8,128)}, s32[1]{0:T(128)}) custom-call(bf16[768,512]{1,0:T(8,128)(2,1)} %bitcast.110, s32[4,768]{1,0:T(4,128)} %copy-done.22, s32[4,896]{1,0:T(4,128)} %broadcast_add_fusion.row_of, s32[4,16]{1,0:T(4,128)} %pad_add_fusion.groups, s32[1]{0:T(128)} %get-tuple-element.98.order, bf16[8,1024,512]{2,1,0:T(8,128)(2,1)} %bitcast.101, ...), custom_call_target="tpu_custom_call" | custom-call | flops 4831838208 | bytes 18874368 | tf_op jit(solution)/shard_map/owner_add/pallas_call | solution.py:498
  291.8 3.5 pack_values.6
  295.3 7.8 %all-to-all-start.3 = ((bf16[32,24,512]{2,1,0:T(8,128)(2,1)}), bf16[32,24,512]{2,1,0:T(8,128)(2,1)S(1)}, u32[]{:S(2)}, u32[]{:S(2)}) async-start(bf16[32,24,512]{2,1,0:T(8,128)(2,1)} %bitcast.105), calls=%async_computation.3 | async-start | bytes 1572864 | tf_op jit(solution)/shard_map/all_to_all | solution.py:637
  305.1 15.4 %collective-permute-done.15.near = bf16[64,4096]{1,0:T(8,128)(2,1)S(1)} collective-permute-done((bf16[64,4096]{1,0:T(8,128)(2,1)S(1)}, bf16[64,4096]{1,0:T(8,128)(2,1)S(1)}, u32[]{:S(2)}, u32[]{:S(2)}) %collective-permute-start.15) | collective-permute-done | bytes 524320 | tf_op jit(solution)/shard_map/ppermute | solution.py:615
  321.3 9.3 %backward_map.13 = (bf16[64,4096]{1,0:T(8,128)(2,1)}, bf16[16,4096]{1,0:T(8,128)(2,1)}, bf16[4,64,4096]{2,1,0:T(8,128)(2,1)}, bf16[4,64,4096]{2,1,0:T(8,128)(2,1)}, s32[1]{0:T(128)}) custom-call(s32[4]{0:T(128)} %add_add_fusion.2.info, bf16[64,4096]{1,0:T(8,128)(2,1)} %copy-done.17, ...), custom_call_target="tpu_custom_call", output_to_operand_aliasing={{2}: (13, {}), {3}: (14, {})} | custom-call | flops 32768000 | bytes 14680064 | tf_op jit(solution)/shard_map/backward_map/pallas_call | solution.py:335
  331.5 12.4 %owner_add.6 = (f32[1024,1024]{1,0:T(8,128)}, s32[1]{0:T(128)}) custom-call(bf16[768,512]{1,0:T(8,128)(2,1)} %bitcast.109, s32[4,768]{1,0:T(4,128)} %copy-done.22, s32[4,896]{1,0:T(4,128)} %broadcast_add_fusion.row_of, s32[4,16]{1,0:T(4,128)} %pad_add_fusion.groups, s32[1]{0:T(128)} %get-tuple-element.101.order, bf16[8,1024,512]{2,1,0:T(8,128)(2,1)} %bitcast.102, ...), custom_call_target="tpu_custom_call" | custom-call | flops 4831838208 | bytes 18874368 | tf_op jit(solution)/shard_map/owner_add/pallas_call | solution.py:498
  344.0 3.4 pack_values.7
  347.4 22.3 %all_to_all.50 = bf16[32,24,512]{2,1,0:T(8,128)(2,1)} all-to-all(bf16[32,24,512]{2,1,0:T(8,128)(2,1)} %bitcast.108), channel_id=1, replica_groups=mesh['section'=4,'table'=32] {'table'}, dimensions={0} | all-to-all | bytes 1572864 | tf_op jit(solution)/shard_map/all_to_all | solution.py:637
  369.7 12.4 %owner_add.7 = (f32[1024,1024]{1,0:T(8,128)}, s32[1]{0:T(128)}) custom-call(bf16[768,512]{1,0:T(8,128)(2,1)} %bitcast.112, s32[4,768]{1,0:T(4,128)} %copy-done.22, s32[4,896]{1,0:T(4,128)} %broadcast_add_fusion.row_of, s32[4,16]{1,0:T(4,128)} %pad_add_fusion.groups, s32[1]{0:T(128)} %get-tuple-element.101.order, bf16[8,1024,512]{2,1,0:T(8,128)(2,1)} %bitcast.103, ...), custom_call_target="tpu_custom_call" | custom-call | flops 4831838208 | bytes 18874368 | tf_op jit(solution)/shard_map/owner_add/pallas_call | solution.py:498
  (111 shorter events, 35.5 us)
Async XLA Ops:
  2.5 51.9 %collective-permute-start = (bf16[4,16,4096]{2,1,0:T(8,128)(2,1)}, bf16[4,16,4096]{2,1,0:T(8,128)(2,1)S(1)}, u32[]{:S(2)}, u32[]{:S(2)}) collective-permute-start(bf16[4,16,4096]{2,1,0:T(8,128)(2,1)} %slice.27), channel_id=1, source_target_pairs={{1,0},{2,1},{3,2},{4,3},{5,4},{6,5},{7,6},{8,7},{9,8},{10,9},{11,1... | collective-permute-start | bytes 1572872 | tf_op jit(solution)/shard_map/ppermute | solution.py:586
  8.1 26.5 %collective-permute-start.1 = (bf16[4,16,4096]{2,1,0:T(8,128)(2,1)}, bf16[4,16,4096]{2,1,0:T(8,128)(2,1)S(1)}, u32[]{:S(2)}, u32[]{:S(2)}) collective-permute-start(bf16[4,16,4096]{2,1,0:T(8,128)(2,1)} %get-tuple-element.111), channel_id=1, source_target_pairs={{1,0},{2,1},{3,2},{4,3},{5,4},{6,5},{7,6},{8,7},{9,8},{10,9},{11,1... | collective-permute-start | bytes 1572872 | tf_op jit(solution)/shard_map/ppermute | solution.py:585
  10.0 4.7 %copy-start.5 = (bf16[1,8,1024,512]{3,2,1,0:T(8,128)(2,1)S(1)}, bf16[1,8,1024,512]{3,2,1,0:T(8,128)(2,1)}, u32[]{:S(2)}) copy-start(bf16[1,8,1024,512]{3,2,1,0:T(8,128)(2,1)} %param.10) | copy-start | bytes 25165828
  17.5 2.0 copy-start
  17.5 15.4 %copy-start.21 = (f32[1,4,4096]{2,1,0:T(4,128)S(1)}, f32[1,4,4096]{2,1,0:T(4,128)}, u32[]{:S(2)}) copy-start(f32[1,4,4096]{2,1,0:T(4,128)} %param.12) | copy-start | bytes 196612
  21.0 16.3 %collective-permute-start.2 = (f32[4,16,4096]{2,1,0:T(8,128)}, f32[4,16,4096]{2,1,0:T(8,128)S(1)}, u32[]{:S(2)}, u32[]{:S(2)}) collective-permute-start(f32[4,16,4096]{2,1,0:T(8,128)} %get-tuple-element.109), channel_id=1, source_target_pairs={{1,0},{2,1},{3,2},{4,3},{5,4},{6,5},{7,6},{8,7},{9,8},{10,9},{11,1... | collective-permute-start | bytes 3145736 | tf_op jit(solution)/shard_map/ppermute | solution.py:590
  22.9 11.7 %collective-permute-start.3 = (bf16[4,16,4096]{2,1,0:T(8,128)(2,1)}, bf16[4,16,4096]{2,1,0:T(8,128)(2,1)}, u32[]{:S(2)}, u32[]{:S(2)}) collective-permute-start(bf16[4,16,4096]{2,1,0:T(8,128)(2,1)} %get-tuple-element.110), channel_id=1, source_target_pairs={{0,1},{1,2},{2,3},{3,4},{4,5},{5,6},{6,7},{7,8},{8,9},{9,10},{10,1... | collective-permute-start | bytes 1572872 | tf_op jit(solution)/shard_map/ppermute | solution.py:584
  26.6 17.7 %collective-permute-start.4 = (f32[4,16,4096]{2,1,0:T(8,128)}, f32[4,16,4096]{2,1,0:T(8,128)S(1)}, u32[]{:S(2)}, u32[]{:S(2)}) collective-permute-start(f32[4,16,4096]{2,1,0:T(8,128)} %get-tuple-element.108), channel_id=1, source_target_pairs={{0,1},{1,2},{2,3},{3,4},{4,5},{5,6},{6,7},{7,8},{8,9},{9,10},{10,1... | collective-permute-start | bytes 3145736 | tf_op jit(solution)/shard_map/ppermute | solution.py:589
  34.7 9.6 %copy-start.2 = (bf16[4,16,4096]{2,1,0:T(8,128)(2,1)}, bf16[4,16,4096]{2,1,0:T(8,128)(2,1)S(1)}, u32[]{:S(2)}) copy-start(bf16[4,16,4096]{2,1,0:T(8,128)(2,1)S(1)} %collective-permute-done.1.xa.xa_all) | copy-start | bytes 1572868
  37.3 6.9 %copy-start.1 = (f32[4,16,4096]{2,1,0:T(8,128)}, f32[4,16,4096]{2,1,0:T(8,128)S(1)}, u32[]{:S(2)}) copy-start(f32[4,16,4096]{2,1,0:T(8,128)S(1)} %collective-permute-done.2.va.va_all) | copy-start | bytes 3145732
  44.2 1.0 copy-start.4
  54.4 1.6 copy-start.3
  56.0 2.0 copy-start.23
  58.7 13.7 %collective-permute-start.5 = (bf16[64,4096]{1,0:T(8,128)(2,1)}, bf16[64,4096]{1,0:T(8,128)(2,1)S(1)}, u32[]{:S(2)}, u32[]{:S(2)}) collective-permute-start(bf16[64,4096]{1,0:T(8,128)(2,1)} %get-tuple-element.57), channel_id=1, source_target_pairs={{32,0},{64,32},{96,64},{33,1},{65,33},{97,65},{34,2},{66,34},{98,6... | collective-permute-start | bytes 1572872 | tf_op jit(solution)/shard_map/ppermute | solution.py:615
  60.0 12.4 %collective-permute-start.6 = (bf16[16,4096]{1,0:T(8,128)(2,1)}, bf16[16,4096]{1,0:T(8,128)(2,1)S(1)}, u32[]{:S(2)}, u32[]{:S(2)}) collective-permute-start(bf16[16,4096]{1,0:T(8,128)(2,1)} %get-tuple-element.58), channel_id=1, source_target_pairs={{33,0},{34,1},{35,2},{36,3},{37,4},{38,5},{39,6},{40,7},{41,8},{42... | collective-permute-start | bytes 393224 | tf_op jit(solution)/shard_map/ppermute | solution.py:616
  72.4 0.6 copy-start.20
  72.5 0.8 copy-start.12
  75.3 31.4 %collective-permute-start.7 = (bf16[64,4096]{1,0:T(8,128)(2,1)}, bf16[64,4096]{1,0:T(8,128)(2,1)S(1)}, u32[]{:S(2)}, u32[]{:S(2)}) collective-permute-start(bf16[64,4096]{1,0:T(8,128)(2,1)} %get-tuple-element.65), channel_id=1, source_target_pairs={{32,0},{64,32},{96,64},{33,1},{65,33},{97,65},{34,2},{66,34},{98,6... | collective-permute-start | bytes 1572872 | tf_op jit(solution)/shard_map/ppermute | solution.py:615
  77.4 29.2 %collective-permute-start.8 = (bf16[16,4096]{1,0:T(8,128)(2,1)}, bf16[16,4096]{1,0:T(8,128)(2,1)S(1)}, u32[]{:S(2)}, u32[]{:S(2)}) collective-permute-start(bf16[16,4096]{1,0:T(8,128)(2,1)} %get-tuple-element.66), channel_id=1, source_target_pairs={{33,0},{34,1},{35,2},{36,3},{37,4},{38,5},{39,6},{40,7},{41,8},{42... | collective-permute-start | bytes 393224 | tf_op jit(solution)/shard_map/ppermute | solution.py:616
  80.1 32.0 %all-to-all-start.1 = ((s32[32,1,96]{2,1,0:T(1,128)}), s32[32,1,96]{2,1,0:T(1,128)S(1)}, u32[]{:S(2)}, u32[]{:S(2)}) async-start(s32[32,1,96]{2,1,0:T(1,128)} %bitcast.32), calls=%async_computation.1 | async-start | bytes 32768 | tf_op jit(solution)/shard_map/all_to_all | solution.py:622
  106.7 0.7 copy-start.19
  106.7 0.8 copy-start.11
  109.5 28.2 %collective-permute-start.9 = (bf16[64,4096]{1,0:T(8,128)(2,1)}, bf16[64,4096]{1,0:T(8,128)(2,1)S(1)}, u32[]{:S(2)}, u32[]{:S(2)}) collective-permute-start(bf16[64,4096]{1,0:T(8,128)(2,1)} %get-tuple-element.73), channel_id=1, source_target_pairs={{32,0},{64,32},{96,64},{33,1},{65,33},{97,65},{34,2},{66,34},{98,6... | collective-permute-start | bytes 1572872 | tf_op jit(solution)/shard_map/ppermute | solution.py:615
  110.8 26.3 %collective-permute-start.10 = (bf16[16,4096]{1,0:T(8,128)(2,1)}, bf16[16,4096]{1,0:T(8,128)(2,1)S(1)}, u32[]{:S(2)}, u32[]{:S(2)}) collective-permute-start(bf16[16,4096]{1,0:T(8,128)(2,1)} %get-tuple-element.74), channel_id=1, source_target_pairs={{33,0},{34,1},{35,2},{36,3},{37,4},{38,5},{39,6},{40,7},{41,8},{42... | collective-permute-start | bytes 393224 | tf_op jit(solution)/shard_map/ppermute | solution.py:616
  137.2 0.7 copy-start.18
  137.7 0.8 copy-start.10
  147.8 34.2 %copy-start.26 = (bf16[64,4096]{1,0:T(8,128)(2,1)S(1)}, bf16[64,4096]{1,0:T(8,128)(2,1)}, u32[]{:S(2)}) copy-start(bf16[64,4096]{1,0:T(8,128)(2,1)} %get-tuple-element.81) | copy-start | bytes 1572868
  147.8 22.6 %collective-permute-start.12 = (bf16[16,4096]{1,0:T(8,128)(2,1)}, bf16[16,4096]{1,0:T(8,128)(2,1)S(1)}, u32[]{:S(2)}, u32[]{:S(2)}) collective-permute-start(bf16[16,4096]{1,0:T(8,128)(2,1)} %get-tuple-element.82), channel_id=1, source_target_pairs={{33,0},{34,1},{35,2},{36,3},{37,4},{38,5},{39,6},{40,7},{41,8},{42... | collective-permute-start | bytes 393224 | tf_op jit(solution)/shard_map/ppermute | solution.py:616
  170.5 0.7 copy-start.16
  174.7 44.8 %all-to-all-start = ((bf16[32,24,512]{2,1,0:T(8,128)(2,1)}), bf16[32,24,512]{2,1,0:T(8,128)(2,1)S(1)}, u32[]{:S(2)}, u32[]{:S(2)}) async-start(bf16[32,24,512]{2,1,0:T(8,128)(2,1)} %bitcast.107), calls=%async_computation | async-start | bytes 1572864 | tf_op jit(solution)/shard_map/all_to_all | solution.py:637
  181.4 36.8 %copy-start.22 = (s32[4,768]{1,0:T(4,128)}, s32[4,768]{1,0:T(4,128)S(1)}, u32[]{:S(2)}) copy-start(s32[4,768]{1,0:T(4,128)S(1)} %broadcast_add_fusion.1.place_of) | copy-start | bytes 36868
  182.0 26.0 %collective-permute-start.11 = (bf16[64,4096]{1,0:T(8,128)(2,1)S(1)}, bf16[64,4096]{1,0:T(8,128)(2,1)S(1)}, u32[]{:S(2)}, u32[]{:S(2)}) collective-permute-start(bf16[64,4096]{1,0:T(8,128)(2,1)S(1)} %copy-done.26), channel_id=1, source_target_pairs={{32,0},{64,32},{96,64},{33,1},{65,33},{97,65},{34,2},{66,34},{98,6... | collective-permute-start | bytes 1572872 | tf_op jit(solution)/shard_map/ppermute | solution.py:615
  208.0 0.8 copy-start.14
  218.1 14.6 %collective-permute-start.14 = (bf16[16,4096]{1,0:T(8,128)(2,1)}, bf16[16,4096]{1,0:T(8,128)(2,1)S(1)}, u32[]{:S(2)}, u32[]{:S(2)}) collective-permute-start(bf16[16,4096]{1,0:T(8,128)(2,1)} %get-tuple-element.86), channel_id=1, source_target_pairs={{33,0},{34,1},{35,2},{36,3},{37,4},{38,5},{39,6},{40,7},{41,8},{42... | collective-permute-start | bytes 393224 | tf_op jit(solution)/shard_map/ppermute | solution.py:616
  219.5 0.9 copy-start.9
  232.7 11.9 %copy-start.25 = (bf16[64,4096]{1,0:T(8,128)(2,1)S(1)}, bf16[64,4096]{1,0:T(8,128)(2,1)}, u32[]{:S(2)}) copy-start(bf16[64,4096]{1,0:T(8,128)(2,1)} %get-tuple-element.85) | copy-start | bytes 1572868
  232.7 0.7 copy-start.15
  236.9 40.9 %all-to-all-start.2 = ((bf16[32,24,512]{2,1,0:T(8,128)(2,1)}), bf16[32,24,512]{2,1,0:T(8,128)(2,1)S(1)}, u32[]{:S(2)}, u32[]{:S(2)}) async-start(bf16[32,24,512]{2,1,0:T(8,128)(2,1)} %bitcast.106), calls=%async_computation.2 | async-start | bytes 1572864 | tf_op jit(solution)/shard_map/all_to_all | solution.py:637
  244.7 21.7 %collective-permute-start.13 = (bf16[64,4096]{1,0:T(8,128)(2,1)S(1)}, bf16[64,4096]{1,0:T(8,128)(2,1)S(1)}, u32[]{:S(2)}, u32[]{:S(2)}) collective-permute-start(bf16[64,4096]{1,0:T(8,128)(2,1)S(1)} %copy-done.25), channel_id=1, source_target_pairs={{32,0},{64,32},{96,64},{33,1},{65,33},{97,65},{34,2},{66,34},{98,6... | collective-permute-start | bytes 1572872 | tf_op jit(solution)/shard_map/ppermute | solution.py:615
  266.4 0.8 copy-start.13
  276.5 14.7 %collective-permute-start.16 = (bf16[16,4096]{1,0:T(8,128)(2,1)}, bf16[16,4096]{1,0:T(8,128)(2,1)S(1)}, u32[]{:S(2)}, u32[]{:S(2)}) collective-permute-start(bf16[16,4096]{1,0:T(8,128)(2,1)} %get-tuple-element.90), channel_id=1, source_target_pairs={{33,0},{34,1},{35,2},{36,3},{37,4},{38,5},{39,6},{40,7},{41,8},{42... | collective-permute-start | bytes 393224 | tf_op jit(solution)/shard_map/ppermute | solution.py:616
  277.8 0.9 copy-start.8
  291.1 12.0 %copy-start.24 = (bf16[64,4096]{1,0:T(8,128)(2,1)S(1)}, bf16[64,4096]{1,0:T(8,128)(2,1)}, u32[]{:S(2)}) copy-start(bf16[64,4096]{1,0:T(8,128)(2,1)} %get-tuple-element.89) | copy-start | bytes 1572868
  291.2 0.7 copy-start.6
  295.3 35.3 %all-to-all-start.3 = ((bf16[32,24,512]{2,1,0:T(8,128)(2,1)}), bf16[32,24,512]{2,1,0:T(8,128)(2,1)S(1)}, u32[]{:S(2)}, u32[]{:S(2)}) async-start(bf16[32,24,512]{2,1,0:T(8,128)(2,1)} %bitcast.105), calls=%async_computation.3 | async-start | bytes 1572864 | tf_op jit(solution)/shard_map/all_to_all | solution.py:637
  303.1 17.4 %collective-permute-start.15 = (bf16[64,4096]{1,0:T(8,128)(2,1)S(1)}, bf16[64,4096]{1,0:T(8,128)(2,1)S(1)}, u32[]{:S(2)}, u32[]{:S(2)}) collective-permute-start(bf16[64,4096]{1,0:T(8,128)(2,1)S(1)} %copy-done.24), channel_id=1, source_target_pairs={{32,0},{64,32},{96,64},{33,1},{65,33},{97,65},{34,2},{66,34},{98,6... | collective-permute-start | bytes 1572872 | tf_op jit(solution)/shard_map/ppermute | solution.py:615
  320.5 0.8 copy-start.17
  330.6 0.9 copy-start.7

commit v3 on v2

v3 whole, which is shorter than its diff:
```python
import functools
import math

import jax
import jax.numpy as jnp
from jax import lax
from jax.experimental import pallas as pl
from jax.experimental.pallas import tpu as pltpu
from jax.sharding import PartitionSpec as P

TABLE_DEV = 1024
HALO = 16
EPS = 1e-06
LANES = 128
STEP = 512
SPLIT = 4
MIB = 1 << 20
VMEM_LIMIT = 60 * MIB

f32 = jnp.float32
bf16 = jnp.bfloat16


def row_total(partial):
    return jnp.broadcast_to(jnp.sum(partial, -1, keepdims=True), partial.shape)


def columns(chunk):
    return pl.ds(pl.multiple_of(chunk * STEP, STEP), STEP)


def wide(narrow):
    return jnp.concatenate([narrow] * (STEP // LANES), 1)


def fold(chunk):
    return sum(chunk[:, i : i + LANES] for i in range(0, STEP, LANES))


def forward_kernel(
    batch, live_ref, xb, xm, xa, vb, vm, va, taps, order, hid_out, der_out, scal_out,
    x_win, v_win, hid, der, scal, rms_now, sems,
):
    width = xm.shape[-1]
    rows = x_win.shape[0]
    keep = rows - HALO
    chunks = width // STEP
    live = live_ref[0]
    length = xm.shape[-2]
    parts = ((xb, vb, 0, HALO), (xm, vm, HALO, length), (xa, va, HALO + length, HALO))
    loads = []
    for q in range(SPLIT):
        cols = pl.ds(q * (width // SPLIT), width // SPLIT)
        loads.append([])
        for i, (x_part, v_part, at, size) in enumerate(parts):
            for j, (part, window) in enumerate(((x_part, x_win), (v_part, v_win))):
                loads[q].append(
                    pltpu.make_async_copy(
                        part.at[batch, :, cols],
                        window.at[pl.ds(at, size), cols],
                        sems.at[2 + 3 * j + i, q],
                    )
                )
                loads[q][-1].start()

    def load(chunk, sums):
        cols = columns(chunk)
        x = x_win[:, cols].astype(f32)
        v = v_win[:, cols]
        return sums[0] + fold(x * x), sums[1] + fold(v * v), sums[2] + fold(x * v)

    zero = jnp.zeros((rows, LANES), f32)
    sums = (zero, zero, zero)
    for q in range(SPLIT):
        for copy in loads[q]:
            copy.wait()
        sums = lax.fori_loop(q * chunks // SPLIT, (q + 1) * chunks // SPLIT, load, sums)
    xx, vv, xv = sums
    xv = row_total(xv)
    rx = lax.rsqrt(row_total(xx) / width + EPS)
    rv = lax.rsqrt(row_total(vv) / width + EPS)
    gate = jax.nn.sigmoid(rx * rv * xv / math.sqrt(width))
    scal[4] = rx[HALO:]
    scal[5] = rv[HALO:]
    scal[6] = xv[HALO:]
    scal[7] = gate[HALO:]
    rms_now[...] = gate

    def mix(chunk, total):
        cols = columns(chunk)
        hidden = x_win[:, cols].astype(f32) + wide(rms_now[...]) * v_win[:, cols]
        hid[0, :, cols] = hidden
        return total + fold(hidden * hidden)

    total = lax.fori_loop(0, chunks, mix, zero)

    def hidden_copy(layer):
        return pltpu.make_async_copy(
            hid.at[layer, pl.ds(HALO, keep)], hid_out.at[layer], sems.at[0, layer]
        )

    def slope_copy(layer):
        return pltpu.make_async_copy(der.at[layer], der_out.at[layer], sems.at[1, layer])

    def layer_step(layer, total):
        hidden_copy(layer).start()
        rms = lax.rsqrt(row_total(total) / width + EPS)
        scal[layer] = rms[HALO:]
        rms_now[...] = rms

        def one(chunk, total):
            cols = columns(chunk)
            hidden = hid[layer, :, cols]
            unit = hidden * wide(rms_now[...])
            mixed = taps[layer, 0:1, cols] * unit
            for k in range(1, 4):
                mixed = mixed + taps[layer, k : k + 1, cols] * pltpu.roll(unit, k, 0)
            bend = jnp.tanh(mixed)
            rise = 1.0 + bend
            silu = mixed * rise
            der[layer, :, cols] = (rise + silu * (1.0 - bend))[HALO:]
            after = hidden + silu
            hid[layer + 1, :, cols] = after
            return total + fold(after * after)

        total = lax.fori_loop(0, chunks, one, zero)
        slope_copy(layer).start()
        return total

    lax.fori_loop(0, live, layer_step, total)
    out = pltpu.make_async_copy(scal, scal_out, sems.at[0, 4])
    out.start()

    def finish(layer, carry):
        hidden_copy(layer).wait()
        slope_copy(layer).wait()
        return carry

    lax.fori_loop(0, live, finish, 0)
    out.wait()


def forward_map(batch, live, x, x_before, x_after, v, v_before, v_after, taps, order):
    length, width = x.shape[1:]
    keep = length + HALO
    rows = keep + HALO
    layers = taps.shape[0]
    hbm = pl.BlockSpec(memory_space=pltpu.HBM)
    return pl.pallas_call(
        functools.partial(forward_kernel, batch),
        out_shape=(
            jax.ShapeDtypeStruct((layers, keep, width), f32),
            jax.ShapeDtypeStruct((layers, keep, width), f32),
            jax.ShapeDtypeStruct((8, keep, LANES), f32),
        ),
        in_specs=[pl.BlockSpec(memory_space=pltpu.SMEM)]
        + [hbm] * 6
        + [pl.BlockSpec(memory_space=pltpu.VMEM), pl.BlockSpec(memory_space=pltpu.SMEM)],
        out_specs=[hbm] * 3,
        scratch_shapes=[
            pltpu.VMEM((rows, width), bf16),
            pltpu.VMEM((rows, width), f32),
            pltpu.VMEM((layers + 1, rows, width), f32),
            pltpu.VMEM((layers, keep, width), f32),
            pltpu.VMEM((8, keep, LANES), f32),
            pltpu.VMEM((rows, LANES), f32),
            pltpu.SemaphoreType.DMA((8, layers + 1)),
        ],
        compiler_params=pltpu.CompilerParams(vmem_limit_bytes=VMEM_LIMIT),
        cost_estimate=pl.CostEstimate(
            flops=30 * layers * rows * width,
            bytes_accessed=16 * MIB,
            transcendentals=layers * rows * width,
        ),
        name="forward_map",
    )(live, x_before, x, x_after, v_before, v, v_after, taps, order)


def backward_kernel(
    held, info, near, near_halo, top, top_halo, x_all, xa_all, v_all, va_all, taps, *refs,
):
    saved = [refs[3 * i : 3 * i + 3] for i in range(held[1])]
    refs = refs[3 * held[1] :]
    if held[2]:
        refs = refs[2:]
    (
        grad_send, halo_send, grads_all, gv_all, order_out,
        hid, der, scal, v_in, g, u, coef, x_in, g_in, ga_in, gx, gv, sems,
    ) = refs
    which = info[0]
    active = info[1]
    is_top = info[2]
    live = info[3]
    length, width = grad_send.shape
    rows = g.shape[0]
    chunks = width // STEP
    quarter = width // SPLIT
    first, count = held[0], held[1]
    order_out[0] = 0

    def part(q):
        return pl.ds(pl.multiple_of(q * quarter, quarter), quarter)

    def scal_copy(i):
        return pltpu.make_async_copy(saved[i][2], scal, sems.at[2, 0])

    def layer_copies(i, layer, q):
        cols = part(q)
        return (
            pltpu.make_async_copy(
                saved[i][1].at[layer, :, cols], der.at[layer, :, cols], sems.at[1, 4 * layer + q]
            ),
            pltpu.make_async_copy(
                saved[i][0].at[layer, :, cols], hid.at[layer, :, cols], sems.at[0, 4 * layer + q]
            ),
        )

    def input_copies():
        return (
            pltpu.make_async_copy(x_all.at[which], x_in, sems.at[2, 1]),
            pltpu.make_async_copy(v_all.at[which], v_in, sems.at[2, 3]),
        )

    def grad_copies(source, source_halo):
        return (
            pltpu.make_async_copy(source, g_in, sems.at[3, 0]),
            pltpu.make_async_copy(source_halo, ga_in, sems.at[3, 1]),
        )

    @pl.when(active == 1)
    def _():
        @pl.when(is_top == 1)
        def _():
            for copy in grad_copies(top.at[which], top_halo.at[which]):
                copy.start()

        @pl.when(is_top == 0)
        def _():
            for copy in grad_copies(near, near_halo):
                copy.start()

        for i in range(count):
            @pl.when(which == first + i)
            def _():
                def begin(step, carry):
                    layer = live - 1 - step
                    for q in range(SPLIT):
                        for copy in layer_copies(i, layer, q):
                            copy.start()
                    return carry

                begin(0, 0)
                scal_copy(i).start()
                lax.fori_loop(1, live, begin, 0)

        for copy in input_copies():
            copy.start()

        for copy in grad_copies(near, near_halo):
            copy.wait()

        def into_taps(layer, cols, grad):
            size = grad.shape[0]
            slope = grad * der[layer, 0:size, cols]
            out = taps[layer, 0:1, cols] * slope
            for k in range(1, 4):
                out = out + taps[layer, k : k + 1, cols] * pltpu.roll(slope, size - k, 0)
            u[0:size, cols] = out
            return fold(out * hid[layer, 0:size, cols])

        last = live - 1
        total = jnp.zeros((rows, LANES), f32)
        for q in range(SPLIT):
            for copy in layer_copies(0, last, q):
                copy.wait()

            def start(chunk, total):
                cols = columns(chunk)
                g[0:length, cols] = g_in[:, cols].astype(f32)
                g[length:rows, cols] = ga_in[:, cols].astype(f32)
                return total + into_taps(last, cols, g[:, cols])

            total = lax.fori_loop(q * chunks // SPLIT, (q + 1) * chunks // SPLIT, start, total)
        scal_copy(0).wait()

        def coefficients(layer, total):
            size = total.shape[0]
            rms = scal[layer, 0:size]
            coef[0, 0:size] = rms
            coef[1, 0:size] = -rms * rms * rms * (row_total(total) / width)

        def through_rms(layer, cols, size):
            return g[0:size, cols] + (
                wide(coef[0, 0:size]) * u[0:size, cols]
                + wide(coef[1, 0:size]) * hid[layer, 0:size, cols]
            )

        def layer_step(size, step, total):
            layer = live - 1 - step
            coefficients(layer, total)
            for q in range(SPLIT):
                for copy in layer_copies(0, layer - 1, q):
                    copy.wait()

            def one(chunk, total):
                cols = columns(chunk)
                grad = through_rms(layer, cols, size)
                g[0:size, cols] = grad
                return total + into_taps(layer - 1, cols, grad)

            return lax.fori_loop(0, chunks, one, jnp.zeros((size, LANES), f32))

        total = lax.fori_loop(
            0, jnp.minimum(live - 1, 1), functools.partial(layer_step, rows), total
        )
        fewer = rows - HALO // 2
        total = lax.fori_loop(
            1, live - 1, functools.partial(layer_step, fewer), total[0:fewer]
        )
        coefficients(0, total[0:length])
        for copy in input_copies():
            copy.wait()

        def to_gate(chunk, total):
            cols = columns(chunk)
            grad = through_rms(0, cols, length)
            g[0:length, cols] = grad
            return total + fold(grad * v_in[:, cols])

        total = row_total(lax.fori_loop(0, chunks, to_gate, jnp.zeros((length, LANES), f32)))
        rx, rv, xv, gate = (scal[i, 0:length] for i in range(4, 8))
        both = total * gate * (1.0 - gate) * (1.0 / math.sqrt(width)) * rx * rv
        mean = xv / width
        coef[0, 0:length] = both
        coef[1, 0:length] = -both * rx * rx * mean
        coef[2, 0:length] = -both * rv * rv * mean
        coef[3, 0:length] = gate

        def finish(chunk, carry):
            cols = columns(chunk)
            grad = g[0:length, cols]
            x = x_in[:, cols].astype(f32)
            v = v_in[:, cols]
            cross = wide(coef[0, 0:length])
            grad_x = grad + cross * v + wide(coef[1, 0:length]) * x
            grad_v = wide(coef[3, 0:length]) * grad + cross * x + wide(coef[2, 0:length]) * v
            gx[:, cols] = grad_x.astype(bf16)
            gv[:, cols] = grad_v.astype(bf16)
            return carry

        outs = []
        for q in range(SPLIT):
            lax.fori_loop(q * chunks // SPLIT, (q + 1) * chunks // SPLIT, finish, 0)
            cols = part(q)
            for i, (source, target) in enumerate((
                (gx.at[:, cols], grad_send.at[:, cols]),
                (gx.at[pl.ds(0, HALO), cols], halo_send.at[:, cols]),
                (gx.at[:, cols], grads_all.at[which, :, cols]),
                (gv.at[:, cols], gv_all.at[which, :, cols]),
            )):
                outs.append(pltpu.make_async_copy(source, target, sems.at[4, 4 * i + q]))
                outs[-1].start()
        for copy in outs:
            copy.wait()


def backward_map(info, near, near_halo, top, top_halo, x, x_after, v, v_after, taps, first, saved, previous):
    batches, length, width = x.shape
    rows = length + HALO
    layers = taps.shape[0]
    flat = [array for group in saved for array in group]
    some = pl.BlockSpec(memory_space=pl.ANY)
    hbm = pl.BlockSpec(memory_space=pltpu.HBM)
    extra = () if previous is None else previous
    operands = (info, near, near_halo, top, top_halo, x, x_after, v, v_after, taps, *flat, *extra)
    aliases = {} if previous is None else {len(operands) - 2: 2, len(operands) - 1: 3}
    return pl.pallas_call(
        functools.partial(backward_kernel, (first, len(saved), previous is not None)),
        out_shape=(
            jax.ShapeDtypeStruct((length, width), bf16),
            jax.ShapeDtypeStruct((HALO, width), bf16),
            jax.ShapeDtypeStruct((batches, length, width), bf16),
            jax.ShapeDtypeStruct((batches, length, width), bf16),
            jax.ShapeDtypeStruct((1,), jnp.int32),
        ),
        in_specs=[pl.BlockSpec(memory_space=pltpu.SMEM)]
        + [some] * 2
        + [hbm] * 6
        + [pl.BlockSpec(memory_space=pltpu.VMEM)]
        + [hbm] * (len(flat) + len(extra)),
        out_specs=[some] * 2
        + [hbm] * 2
        + [pl.BlockSpec(memory_space=pltpu.SMEM)],
        scratch_shapes=[
            pltpu.VMEM((layers, rows, width), f32),
            pltpu.VMEM((layers, rows, width), f32),
            pltpu.VMEM((8, rows, LANES), f32),
            pltpu.VMEM((length, width), f32),
            pltpu.VMEM((rows, width), f32),
            pltpu.VMEM((rows, width), f32),
            pltpu.VMEM((4, rows, LANES), f32),
            pltpu.VMEM((length, width), bf16),
            pltpu.VMEM((length, width), bf16),
            pltpu.VMEM((HALO, width), bf16),
            pltpu.VMEM((length, width), bf16),
            pltpu.VMEM((length, width), bf16),
            pltpu.SemaphoreType.DMA((5, 16)),
        ],
        input_output_aliases=aliases,
        compiler_params=pltpu.CompilerParams(vmem_limit_bytes=VMEM_LIMIT),
        cost_estimate=pl.CostEstimate(flops=25 * layers * rows * width, bytes_accessed=14 * MIB, transcendentals=0),
        name="backward_map",
    )(*operands)


def pack_kernel(dest, gv_all, order, *refs):
    out, stacked = refs[-2:]
    heads, width = 8, out.shape[-1]
    length = gv_all.shape[1]
    for head in range(heads):
        stacked[head * length : (head + 1) * length, :] = gv_all[0, :, head * width : (head + 1) * width]
    slot = lax.broadcasted_iota(jnp.int32, (out.shape[0], heads * length), 0)
    place = jnp.where(slot == dest[...], 1.0, 0.0).astype(bf16)
    out[...] = jnp.dot(place, stacked[...], preferred_element_type=f32).astype(bf16)


def pack_values(batch, dest, gv_all, slots, order, into, at, total):
    batches, length, model = gv_all.shape
    feature = model // 8
    operands = [dest, gv_all, order] + ([] if into is None else [into])
    specs = [
        pl.BlockSpec(dest.shape, lambda i: (0, 0)),
        pl.BlockSpec((1, length, model), lambda i: (batch, 0, 0)),
        pl.BlockSpec(memory_space=pltpu.SMEM),
    ] + ([] if into is None else [pl.BlockSpec(memory_space=pltpu.HBM)])
    return pl.pallas_call(
        pack_kernel,
        out_shape=jax.ShapeDtypeStruct((slots, total * feature), bf16),
        grid=(1,),
        in_specs=specs,
        out_specs=pl.BlockSpec((slots, feature), lambda i: (0, at)),
        scratch_shapes=[pltpu.VMEM((8 * length, feature), bf16)],
        input_output_aliases={} if into is None else {3: 0},
        compiler_params=pltpu.CompilerParams(vmem_limit_bytes=VMEM_LIMIT),
        cost_estimate=pl.CostEstimate(
            flops=2 * slots * 8 * length * feature, bytes_accessed=2 * MIB, transcendentals=0
        ),
        name="pack_values",
    )(*operands)


def owner_kernel(first, count, has_table, got, place_of, row_of, groups, order, weight, *refs):
    if has_table:
        table_in, refs = refs[0], refs[1:]
    table, sorted_in, joined, rows, place = refs
    heads, row_width, feature = weight.shape
    table_rows = table.shape[0]
    slots = got.shape[0]
    room = rows.shape[1] - 128
    step = 128
    half = room // 2
    for m in range(count):
        b = first + m

        def sort(tile, carry):
            at = pl.multiple_of(tile * half, half)
            slot = lax.broadcasted_iota(jnp.int32, (half, slots), 0) + at
            pick = jnp.where(slot == place_of[b : b + 1, :], 1.0, 0.0).astype(bf16)
            sorted_in[m, pl.ds(at, half), :] = jnp.dot(
                pick, got[:, m * feature : (m + 1) * feature], preferred_element_type=f32
            ).astype(bf16)
            return carry

        lax.fori_loop(0, 2, sort, 0)

        def mark(tile, carry):
            at = pl.multiple_of(tile * step, step)
            row = lax.broadcasted_iota(jnp.int32, (step, room), 0) + at
            place[pl.ds(at, step), m * room : (m + 1) * room] = jnp.where(
                row == row_of[b : b + 1, :], 1.0, 0.0
            ).astype(bf16)
            return carry

        lax.fori_loop(0, table_rows // step, mark, 0)
        rows[m, 0:room, :] = jnp.zeros((room, row_width), bf16)

    def head_step(h, carry):
        most = groups[first, heads + h]
        for m in range(1, count):
            most = jnp.maximum(most, groups[first + m, heads + h])

        def multiply(tile, carry):
            ats = []
            for m in range(count):
                at = jnp.where(
                    tile < groups[first + m, heads + h], groups[first + m, h] + tile * step, room
                )
                ats.append(pl.ds(pl.multiple_of(at, 16), step))
                joined[m * step : (m + 1) * step, :] = sorted_in[m, ats[m], :]
            out = lax.dot_general(
                joined[...], weight[h], (((1,), (1,)), ((), ())), preferred_element_type=f32
            ).astype(bf16)
            for m in range(count):
                rows[m, ats[m], :] = out[m * step : (m + 1) * step]
            return carry

        return lax.fori_loop(0, most, multiply, carry)

    lax.fori_loop(0, heads, head_step, 0)
    tile = 512
    for block in range(row_width // tile):
        cols = pl.ds(block * tile, tile)
        part = None
        for m in range(count):
            more = jnp.dot(
                place[:, m * room : (m + 1) * room], rows[m, 0:room, cols], preferred_element_type=f32
            )
            part = more if part is None else part + more
        if has_table:
            part = part + table_in[:, cols]
        table[:, cols] = part


def owner_add(first, count, table, got, place_of, row_of, groups, weight, order):
    heads, row_width, feature = weight.shape
    slots = got.shape[0]
    room = row_of.shape[1]
    vmem = pl.BlockSpec(memory_space=pltpu.VMEM)
    smem = pl.BlockSpec(memory_space=pltpu.SMEM)
    operands = [got, place_of, row_of, groups, order, weight]
    specs = [vmem, vmem, vmem, smem, smem, vmem]
    if table is not None:
        operands.append(table)
        specs.append(vmem)
    return pl.pallas_call(
        functools.partial(owner_kernel, first, count, table is not None),
        out_shape=jax.ShapeDtypeStruct((TABLE_DEV, row_width), f32),
        in_specs=specs,
        out_specs=vmem,
        scratch_shapes=[
            pltpu.VMEM((count, room + 128, feature), bf16),
            pltpu.VMEM((count * 128, feature), bf16),
            pltpu.VMEM((count, room + 128, row_width), bf16),
            pltpu.VMEM((TABLE_DEV, count * room), bf16),
        ],
        compiler_params=pltpu.CompilerParams(vmem_limit_bytes=44 * MIB),
        cost_estimate=pl.CostEstimate(
            flops=6 * count * slots * row_width * TABLE_DEV,
            bytes_accessed=18 * MIB,
            transcendentals=0,
        ),
        name="owner_add",
    )(*operands)


def slots_of(row_ids, owners, capacity):
    batches, length, heads = row_ids.shape
    ids = row_ids.transpose(0, 2, 1).reshape(batches, heads * length)
    owner = ids // TABLE_DEV
    local = ids - owner * TABLE_DEV
    head = jnp.arange(heads * length, dtype=jnp.int32) // length
    order = jnp.arange(heads * length, dtype=jnp.int32)
    ahead = (owner[:, None, :] == owner[:, :, None]) & (order[None, :] < order[:, None])
    rank = jnp.sum(ahead.astype(jnp.int32), -1)
    dest = owner * capacity + rank
    code = local * heads + head
    slot = jnp.arange(owners * capacity, dtype=jnp.int32)
    hit = dest[:, None, :] == slot[:, None]
    holds = jnp.sum(jnp.where(hit, code[:, None, :] + 1, 0), -1) - 1
    return dest, holds


def groups_of(holds, heads):
    batches, slots = holds.shape
    room = -(-(slots + 15 * heads) // 128) * 128
    valid = holds >= 0
    head = jnp.where(valid, holds % heads, -1)
    member = head[..., None] == jnp.arange(heads, dtype=jnp.int32)
    order = jnp.arange(slots, dtype=jnp.int32)
    below = (order[None, :] < order[:, None]).astype(bf16)
    rank = jnp.einsum("ij,bjh->bih", below, member.astype(bf16), preferred_element_type=f32)
    counts = jnp.sum(member.astype(jnp.int32), 1)
    padded = (counts + 15) // 16 * 16
    number = jnp.arange(heads, dtype=jnp.int32)
    starts = jnp.sum(jnp.where(number[None, :] < number[:, None], padded[:, None, :], 0), -1)
    place = jnp.sum(jnp.where(member, rank.astype(jnp.int32) + starts[:, None, :] + 1, 0), -1) - 1
    spot = jnp.arange(room, dtype=jnp.int32)
    hit = place[:, None, :] == spot[:, None]
    row = jnp.sum(jnp.where(hit, (holds // heads)[:, None, :] + 1, 0), -1) - 1
    groups = jnp.concatenate([starts, (counts + 127) // 128], 1)
    return place, row, groups


def shards(
    saved_inputs, memory, value_weight, conv_weight, norm_gain, layer_counts, row_ids, out_grad
):
    section = lax.axis_index("section")
    sections = lax.axis_size("section")
    owners = lax.axis_size("table")
    batches, length, width = out_grad.shape
    heads = memory.shape[3]
    capacity = 3 * length * heads // (2 * owners)
    slots = owners * capacity
    weight = value_weight[0]
    live = layer_counts[0]
    taps = 0.5 * conv_weight[0] * norm_gain[0][:, None, :]
    x = saved_inputs[0]
    is_top = section == sections - 1

    to_next = [(i, i + 1) for i in range(owners - 1)]
    to_last = [(i + 1, i) for i in range(owners - 1)]
    down = [(i + 1, i) for i in range(sections - 1)]
    down_halo = [
        ((i + 1) * owners + t + 1, i * owners + t)
        for i in range(sections - 1)
        for t in range(owners - 1)
    ]
    x_before = lax.ppermute(x[:, length - HALO :], "table", to_next)
    x_after = lax.ppermute(x[:, :HALO], "table", to_last)
    top_halo = lax.ppermute(out_grad[:, :HALO], "table", to_last)
    v = jnp.einsum("bthr,hrc->bthc", memory[0], weight, preferred_element_type=f32)
    v = v.reshape(batches, length, width)
    v_before = lax.ppermute(v[:, length - HALO :], "table", to_next)
    v_after = lax.ppermute(v[:, :HALO], "table", to_last)

    saved = []
    near = jnp.zeros((length, width), bf16)
    near_halo = jnp.zeros((HALO, width), bf16)
    outputs = table = dest = holds = place_of = row_of = groups = got = packed = None
    order = jnp.zeros((1,), jnp.int32)
    ticks = batches + sections - 1
    for tick in range(ticks):
        if tick < batches:
            saved.append(
                forward_map(
                    tick, live.reshape(1), x, x_before, x_after, v, v_before, v_after, taps, order
                )
            )
        position = tick - (sections - 1 - section)
        which = jnp.clip(position, 0, batches - 1)
        active = (position >= 0) & (position < batches)
        info = jnp.stack([which, active, is_top, live]).astype(jnp.int32)
        first = max(0, tick - (sections - 1))
        grad_send, halo_send, *outputs, order = backward_map(
            info, near, near_halo, out_grad, top_halo, x, x_after, v, v_after, taps,
            first, saved[first : tick + 1], outputs,
        )
        if tick < ticks - 1:
            near = lax.ppermute(grad_send, "section", down)
            near_halo = lax.ppermute(halo_send, ("section", "table"), down_halo)
        if tick == 0:
            dest, holds = slots_of(row_ids[0] + order, owners, capacity)
            holds = holds.reshape(batches, owners, capacity).transpose(1, 0, 2)
            holds = holds.reshape(owners, batches * capacity)
        if tick == sections - 1:
            holds = lax.all_to_all(holds + order, "table", 0, 0, tiled=True)
            holds = holds.reshape(owners, batches, capacity).transpose(1, 0, 2)
            holds = holds.reshape(batches, slots)
        if tick == sections:
            place_of, row_of, groups = groups_of(holds + order, heads)
        batch = tick - (sections - 1)
        if 0 <= batch < batches - 1:
            packed = pack_values(
                batch, dest[batch][None, :], outputs[1], slots, order, packed, batch, batches - 1
            )
        if batch == batches - 2:
            got = lax.all_to_all(packed, "table", 0, 0, tiled=True)
    last = batches - 1
    packed = pack_values(last, dest[last][None, :], outputs[1], slots, order, None, 0, 1)
    rest = lax.all_to_all(packed, "table", 0, 0, tiled=True)
    table = owner_add(0, last, None, got, place_of, row_of, groups, weight, order)
    table = owner_add(last, 1, table, rest, place_of, row_of, groups, weight, order)
    return (outputs[0][None], table[None])


def solution(mesh):
    placed = (
        P("section", None, "table", None),
        P("section", None, "table", None, None),
        P("section", None, None, None),
        P("section", None, None, None),
        P("section", None, None),
        P("section"),
        P("section", None, "table", None),
        P(None, "table", None),
    )
    return jax.shard_map(
        shards,
        mesh=mesh,
        in_specs=placed,
        out_specs=(P("section", None, "table", None), P("section", "table", None)),
        check_vma=False,
    )
```

time: 380 us -> 294 us (0.77)
  Pallas kernels: 145 us -> 105 us
  blocking collectives: 22.3 us -> 0 us
  waiting for transfers between devices: 103 us -> 85.5 us
  starting transfers between devices: 67.1 us -> 63.1 us
    ppermute x6, waiting for transfers between devices: 58.4 us -> 1.74 us  [shards(): near = lax.ppermute(grad_send, 'section', down)]
    ppermute x6, waiting for transfers between devices: 34.7 us -> 73.6 us  [shards(): near_halo = lax.ppermute(halo_send, ('section', 'table'), down_halo)]
    all_to_all x1 -> x0, blocking collectives: 22.3 us -> none  [shards(): got = lax.all_to_all(packed, 'table', 0, 0, tiled=True)]
    pallas_call x8 -> x6, Pallas kernels: 63.6 us -> 46.6 us  [the longest x2 34 us: owner_add(): pl.pallas_call(functools.partial(owner_kernel, first, count, table is not...]
    pallas_call x4, Pallas kernels: 38.6 us -> 26.3 us  [forward_map(): pl.pallas_call(functools.partial(forward_kernel, batch), out_shape=(jax.S...]
    pallas_call x7, Pallas kernels: 43.3 us -> 32 us  [backward_map(): pl.pallas_call(functools.partial(backward_kernel, (first, len(saved), pre...]
    all_to_all x3 -> x1, starting transfers between devices: 22.2 us -> 13.4 us  [shards(): got = lax.all_to_all(packed, 'table', 0, 0, tiled=True)]
    ppermute x1, waiting for transfers between devices: 6.9 us -> 0.01 us  [shards(): v_before = lax.ppermute(v[:, length - HALO:], 'table', to_next)]
  transfers between devices with their start and end apart: 21 -> 20, of which waited for: 8 -> 9; matrix products, arithmetic and copies ran while one was open for 7% -> 5% of each run, Pallas kernels for 24% -> 24%
where the time goes in v3:
time: 294 us; the launch traced here: 293 us
  Pallas kernels  105 us (36%)
  waiting for transfers between devices  85.5 us (29%)
  starting transfers between devices  63.1 us (21%)
  local copies, waits for them, and re-layouts  24.4 us (8%)
  other arithmetic  10.9 us (4%)
    ppermute x6, waiting for transfers between devices, shards(): near_halo = lax.ppermute(halo_send, ('section', 'table'), down_halo)  73.6 us
    pallas_call x2, Pallas kernels, owner_add(): pl.pallas_call(functools.partial(owner_kernel, first, count, table is not...  34 us
    pallas_call x7, Pallas kernels, backward_map(): pl.pallas_call(functools.partial(backward_kernel, (first, len(saved), pre...  32 us
    pallas_call x4, Pallas kernels, forward_map(): pl.pallas_call(functools.partial(forward_kernel, batch), out_shape=(jax.S...  26.3 us
    all_to_all x1, starting transfers between devices, shards(): holds = lax.all_to_all(holds + order, 'table', 0, 0, tiled=True)  14.2 us
    all_to_all x1, starting transfers between devices, shards(): got = lax.all_to_all(packed, 'table', 0, 0, tiled=True)  13.4 us
    pallas_call x4, Pallas kernels, pack_values(): pl.pallas_call(pack_kernel, out_shape=jax.ShapeDtypeStruct((slots, total...  12.6 us
    unnamed x52, local copies, waits for them, and re-layouts  12.4 us
  transfers between devices with their start and end apart: 20, of which 9 were waited for; matrix products, arithmetic and copies ran while one was open for 5% of the time, Pallas kernels for 24%

profile of v3, /device:TPU:1, one launch (start us, length us, event | category | flops | bytes accessed | tf_op | source)
XLA Modules:
  0.0 293.4 jit_solution(3213420794375846159)
XLA Ops:
  0.6 4.7 %copy.35 = bf16[4,64,8,1024]{3,1,0,2:T(8,128)(2,1)S(1)} copy(bf16[4,64,8,1024]{3,2,1,0:T(8,128)(2,1)} %bitcast.102) | data formatting | bytes 8388608 | tf_op jit(solution)/shard_map/squeeze | solution.py:621
  5.3 2.3 fusion.36
  8.1 2.1 copy-done.2
  10.2 1.5 fusion.38
  11.7 3.3 %collective-permute-start.2 = (f32[4,16,4096]{2,1,0:T(8,128)}, f32[4,16,4096]{2,1,0:T(8,128)S(1)}, u32[]{:S(2)}, u32[]{:S(2)}) collective-permute-start(f32[4,16,4096]{2,1,0:T(8,128)} %get-tuple-element.95), channel_id=1, source_target_pairs={{1,0},{2,1},{3,2},{4,3},{5,4},{6,5},{7,6},{8,7},{9,8},{10,9},{11,1... | collective-permute-start | bytes 3145736 | tf_op jit(solution)/shard_map/ppermute | solution.py:624
  16.1 1.9 collective-permute-start.1
  18.0 3.6 %collective-permute-start.4 = (f32[4,16,4096]{2,1,0:T(8,128)}, f32[4,16,4096]{2,1,0:T(8,128)}, u32[]{:S(2)}, u32[]{:S(2)}) collective-permute-start(f32[4,16,4096]{2,1,0:T(8,128)} %get-tuple-element.94), channel_id=1, source_target_pairs={{0,1},{1,2},{2,3},{3,4},{4,5},{5,6},{6,7},{7,8},{8,9},{9,10},{10,1... | collective-permute-start | bytes 3145736 | tf_op jit(solution)/shard_map/ppermute | solution.py:623
  21.7 1.9 collective-permute-start.3
  24.7 2.4 collective-permute-start
  29.2 5.4 %collective-permute-done.1.xa.xa_all = bf16[4,16,4096]{2,1,0:T(8,128)(2,1)S(1)} collective-permute-done((bf16[4,16,4096]{2,1,0:T(8,128)(2,1)}, bf16[4,16,4096]{2,1,0:T(8,128)(2,1)S(1)}, u32[]{:S(2)}, u32[]{:S(2)}) %collective-permute-start.1) | collective-permute-done | bytes 524320 | tf_op jit(solution)/shard_map/ppermute | solution.py:619
  34.6 4.7 %collective-permute-done.3.xb = bf16[4,16,4096]{2,1,0:T(8,128)(2,1)S(1)} collective-permute-done((bf16[4,16,4096]{2,1,0:T(8,128)(2,1)}, bf16[4,16,4096]{2,1,0:T(8,128)(2,1)S(1)}, u32[]{:S(2)}, u32[]{:S(2)}) %collective-permute-start.3) | collective-permute-done | bytes 524320 | tf_op jit(solution)/shard_map/ppermute | solution.py:618
  40.5 6.1 %forward_map.4 = (f32[4,80,4096]{2,1,0:T(8,128)}, f32[4,80,4096]{2,1,0:T(8,128)}, f32[8,80,128]{2,1,0:T(8,128)}) custom-call(s32[1]{0:T(128)S(6)} %copy.55.live_ref, bf16[4,16,4096]{2,1,0:T(8,128)(2,1)} %copy-done.8, bf16[4,64,4096]{2,1,0:T(8,128)(2,1)} %bitcast.84, bf16[4,16,4096]{2,1,0:T(8,128)(2,1)} %copy-done.5, ...), custom_call_target="tpu_custom_call" | custom-call | flops 47185920 | bytes 16777216 | tf_op jit(solution)/shard_map/forward_map/pallas_call | solution.py:149
  48.2 2.2 backward_map.7
  50.4 1.3 collective-permute-start.5
  51.7 1.3 collective-permute-start.6
  53.7 6.7 %forward_map.5 = (f32[4,80,4096]{2,1,0:T(8,128)}, f32[4,80,4096]{2,1,0:T(8,128)}, f32[8,80,128]{2,1,0:T(8,128)}) custom-call(s32[1]{0:T(128)S(6)} %copy.55.live_ref, bf16[4,16,4096]{2,1,0:T(8,128)(2,1)} %copy-done.8, bf16[4,64,4096]{2,1,0:T(8,128)(2,1)} %bitcast.86, bf16[4,16,4096]{2,1,0:T(8,128)(2,1)} %copy-done.5, ...), custom_call_target="tpu_custom_call" | custom-call | flops 47185920 | bytes 16777216 | tf_op jit(solution)/shard_map/forward_map/pallas_call | solution.py:149
  60.4 3.6 %collective-permute-done.6.near_halo = bf16[16,4096]{1,0:T(8,128)(2,1)S(1)} collective-permute-done((bf16[16,4096]{1,0:T(8,128)(2,1)}, bf16[16,4096]{1,0:T(8,128)(2,1)S(1)}, u32[]{:S(2)}, u32[]{:S(2)}) %collective-permute-start.6) | collective-permute-done | bytes 131104 | tf_op jit(solution)/shard_map/ppermute | solution.py:650
  66.0 2.2 backward_map.8
  68.2 1.3 collective-permute-start.7
  72.7 6.8 %forward_map.6 = (f32[4,80,4096]{2,1,0:T(8,128)}, f32[4,80,4096]{2,1,0:T(8,128)}, f32[8,80,128]{2,1,0:T(8,128)}) custom-call(s32[1]{0:T(128)S(6)} %copy.55.live_ref, bf16[4,16,4096]{2,1,0:T(8,128)(2,1)} %copy-done.8, bf16[4,64,4096]{2,1,0:T(8,128)(2,1)} %bitcast.88, bf16[4,16,4096]{2,1,0:T(8,128)(2,1)} %copy-done.5, ...), custom_call_target="tpu_custom_call" | custom-call | flops 47185920 | bytes 16777216 | tf_op jit(solution)/shard_map/forward_map/pallas_call | solution.py:149
  79.5 8.4 %collective-permute-done.8.near_halo = bf16[16,4096]{1,0:T(8,128)(2,1)S(1)} collective-permute-done((bf16[16,4096]{1,0:T(8,128)(2,1)}, bf16[16,4096]{1,0:T(8,128)(2,1)S(1)}, u32[]{:S(2)}, u32[]{:S(2)}) %collective-permute-start.8) | collective-permute-done | bytes 131104 | tf_op jit(solution)/shard_map/ppermute | solution.py:650
  88.7 2.4 backward_map.9
  91.1 1.3 collective-permute-start.9
  95.1 6.7 %forward_map.7 = (f32[4,80,4096]{2,1,0:T(8,128)}, f32[4,80,4096]{2,1,0:T(8,128)}, f32[8,80,128]{2,1,0:T(8,128)}) custom-call(s32[1]{0:T(128)S(6)} %copy.55.live_ref, bf16[4,16,4096]{2,1,0:T(8,128)(2,1)} %copy-done.8, bf16[4,64,4096]{2,1,0:T(8,128)(2,1)} %bitcast.90, bf16[4,16,4096]{2,1,0:T(8,128)(2,1)} %copy-done.5, ...), custom_call_target="tpu_custom_call" | custom-call | flops 47185920 | bytes 16777216 | tf_op jit(solution)/shard_map/forward_map/pallas_call | solution.py:149
  101.8 21.3 %collective-permute-done.10.near_halo = bf16[16,4096]{1,0:T(8,128)(2,1)S(1)} collective-permute-done((bf16[16,4096]{1,0:T(8,128)(2,1)}, bf16[16,4096]{1,0:T(8,128)(2,1)S(1)}, u32[]{:S(2)}, u32[]{:S(2)}) %collective-permute-start.10) | collective-permute-done | bytes 131104 | tf_op jit(solution)/shard_map/ppermute | solution.py:650
  124.5 6.3 %backward_map.10 = (bf16[64,4096]{1,0:T(8,128)(2,1)}, bf16[16,4096]{1,0:T(8,128)(2,1)}, bf16[4,64,4096]{2,1,0:T(8,128)(2,1)}, bf16[4,64,4096]{2,1,0:T(8,128)(2,1)}, s32[1]{0:T(128)}) custom-call(s32[4]{0:T(128)} %add_add_fusion.5.info, bf16[64,4096]{1,0:T(8,128)(2,1)} %copy-done.12, ...), custom_call_target="tpu_custom_call", output_to_operand_aliasing={{2}: (22, {}), {3}: (23, {})} | custom-call | flops 32768000 | bytes 14680064 | tf_op jit(solution)/shard_map/backward_map/pallas_call | solution.py:377
  130.8 1.3 collective-permute-start.11
  133.3 1.3 collective-permute-start.12
  135.2 3.2 %pack_values.5.refs_0_ = bf16[768,1536]{1,0:T(8,128)(2,1)} custom-call(s32[1,512]{1,0:T(1,128)} %get-tuple-element.100.dest, bf16[4,64,4096]{2,1,0:T(8,128)(2,1)} %get-tuple-element.77.refs_10_.gv_all, s32[1]{0:T(128)} %get-tuple-element.89.order), custom_call_target="tpu_custom_call" | custom-call | flops 402653184 | bytes 2097152 | tf_op jit(solution)/shard_map/pack_values/pallas_call | solution.py:436
  138.4 12.2 %collective-permute-done.12.near_halo = bf16[16,4096]{1,0:T(8,128)(2,1)S(1)} collective-permute-done((bf16[16,4096]{1,0:T(8,128)(2,1)}, bf16[16,4096]{1,0:T(8,128)(2,1)S(1)}, u32[]{:S(2)}, u32[]{:S(2)}) %collective-permute-start.12) | collective-permute-done | bytes 131104 | tf_op jit(solution)/shard_map/ppermute | solution.py:650
  151.5 6.3 %backward_map.11 = (bf16[64,4096]{1,0:T(8,128)(2,1)}, bf16[16,4096]{1,0:T(8,128)(2,1)}, bf16[4,64,4096]{2,1,0:T(8,128)(2,1)}, bf16[4,64,4096]{2,1,0:T(8,128)(2,1)}, s32[1]{0:T(128)}) custom-call(s32[4]{0:T(128)} %add_add_fusion.4.info, bf16[64,4096]{1,0:T(8,128)(2,1)} %copy-done.13, ...), custom_call_target="tpu_custom_call", output_to_operand_aliasing={{2}: (19, {}), {3}: (20, {})} | custom-call | flops 32768000 | bytes 14680064 | tf_op jit(solution)/shard_map/backward_map/pallas_call | solution.py:377
  157.8 1.3 collective-permute-start.13
  162.7 14.2 %all-to-all-start.1 = ((s32[32,1,96]{2,1,0:T(1,128)}), s32[32,1,96]{2,1,0:T(1,128)S(1)}, u32[]{:S(2)}, u32[]{:S(2)}) async-start(s32[32,1,96]{2,1,0:T(1,128)} %bitcast.32), calls=%async_computation.1 | async-start | bytes 32768 | tf_op jit(solution)/shard_map/all_to_all | solution.py:656
  176.9 3.1 %pack_values.6.refs_0_ = bf16[768,1536]{1,0:T(8,128)(2,1)} custom-call(s32[1,512]{1,0:T(1,128)} %get-tuple-element.101.dest, bf16[4,64,4096]{2,1,0:T(8,128)(2,1)} %get-tuple-element.81.refs_7_.gv_all, s32[1]{0:T(128)} %get-tuple-element.90.order, bf16[768,1536]{1,0:T(8,128)(2,1)} %pack_values.5.refs_0_), custom_call_target="tpu_custom_call", output_to_operand_aliasing={{}: (3, {})} | custom-call | flops 402653184 | bytes 2097152 | tf_op jit(solution)/shard_map/pack_values/pallas_call | solution.py:436
  180.8 6.3 %backward_map.12 = (bf16[64,4096]{1,0:T(8,128)(2,1)}, bf16[16,4096]{1,0:T(8,128)(2,1)}, bf16[4,64,4096]{2,1,0:T(8,128)(2,1)}, bf16[4,64,4096]{2,1,0:T(8,128)(2,1)}, s32[1]{0:T(128)}) custom-call(s32[4]{0:T(128)} %add_add_fusion.3.info, bf16[64,4096]{1,0:T(8,128)(2,1)} %copy-done.11, ...), custom_call_target="tpu_custom_call", output_to_operand_aliasing={{2}: (16, {}), {3}: (17, {})} | custom-call | flops 32768000 | bytes 14680064 | tf_op jit(solution)/shard_map/backward_map/pallas_call | solution.py:377
  187.2 3.2 %pack_values.7 = bf16[768,1536]{1,0:T(8,128)(2,1)} custom-call(s32[1,512]{1,0:T(1,128)} %get-tuple-element.102.dest, bf16[4,64,4096]{2,1,0:T(8,128)(2,1)} %get-tuple-element.85.refs_4_.gv_all, s32[1]{0:T(128)} %get-tuple-element.91.order, bf16[768,1536]{1,0:T(8,128)(2,1)} %pack_values.6.refs_0_), custom_call_target="tpu_custom_call", output_to_operand_aliasing={{}: (3, {})} | custom-call | flops 402653184 | bytes 2097152 | tf_op jit(solution)/shard_map/pack_values/pallas_call | solution.py:436
  190.3 13.4 %all-to-all-start.2 = ((bf16[32,24,1536]{2,1,0:T(8,128)(2,1)}), bf16[32,24,1536]{2,1,0:T(8,128)(2,1)S(1)}, u32[]{:S(2)}, u32[]{:S(2)}) async-start(bf16[32,24,1536]{2,1,0:T(8,128)(2,1)} %bitcast.97), calls=%async_computation.2 | async-start | bytes 4718592 | tf_op jit(solution)/shard_map/all_to_all | solution.py:667
  205.9 1.5 collective-permute-start.15
  207.5 1.4 select_reduce_fusion
  208.9 1.3 collective-permute-start.16
  210.3 28.1 %collective-permute-done.16.near_halo = bf16[16,4096]{1,0:T(8,128)(2,1)S(1)} collective-permute-done((bf16[16,4096]{1,0:T(8,128)(2,1)S(1)}, bf16[16,4096]{1,0:T(8,128)(2,1)S(1)}, u32[]{:S(2)}, u32[]{:S(2)}) %collective-permute-start.16) | collective-permute-done | bytes 131104 | tf_op jit(solution)/shard_map/ppermute | solution.py:650
  239.2 6.3 %backward_map.13 = (bf16[64,4096]{1,0:T(8,128)(2,1)}, bf16[16,4096]{1,0:T(8,128)(2,1)}, bf16[4,64,4096]{2,1,0:T(8,128)(2,1)}, bf16[4,64,4096]{2,1,0:T(8,128)(2,1)}, s32[1]{0:T(128)}) custom-call(s32[4]{0:T(128)} %add_add_fusion.2.info, bf16[64,4096]{1,0:T(8,128)(2,1)} %copy-done.14, ...), custom_call_target="tpu_custom_call", output_to_operand_aliasing={{2}: (13, {}), {3}: (14, {})} | custom-call | flops 32768000 | bytes 14680064 | tf_op jit(solution)/shard_map/backward_map/pallas_call | solution.py:377
  245.5 3.1 %pack_values.4 = bf16[768,512]{1,0:T(8,128)(2,1)} custom-call(s32[1,512]{1,0:T(1,128)} %get-tuple-element.103.dest, bf16[4,64,4096]{2,1,0:T(8,128)(2,1)} %get-tuple-element.87.gv_all, s32[1]{0:T(128)} %get-tuple-element.88.order), custom_call_target="tpu_custom_call" | custom-call | flops 402653184 | bytes 2097152 | tf_op jit(solution)/shard_map/pack_values/pallas_call | solution.py:436
  248.6 6.6 %all-to-all-start = ((bf16[32,24,512]{2,1,0:T(8,128)(2,1)}), bf16[32,24,512]{2,1,0:T(8,128)(2,1)S(1)}, u32[]{:S(2)}, u32[]{:S(2)}) async-start(bf16[32,24,512]{2,1,0:T(8,128)(2,1)} %bitcast.103), calls=%async_computation | async-start | bytes 1572864 | tf_op jit(solution)/shard_map/all_to_all | solution.py:670
  255.2 20.2 %owner_add.2.refs_0_ = f32[1024,1024]{1,0:T(8,128)S(1)} custom-call(bf16[768,1536]{1,0:T(8,128)(2,1)S(1)} %bitcast.70, s32[4,768]{1,0:T(4,128)S(1)} %broadcast_add_fusion.1.place_of, s32[4,896]{1,0:T(4,128)S(1)} %broadcast_add_fusion.row_of, s32[4,16]{1,0:T(4,128)S(1)} %pad_add_fusion.groups, s32[1]{0:T(128)} %get-tuple-element.88.order, ...), custom_call_target="tpu_custom_call" | custom-call | flops 14495514624 | bytes 18874368 | tf_op jit(solution)/shard_map/owner_add/pallas_call | solution.py:535
  275.5 2.0 copy-done
  277.5 2.2 copy-done.1
  279.7 13.8 %owner_add.3 = f32[1024,1024]{1,0:T(8,128)} custom-call(bf16[768,512]{1,0:T(8,128)(2,1)S(1)} %bitcast.71, s32[4,768]{1,0:T(4,128)S(1)} %broadcast_add_fusion.1.place_of, s32[4,896]{1,0:T(4,128)S(1)} %broadcast_add_fusion.row_of, s32[4,16]{1,0:T(4,128)S(1)} %pad_add_fusion.groups, s32[1]{0:T(128)} %get-tuple-element.88.order, ...), custom_call_target="tpu_custom_call" | custom-call | flops 4831838208 | bytes 18874368 | tf_op jit(solution)/shard_map/owner_add/pallas_call | solution.py:535
  (105 shorter events, 27.5 us)
Async XLA Ops:
  0.6 4.7 %copy-start.7 = (bf16[1,8,1024,512]{3,2,1,0:T(8,128)(2,1)S(1)}, bf16[1,8,1024,512]{3,2,1,0:T(8,128)(2,1)}, u32[]{:S(2)}) copy-start(bf16[1,8,1024,512]{3,2,1,0:T(8,128)(2,1)} %param.10) | copy-start | bytes 25165828
  8.1 2.1 copy-start.2
  8.1 6.9 %copy-start.3 = (bf16[1,4,64,4096]{3,2,1,0:T(8,128)(2,1)S(1)}, bf16[1,4,64,4096]{3,2,1,0:T(8,128)(2,1)}, u32[]{:S(2)}) copy-start(bf16[1,4,64,4096]{3,2,1,0:T(8,128)(2,1)} %param.8) | copy-start | bytes 6291460
  8.1 19.0 %copy-start.22 = (f32[1,4,4096]{2,1,0:T(4,128)S(1)}, f32[1,4,4096]{2,1,0:T(4,128)}, u32[]{:S(2)}) copy-start(f32[1,4,4096]{2,1,0:T(4,128)} %param.12) | copy-start | bytes 196612
  8.1 20.3 %copy-start.15 = (f32[1,4,4,4096]{3,2,1,0:T(4,128)S(1)}, f32[1,4,4,4096]{3,2,1,0:T(4,128)}, u32[]{:S(2)}) copy-start(f32[1,4,4,4096]{3,2,1,0:T(4,128)} %param.11) | copy-start | bytes 786436
  11.7 27.6 %collective-permute-start.2 = (f32[4,16,4096]{2,1,0:T(8,128)}, f32[4,16,4096]{2,1,0:T(8,128)S(1)}, u32[]{:S(2)}, u32[]{:S(2)}) collective-permute-start(f32[4,16,4096]{2,1,0:T(8,128)} %get-tuple-element.95), channel_id=1, source_target_pairs={{1,0},{2,1},{3,2},{4,3},{5,4},{6,5},{7,6},{8,7},{9,8},{10,9},{11,1... | collective-permute-start | bytes 3145736 | tf_op jit(solution)/shard_map/ppermute | solution.py:624
  16.1 18.5 %collective-permute-start.1 = (bf16[4,16,4096]{2,1,0:T(8,128)(2,1)}, bf16[4,16,4096]{2,1,0:T(8,128)(2,1)S(1)}, u32[]{:S(2)}, u32[]{:S(2)}) collective-permute-start(bf16[4,16,4096]{2,1,0:T(8,128)(2,1)} %get-tuple-element.97), channel_id=1, source_target_pairs={{1,0},{2,1},{3,2},{4,3},{5,4},{6,5},{7,6},{8,7},{9,8},{10,9},{11,1... | collective-permute-start | bytes 1572872 | tf_op jit(solution)/shard_map/ppermute | solution.py:619
  18.0 21.3 %collective-permute-start.4 = (f32[4,16,4096]{2,1,0:T(8,128)}, f32[4,16,4096]{2,1,0:T(8,128)}, u32[]{:S(2)}, u32[]{:S(2)}) collective-permute-start(f32[4,16,4096]{2,1,0:T(8,128)} %get-tuple-element.94), channel_id=1, source_target_pairs={{0,1},{1,2},{2,3},{3,4},{4,5},{5,6},{6,7},{7,8},{8,9},{9,10},{10,1... | collective-permute-start | bytes 3145736 | tf_op jit(solution)/shard_map/ppermute | solution.py:623
  21.7 17.7 %collective-permute-start.3 = (bf16[4,16,4096]{2,1,0:T(8,128)(2,1)}, bf16[4,16,4096]{2,1,0:T(8,128)(2,1)S(1)}, u32[]{:S(2)}, u32[]{:S(2)}) collective-permute-start(bf16[4,16,4096]{2,1,0:T(8,128)(2,1)} %get-tuple-element.96), channel_id=1, source_target_pairs={{0,1},{1,2},{2,3},{3,4},{4,5},{5,6},{6,7},{7,8},{8,9},{9,10},{10,1... | collective-permute-start | bytes 1572872 | tf_op jit(solution)/shard_map/ppermute | solution.py:618
  24.7 21.9 %collective-permute-start = (bf16[4,16,4096]{2,1,0:T(8,128)(2,1)S(1)}, bf16[4,16,4096]{2,1,0:T(8,128)(2,1)S(1)}, u32[]{:S(2)}, u32[]{:S(2)}) collective-permute-start(bf16[4,16,4096]{2,1,0:T(8,128)(2,1)S(1)} %slice.27), channel_id=1, source_target_pairs={{1,0},{2,1},{3,2},{4,3},{5,4},{6,5},{7,6},{8,7},{9,8},{10,9},{11,1... | collective-permute-start | bytes 1572872 | tf_op jit(solution)/shard_map/ppermute | solution.py:620
  34.6 4.7 %copy-start.5 = (bf16[4,16,4096]{2,1,0:T(8,128)(2,1)}, bf16[4,16,4096]{2,1,0:T(8,128)(2,1)S(1)}, u32[]{:S(2)}) copy-start(bf16[4,16,4096]{2,1,0:T(8,128)(2,1)S(1)} %collective-permute-done.1.xa.xa_all) | copy-start | bytes 1572868
  39.3 0.8 copy-start.8
  39.3 1.1 copy-start.4
  46.6 1.6 copy-start.6
  50.4 14.7 %collective-permute-start.5 = (bf16[64,4096]{1,0:T(8,128)(2,1)}, bf16[64,4096]{1,0:T(8,128)(2,1)S(1)}, u32[]{:S(2)}, u32[]{:S(2)}) collective-permute-start(bf16[64,4096]{1,0:T(8,128)(2,1)} %get-tuple-element.50), channel_id=1, source_target_pairs={{32,0},{64,32},{96,64},{33,1},{65,33},{97,65},{34,2},{66,34},{98,6... | collective-permute-start | bytes 1572872 | tf_op jit(solution)/shard_map/ppermute | solution.py:649
  51.7 12.2 %collective-permute-start.6 = (bf16[16,4096]{1,0:T(8,128)(2,1)}, bf16[16,4096]{1,0:T(8,128)(2,1)S(1)}, u32[]{:S(2)}, u32[]{:S(2)}) collective-permute-start(bf16[16,4096]{1,0:T(8,128)(2,1)} %get-tuple-element.51), channel_id=1, source_target_pairs={{33,0},{34,1},{35,2},{36,3},{37,4},{38,5},{39,6},{40,7},{41,8},{42... | collective-permute-start | bytes 393224 | tf_op jit(solution)/shard_map/ppermute | solution.py:650
  63.9 1.2 copy-start.16
  65.1 0.8 copy-start.9
  68.2 19.7 %collective-permute-start.7 = (bf16[64,4096]{1,0:T(8,128)(2,1)}, bf16[64,4096]{1,0:T(8,128)(2,1)S(1)}, u32[]{:S(2)}, u32[]{:S(2)}) collective-permute-start(bf16[64,4096]{1,0:T(8,128)(2,1)} %get-tuple-element.58), channel_id=1, source_target_pairs={{32,0},{64,32},{96,64},{33,1},{65,33},{97,65},{34,2},{66,34},{98,6... | collective-permute-start | bytes 1572872 | tf_op jit(solution)/shard_map/ppermute | solution.py:649
  70.7 17.2 %collective-permute-start.8 = (bf16[16,4096]{1,0:T(8,128)(2,1)}, bf16[16,4096]{1,0:T(8,128)(2,1)S(1)}, u32[]{:S(2)}, u32[]{:S(2)}) collective-permute-start(bf16[16,4096]{1,0:T(8,128)(2,1)} %get-tuple-element.59), channel_id=1, source_target_pairs={{33,0},{34,1},{35,2},{36,3},{37,4},{38,5},{39,6},{40,7},{41,8},{42... | collective-permute-start | bytes 393224 | tf_op jit(solution)/shard_map/ppermute | solution.py:650
  87.9 0.7 copy-start.17
  87.9 0.8 copy-start.10
  88.7 4.4 %copy-start.23 = (s32[1,4,64,8]{2,3,1,0:T(8,128)S(1)}, s32[1,4,64,8]{2,3,1,0:T(8,128)}, u32[]{:S(2)}) copy-start(s32[1,4,64,8]{2,3,1,0:T(8,128)} %param.14) | copy-start | bytes 24580
  91.1 32.5 %collective-permute-start.9 = (bf16[64,4096]{1,0:T(8,128)(2,1)}, bf16[64,4096]{1,0:T(8,128)(2,1)S(1)}, u32[]{:S(2)}, u32[]{:S(2)}) collective-permute-start(bf16[64,4096]{1,0:T(8,128)(2,1)} %get-tuple-element.66), channel_id=1, source_target_pairs={{32,0},{64,32},{96,64},{33,1},{65,33},{97,65},{34,2},{66,34},{98,6... | collective-permute-start | bytes 1572872 | tf_op jit(solution)/shard_map/ppermute | solution.py:649
  93.8 29.4 %collective-permute-start.10 = (bf16[16,4096]{1,0:T(8,128)(2,1)}, bf16[16,4096]{1,0:T(8,128)(2,1)S(1)}, u32[]{:S(2)}, u32[]{:S(2)}) collective-permute-start(bf16[16,4096]{1,0:T(8,128)(2,1)} %get-tuple-element.67), channel_id=1, source_target_pairs={{33,0},{34,1},{35,2},{36,3},{37,4},{38,5},{39,6},{40,7},{41,8},{42... | collective-permute-start | bytes 393224 | tf_op jit(solution)/shard_map/ppermute | solution.py:650
  123.1 0.7 copy-start.19
  123.7 0.8 copy-start.12
  130.8 19.9 %collective-permute-start.11 = (bf16[64,4096]{1,0:T(8,128)(2,1)}, bf16[64,4096]{1,0:T(8,128)(2,1)S(1)}, u32[]{:S(2)}, u32[]{:S(2)}) collective-permute-start(bf16[64,4096]{1,0:T(8,128)(2,1)} %get-tuple-element.74), channel_id=1, source_target_pairs={{32,0},{64,32},{96,64},{33,1},{65,33},{97,65},{34,2},{66,34},{98,6... | collective-permute-start | bytes 1572872 | tf_op jit(solution)/shard_map/ppermute | solution.py:649
  133.3 17.3 %collective-permute-start.12 = (bf16[16,4096]{1,0:T(8,128)(2,1)}, bf16[16,4096]{1,0:T(8,128)(2,1)S(1)}, u32[]{:S(2)}, u32[]{:S(2)}) collective-permute-start(bf16[16,4096]{1,0:T(8,128)(2,1)} %get-tuple-element.75), channel_id=1, source_target_pairs={{33,0},{34,1},{35,2},{36,3},{37,4},{38,5},{39,6},{40,7},{41,8},{42... | collective-permute-start | bytes 393224 | tf_op jit(solution)/shard_map/ppermute | solution.py:650
  150.7 0.7 copy-start.21
  150.7 0.8 copy-start.13
  157.8 22.2 %collective-permute-start.13 = (bf16[64,4096]{1,0:T(8,128)(2,1)}, bf16[64,4096]{1,0:T(8,128)(2,1)S(1)}, u32[]{:S(2)}, u32[]{:S(2)}) collective-permute-start(bf16[64,4096]{1,0:T(8,128)(2,1)} %get-tuple-element.78), channel_id=1, source_target_pairs={{32,0},{64,32},{96,64},{33,1},{65,33},{97,65},{34,2},{66,34},{98,6... | collective-permute-start | bytes 1572872 | tf_op jit(solution)/shard_map/ppermute | solution.py:649
  159.9 20.1 %collective-permute-start.14 = (bf16[16,4096]{1,0:T(8,128)(2,1)}, bf16[16,4096]{1,0:T(8,128)(2,1)S(1)}, u32[]{:S(2)}, u32[]{:S(2)}) collective-permute-start(bf16[16,4096]{1,0:T(8,128)(2,1)} %get-tuple-element.79), channel_id=1, source_target_pairs={{33,0},{34,1},{35,2},{36,3},{37,4},{38,5},{39,6},{40,7},{41,8},{42... | collective-permute-start | bytes 393224 | tf_op jit(solution)/shard_map/ppermute | solution.py:650
  162.7 27.6 %all-to-all-start.1 = ((s32[32,1,96]{2,1,0:T(1,128)}), s32[32,1,96]{2,1,0:T(1,128)S(1)}, u32[]{:S(2)}, u32[]{:S(2)}) async-start(s32[32,1,96]{2,1,0:T(1,128)} %bitcast.32), calls=%async_computation.1 | async-start | bytes 32768 | tf_op jit(solution)/shard_map/all_to_all | solution.py:656
  180.0 0.7 copy-start.18
  180.0 0.8 copy-start.11
  190.3 15.6 %copy-start.24 = (bf16[64,4096]{1,0:T(8,128)(2,1)S(1)}, bf16[64,4096]{1,0:T(8,128)(2,1)}, u32[]{:S(2)}) copy-start(bf16[64,4096]{1,0:T(8,128)(2,1)} %get-tuple-element.82) | copy-start | bytes 1572868
  190.3 18.6 %copy-start.25 = (bf16[16,4096]{1,0:T(8,128)(2,1)S(1)}, bf16[16,4096]{1,0:T(8,128)(2,1)}, u32[]{:S(2)}) copy-start(bf16[16,4096]{1,0:T(8,128)(2,1)} %get-tuple-element.83) | copy-start | bytes 393220
  190.3 58.3 %all-to-all-start.2 = ((bf16[32,24,1536]{2,1,0:T(8,128)(2,1)}), bf16[32,24,1536]{2,1,0:T(8,128)(2,1)S(1)}, u32[]{:S(2)}, u32[]{:S(2)}) async-start(bf16[32,24,1536]{2,1,0:T(8,128)(2,1)} %bitcast.97), calls=%async_computation.2 | async-start | bytes 4718592 | tf_op jit(solution)/shard_map/all_to_all | solution.py:667
  205.9 32.4 %collective-permute-start.15 = (bf16[64,4096]{1,0:T(8,128)(2,1)S(1)}, bf16[64,4096]{1,0:T(8,128)(2,1)S(1)}, u32[]{:S(2)}, u32[]{:S(2)}) collective-permute-start(bf16[64,4096]{1,0:T(8,128)(2,1)S(1)} %copy-done.24), channel_id=1, source_target_pairs={{32,0},{64,32},{96,64},{33,1},{65,33},{97,65},{34,2},{66,34},{98,6... | collective-permute-start | bytes 1572872 | tf_op jit(solution)/shard_map/ppermute | solution.py:649
  208.9 29.4 %collective-permute-start.16 = (bf16[16,4096]{1,0:T(8,128)(2,1)S(1)}, bf16[16,4096]{1,0:T(8,128)(2,1)S(1)}, u32[]{:S(2)}, u32[]{:S(2)}) collective-permute-start(bf16[16,4096]{1,0:T(8,128)(2,1)S(1)} %copy-done.25), channel_id=1, source_target_pairs={{33,0},{34,1},{35,2},{36,3},{37,4},{38,5},{39,6},{40,7},{41,8},{42... | collective-permute-start | bytes 393224 | tf_op jit(solution)/shard_map/ppermute | solution.py:650
  238.4 0.6 copy-start.20
  238.4 0.8 copy-start.14
  248.6 28.8 %all-to-all-start = ((bf16[32,24,512]{2,1,0:T(8,128)(2,1)}), bf16[32,24,512]{2,1,0:T(8,128)(2,1)S(1)}, u32[]{:S(2)}, u32[]{:S(2)}) async-start(bf16[32,24,512]{2,1,0:T(8,128)(2,1)} %bitcast.103), calls=%async_computation | async-start | bytes 1572864 | tf_op jit(solution)/shard_map/all_to_all | solution.py:670
  275.4 2.0 copy-start
  277.5 2.2 copy-start.1

commit v4 on v3

--- a/solution.py
+++ b/solution.py
@@ -37,8 +37,84 @@
     return sum(chunk[:, i : i + LANES] for i in range(0, STEP, LANES))
 
 
+def values_kernel(memory, weight, v_out, low_one, high_one, low_rest, high_rest, held, wide_held, flat, v, sems):
+    batches, rows = held.shape[:2]
+    heads, _, feature = weight.shape
+    length = rows // heads
+    loads = [pltpu.make_async_copy(memory.at[b], held.at[b], sems.at[0, b]) for b in range(batches)]
+    copies = [pltpu.make_async_copy(weight.at[h], flat.at[h], sems.at[1, h]) for h in range(heads)]
+    for copy in loads + copies:
+        copy.start()
+    step = 64
+    for b in range(batches):
+        loads[b].wait()
+
+        def widen(tile, carry):
+            at = pl.multiple_of(tile * step, step)
+            block = held[b, pl.ds(at, step), :].astype(f32)
+            for c in range(block.shape[1] // LANES):
+                wide_held[c, pl.ds(b * rows + at, step), :] = block[:, c * LANES : (c + 1) * LANES]
+            return carry
+
+        lax.fori_loop(0, rows // step, widen, 0)
+    outs = []
+    for h in range(heads):
+        copies[h].wait()
+        taken = [
+            wide_held[c, pl.ds(h, batches * length, stride=heads), :].astype(bf16)
+            for c in range(wide_held.shape[0])
+        ]
+        cols = pl.ds(h * feature, feature)
+        v[:, cols] = jnp.dot(
+            jnp.concatenate(taken, 1), flat[h], preferred_element_type=f32
+        )
+        outs.append(pltpu.make_async_copy(v.at[:, cols], v_out.at[:, cols], sems.at[2, h]))
+        outs[-1].start()
+    for b in range(batches):
+        low = low_one.at[0] if b == 0 else low_rest.at[b - 1]
+        high = high_one.at[0] if b == 0 else high_rest.at[b - 1]
+        for i, (target, at) in enumerate(((low, 0), (high, length - HALO))):
+            outs.append(
+                pltpu.make_async_copy(v.at[pl.ds(b * length + at, HALO)], target, sems.at[3 + i, b])
+            )
+            outs[-1].start()
+    for copy in outs:
+        copy.wait()
+
+
+def all_values(memory, weight):
+    batches, length, heads, row_width = memory.shape
+    feature = weight.shape[2]
+    hbm = pl.BlockSpec(memory_space=pltpu.HBM)
+    one = jax.ShapeDtypeStruct((1, HALO, heads * feature), f32)
+    rest = jax.ShapeDtypeStruct((batches - 1, HALO, heads * feature), f32)
+    v, *halos = pl.pallas_call(
+        values_kernel,
+        out_shape=(
+            jax.ShapeDtypeStruct((batches * length, heads * feature), f32), one, one, rest, rest
+        ),
+        in_specs=[hbm] * 2,
+        out_specs=[hbm] * 5,
+        scratch_shapes=[
+            pltpu.VMEM((batches, length * heads, row_width), bf16),
+            pltpu.VMEM((row_width // LANES, batches * length * heads, LANES), f32),
+            pltpu.VMEM(weight.shape, bf16),
+            pltpu.VMEM((batches * length, heads * feature), f32),
+            pltpu.SemaphoreType.DMA((5, heads)),
+        ],
+        compiler_params=pltpu.CompilerParams(vmem_limit_bytes=VMEM_LIMIT),
+        cost_estimate=pl.CostEstimate(
+            flops=2 * batches * length * heads * row_width * feature,
+            bytes_accessed=18 * MIB,
+            transcendentals=0,
+        ),
+        name="all_values",
+    )(memory.reshape(batches, length * heads, row_width), weight)
+    return v.reshape(batches, length, heads * feature), halos
+
+
 def forward_kernel(
-    batch, live_ref, xb, xm, xa, vb, vm, va, taps, order, hid_out, der_out, scal_out,
+    batch, v_halo, live_ref, xb, xm, xa, vb, vm, va, taps, order, hid_out, der_out, scal_out,
     x_win, v_win, hid, der, scal, rms_now, sems,
 ):
     width = xm.shape[-1]
@@ -53,10 +129,11 @@
         cols = pl.ds(q * (width // SPLIT), width // SPLIT)
         loads.append([])
         for i, (x_part, v_part, at, size) in enumerate(parts):
-            for j, (part, window) in enumerate(((x_part, x_win), (v_part, v_win))):
+            here = batch if i == 1 else v_halo
+            for j, (part, window, b) in enumerate(((x_part, x_win, batch), (v_part, v_win, here))):
                 loads[q].append(
                     pltpu.make_async_copy(
-                        part.at[batch, :, cols],
+                        part.at[b, :, cols],
                         window.at[pl.ds(at, size), cols],
                         sems.at[2 + 3 * j + i, q],
                     )
@@ -140,14 +217,14 @@
     out.wait()
 
 
-def forward_map(batch, live, x, x_before, x_after, v, v_before, v_after, taps, order):
+def forward_map(batch, v_halo, live, x, x_before, x_after, v, v_before, v_after, taps, order):
     length, width = x.shape[1:]
     keep = length + HALO
     rows = keep + HALO
     layers = taps.shape[0]
     hbm = pl.BlockSpec(memory_space=pltpu.HBM)
     return pl.pallas_call(
-        functools.partial(forward_kernel, batch),
+        functools.partial(forward_kernel, batch, v_halo),
         out_shape=(
             jax.ShapeDtypeStruct((layers, keep, width), f32),
             jax.ShapeDtypeStruct((layers, keep, width), f32),
@@ -177,12 +254,16 @@
 
 
 def backward_kernel(
-    held, info, near, near_halo, top, top_halo, x_all, xa_all, v_all, va_all, taps, *refs,
+    held, info, near, near_halo, top, top_halo, x_all, v_all, taps, *refs,
 ):
     saved = [refs[3 * i : 3 * i + 3] for i in range(held[1])]
     refs = refs[3 * held[1] :]
     if held[2]:
-        refs = refs[2:]
+        gv_held, refs = refs[1], refs[2:]
+    if held[3]:
+        dest, refs = refs[0], refs[2:]
+        packed, stacked, slots_now = refs[5], refs[-2], refs[-1]
+        refs = refs[:5] + refs[6:-2]
     (
         grad_send, halo_send, grads_all, gv_all, order_out,
         hid, der, scal, v_in, g, u, coef, x_in, g_in, ga_in, gx, gv, sems,
@@ -227,6 +308,15 @@
             pltpu.make_async_copy(source_halo, ga_in, sems.at[3, 1]),
         )
 
+    def pack():
+        spread_heads(gv, stacked)
+        into_slots(dest, stacked, slots_now)
+        feature = slots_now.shape[1]
+        at = pl.ds(packed.shape[1] - feature, feature)
+        copy = pltpu.make_async_copy(slots_now, packed.at[:, at], sems.at[3, 3])
+        copy.start()
+        copy.wait()
+
     @pl.when(active == 1)
     def _():
         @pl.when(is_top == 1)
@@ -360,68 +450,100 @@
             )):
                 outs.append(pltpu.make_async_copy(source, target, sems.at[4, 4 * i + q]))
                 outs[-1].start()
+        if held[3]:
+            pack()
         for copy in outs:
             copy.wait()
 
-
-def backward_map(info, near, near_halo, top, top_halo, x, x_after, v, v_after, taps, first, saved, previous):
+    if held[3]:
+        @pl.when(active == 0)
+        def _():
+            copy = pltpu.make_async_copy(gv_held.at[held[3] - 1], gv, sems.at[3, 2])
+            copy.start()
+            copy.wait()
+            pack()
+
+
+def backward_map(info, near, near_halo, top, top_halo, x, v, taps, first, saved, previous, packing=None):
     batches, length, width = x.shape
     rows = length + HALO
     layers = taps.shape[0]
     flat = [array for group in saved for array in group]
     some = pl.BlockSpec(memory_space=pl.ANY)
     hbm = pl.BlockSpec(memory_space=pltpu.HBM)
-    extra = () if previous is None else previous
-    operands = (info, near, near_halo, top, top_halo, x, x_after, v, v_after, taps, *flat, *extra)
-    aliases = {} if previous is None else {len(operands) - 2: 2, len(operands) - 1: 3}
+    vmem = pl.BlockSpec(memory_space=pltpu.VMEM)
+    smem = pl.BlockSpec(memory_space=pltpu.SMEM)
+    operands = [info, near, near_halo, top, top_halo, x, v, taps, *flat]
+    specs = [smem] + [some] * 2 + [hbm] * 4 + [vmem] + [hbm] * len(flat)
+    shapes = [
+        jax.ShapeDtypeStruct((length, width), bf16),
+        jax.ShapeDtypeStruct((HALO, width), bf16),
+        jax.ShapeDtypeStruct((batches, length, width), bf16),
+        jax.ShapeDtypeStruct((batches, length, width), bf16),
+        jax.ShapeDtypeStruct((1,), jnp.int32),
+    ]
+    out_specs = [some] * 2 + [hbm] * 2 + [smem]
+    scratch = [
+        pltpu.VMEM((layers, rows, width), f32),
+        pltpu.VMEM((layers, rows, width), f32),
+        pltpu.VMEM((8, rows, LANES), f32),
+        pltpu.VMEM((length, width), f32),
+        pltpu.VMEM((rows, width), f32),
+        pltpu.VMEM((rows, width), f32),
+        pltpu.VMEM((4, rows, LANES), f32),
+        pltpu.VMEM((length, width), bf16),
+        pltpu.VMEM((length, width), bf16),
+        pltpu.VMEM((HALO, width), bf16),
+        pltpu.VMEM((length, width), bf16),
+        pltpu.VMEM((length, width), bf16),
+        pltpu.SemaphoreType.DMA((5, 16)),
+    ]
+    aliases = {}
+    if previous is not None:
+        aliases = {len(operands): 2, len(operands) + 1: 3}
+        operands += previous
+        specs += [hbm] * 2
+    if packing is not None:
+        batch, dest, packed = packing
+        aliases[len(operands) + 1] = 5
+        operands += [dest, packed]
+        specs += [vmem, hbm]
+        shapes.append(jax.ShapeDtypeStruct(packed.shape, packed.dtype))
+        out_specs.append(hbm)
+        feature = width // 8
+        scratch += [pltpu.VMEM((8 * length, feature), bf16), pltpu.VMEM((packed.shape[0], feature), bf16)]
+    pack_flag = 0 if packing is None else packing[0] + 1
     return pl.pallas_call(
-        functools.partial(backward_kernel, (first, len(saved), previous is not None)),
-        out_shape=(
-            jax.ShapeDtypeStruct((length, width), bf16),
-            jax.ShapeDtypeStruct((HALO, width), bf16),
-            jax.ShapeDtypeStruct((batches, length, width), bf16),
-            jax.ShapeDtypeStruct((batches, length, width), bf16),
-            jax.ShapeDtypeStruct((1,), jnp.int32),
-        ),
-        in_specs=[pl.BlockSpec(memory_space=pltpu.SMEM)]
-        + [some] * 2
-        + [hbm] * 6
-        + [pl.BlockSpec(memory_space=pltpu.VMEM)]
-        + [hbm] * (len(flat) + len(extra)),
-        out_specs=[some] * 2
-        + [hbm] * 2
-        + [pl.BlockSpec(memory_space=pltpu.SMEM)],
-        scratch_shapes=[
-            pltpu.VMEM((layers, rows, width), f32),
-            pltpu.VMEM((layers, rows, width), f32),
-            pltpu.VMEM((8, rows, LANES), f32),
-            pltpu.VMEM((length, width), f32),
-            pltpu.VMEM((rows, width), f32),
-            pltpu.VMEM((rows, width), f32),
-            pltpu.VMEM((4, rows, LANES), f32),
-            pltpu.VMEM((length, width), bf16),
-            pltpu.VMEM((length, width), bf16),
-            pltpu.VMEM((HALO, width), bf16),
-            pltpu.VMEM((length, width), bf16),
-            pltpu.VMEM((length, width), bf16),
-            pltpu.SemaphoreType.DMA((5, 16)),
-        ],
+        functools.partial(backward_kernel, (first, len(saved), previous is not None, pack_flag)),
+        out_shape=shapes,
+        in_specs=specs,
+        out_specs=out_specs,
+        scratch_shapes=scratch,
         input_output_aliases=aliases,
         compiler_params=pltpu.CompilerParams(vmem_limit_bytes=VMEM_LIMIT),
-        cost_estimate=pl.CostEstimate(flops=25 * layers * rows * width, bytes_accessed=14 * MIB, transcendentals=0),
+        cost_estimate=pl.CostEstimate(
+            flops=25 * layers * rows * width, bytes_accessed=14 * MIB, transcendentals=0
+        ),
         name="backward_map",
     )(*operands)
 
 
+def spread_heads(gv, stacked):
+    length, width = gv.shape[0], stacked.shape[1]
+    for head in range(stacked.shape[0] // length):
+        stacked[head * length : (head + 1) * length, :] = gv[:, head * width : (head + 1) * width]
+
+
+def into_slots(dest, stacked, out):
+    slot = lax.broadcasted_iota(jnp.int32, (out.shape[0], stacked.shape[0]), 0)
+    place = jnp.where(slot == dest[...], 1.0, 0.0).astype(bf16)
+    out[...] = jnp.dot(place, stacked[...], preferred_element_type=f32).astype(bf16)
+
+
 def pack_kernel(dest, gv_all, order, *refs):
     out, stacked = refs[-2:]
-    heads, width = 8, out.shape[-1]
-    length = gv_all.shape[1]
-    for head in range(heads):
-        stacked[head * length : (head + 1) * length, :] = gv_all[0, :, head * width : (head + 1) * width]
-    slot = lax.broadcasted_iota(jnp.int32, (out.shape[0], heads * length), 0)
-    place = jnp.where(slot == dest[...], 1.0, 0.0).astype(bf16)
-    out[...] = jnp.dot(place, stacked[...], preferred_element_type=f32).astype(bf16)
+    spread_heads(gv_all.at[0], stacked)
+    into_slots(dest, stacked, out)
 
 
 def pack_values(batch, dest, gv_all, slots, order, into, at, total):
@@ -449,12 +571,19 @@
     )(*operands)
 
 
-def owner_kernel(first, count, has_table, got, place_of, row_of, groups, order, weight, *refs):
+def owner_kernel(first, count, has_table, got, place_of, row_of, groups, order, weight_in, *refs):
     if has_table:
         table_in, refs = refs[0], refs[1:]
-    table, sorted_in, joined, rows, place = refs
+    table, sorted_in, joined, rows, place, weight, total, sems = refs
     heads, row_width, feature = weight.shape
     table_rows = table.shape[0]
+    copies = [
+        pltpu.make_async_copy(weight_in.at[h], weight.at[h], sems.at[h]) for h in range(heads)
+    ]
+    if has_table:
+        copies.append(pltpu.make_async_copy(table_in, total, sems.at[heads]))
+    for copy in copies:
+        copy.start()
     slots = got.shape[0]
     room = rows.shape[1] - 128
     step = 128
@@ -506,8 +635,13 @@
 
         return lax.fori_loop(0, most, multiply, carry)
 
-    lax.fori_loop(0, heads, head_step, 0)
-    tile = 512
+    for h in range(heads):
+        copies[h].wait()
+        head_step(h, 0)
+    if has_table:
+        copies[heads].wait()
+    tile = 256
+    outs = []
     for block in range(row_width // tile):
         cols = pl.ds(block * tile, tile)
         part = None
@@ -517,8 +651,16 @@
             )
             part = more if part is None else part + more
         if has_table:
-            part = part + table_in[:, cols]
-        table[:, cols] = part
+            part = part + total[:, cols]
+        total[:, cols] = part
+        outs.append(
+            pltpu.make_async_copy(
+                total.at[:, cols], table.at[:, cols], sems.at[heads + 1 + block]
+            )
+        )
+        outs[-1].start()
+    for copy in outs:
+        copy.wait()
 
 
 def owner_add(first, count, table, got, place_of, row_of, groups, weight, order):
@@ -528,22 +670,26 @@
     vmem = pl.BlockSpec(memory_space=pltpu.VMEM)
     smem = pl.BlockSpec(memory_space=pltpu.SMEM)
     operands = [got, place_of, row_of, groups, order, weight]
-    specs = [vmem, vmem, vmem, smem, smem, vmem]
+    hbm = pl.BlockSpec(memory_space=pltpu.HBM)
+    specs = [vmem, vmem, vmem, smem, smem, hbm]
     if table is not None:
         operands.append(table)
-        specs.append(vmem)
+        specs.append(hbm)
     return pl.pallas_call(
         functools.partial(owner_kernel, first, count, table is not None),
         out_shape=jax.ShapeDtypeStruct((TABLE_DEV, row_width), f32),
         in_specs=specs,
-        out_specs=vmem,
+        out_specs=hbm,
         scratch_shapes=[
             pltpu.VMEM((count, room + 128, feature), bf16),
             pltpu.VMEM((count * 128, feature), bf16),
             pltpu.VMEM((count, room + 128, row_width), bf16),
             pltpu.VMEM((TABLE_DEV, count * room), bf16),
+            pltpu.VMEM(weight.shape, bf16),
+            pltpu.VMEM((TABLE_DEV, row_width), f32),
+            pltpu.SemaphoreType.DMA((heads + 1 + row_width // 256,)),
         ],
-        compiler_params=pltpu.CompilerParams(vmem_limit_bytes=44 * MIB),
+        compiler_params=pltpu.CompilerParams(vmem_limit_bytes=VMEM_LIMIT),
         cost_estimate=pl.CostEstimate(
             flops=6 * count * slots * row_width * TABLE_DEV,
             bytes_accessed=18 * MIB,
@@ -617,23 +763,27 @@
     ]
     x_before = lax.ppermute(x[:, length - HALO :], "table", to_next)
     x_after = lax.ppermute(x[:, :HALO], "table", to_last)
+    v, (low_one, high_one, low_rest, high_rest) = all_values(memory[0], weight)
+    v_before = [lax.ppermute(high_one, "table", to_next)]
+    v_after = [lax.ppermute(low_one, "table", to_last)]
     top_halo = lax.ppermute(out_grad[:, :HALO], "table", to_last)
-    v = jnp.einsum("bthr,hrc->bthc", memory[0], weight, preferred_element_type=f32)
-    v = v.reshape(batches, length, width)
-    v_before = lax.ppermute(v[:, length - HALO :], "table", to_next)
-    v_after = lax.ppermute(v[:, :HALO], "table", to_last)
+    v_before.append(lax.ppermute(high_rest, "table", to_next))
+    v_after.append(lax.ppermute(low_rest, "table", to_last))
 
     saved = []
     near = jnp.zeros((length, width), bf16)
     near_halo = jnp.zeros((HALO, width), bf16)
-    outputs = table = dest = holds = place_of = row_of = groups = got = packed = None
+    outputs = table = dest = holds = place_of = row_of = groups = got = None
+    packed = [None, None]
     order = jnp.zeros((1,), jnp.int32)
     ticks = batches + sections - 1
     for tick in range(ticks):
         if tick < batches:
+            which_halo = min(tick, 1)
             saved.append(
                 forward_map(
-                    tick, live.reshape(1), x, x_before, x_after, v, v_before, v_after, taps, order
+                    tick, max(tick - 1, 0), live.reshape(1), x, x_before, x_after,
+                    v, v_before[which_halo], v_after[which_halo], taps, order,
                 )
             )
         position = tick - (sections - 1 - section)
@@ -641,10 +791,14 @@
         active = (position >= 0) & (position < batches)
         info = jnp.stack([which, active, is_top, live]).astype(jnp.int32)
         first = max(0, tick - (sections - 1))
-        grad_send, halo_send, *outputs, order = backward_map(
-            info, near, near_halo, out_grad, top_halo, x, x_after, v, v_after, taps,
-            first, saved[first : tick + 1], outputs,
+        packing = (batches - 1, dest[batches - 1][None, :], packed[1]) if tick == ticks - 1 else None
+        grad_send, halo_send, *outputs = backward_map(
+            info, near, near_halo, out_grad, top_halo, x, v, taps,
+            first, saved[first : tick + 1], outputs, packing,
         )
+        if packing is not None:
+            packed[1] = outputs.pop()
+        order = outputs.pop()
         if tick < ticks - 1:
             near = lax.ppermute(grad_send, "section", down)
             near_halo = lax.ppermute(halo_send, ("section", "table"), down_halo)
@@ -660,16 +814,15 @@
             place_of, row_of, groups = groups_of(holds + order, heads)
         batch = tick - (sections - 1)
         if 0 <= batch < batches - 1:
-            packed = pack_values(
-                batch, dest[batch][None, :], outputs[1], slots, order, packed, batch, batches - 1
+            pair, at = batch // 2, batch % 2
+            packed[pair] = pack_values(
+                batch, dest[batch][None, :], outputs[1], slots, order, packed[pair], at, 2
             )
-        if batch == batches - 2:
-            got = lax.all_to_all(packed, "table", 0, 0, tiled=True)
-    last = batches - 1
-    packed = pack_values(last, dest[last][None, :], outputs[1], slots, order, None, 0, 1)
-    rest = lax.all_to_all(packed, "table", 0, 0, tiled=True)
-    table = owner_add(0, last, None, got, place_of, row_of, groups, weight, order)
-    table = owner_add(last, 1, table, rest, place_of, row_of, groups, weight, order)
+        if batch == 2:
+            got = lax.all_to_all(packed[0], "table", 0, 0, tiled=True)
+    rest = lax.all_to_all(packed[1], "table", 0, 0, tiled=True)
+    table = owner_add(0, 2, None, got, place_of, row_of, groups, weight, order)
+    table = owner_add(2, 2, table, rest, place_of, row_of, groups, weight, order)
     return (outputs[0][None], table[None])
 
 

time: 294 us -> 296 us (level); the launches traced: 293 us -> 291 us
  waiting for transfers between devices: 85.5 us -> 72.9 us
  Pallas kernels: 105 us -> 117 us
  local copies, waits for them, and re-layouts: 24.4 us -> 16.4 us
  starting transfers between devices: 63.1 us -> 69.9 us
    ppermute x6, waiting for transfers between devices: 73.6 us -> 51.2 us  [shards(): near_halo = lax.ppermute(halo_send, ('section', 'table'), down_halo)]
    ppermute x6, waiting for transfers between devices: 1.74 us -> 16.6 us  [shards(): near = lax.ppermute(grad_send, 'section', down)]
    pallas_call x7, Pallas kernels: 32 us -> 42.8 us  [backward_map(): pl.pallas_call(functools.partial(backward_kernel, (first, len(saved), pre...]
    pallas_call x4 -> x5, Pallas kernels: 26.3 us -> 34.3 us  [the longest x4 26.2 us: forward_map(): pl.pallas_call(functools.partial(forward_kernel, batch, v_halo), out_shap...]
    ppermute x1, waiting for transfers between devices: 5.42 us -> 0.01 us  [shards(): x_after = lax.ppermute(x[:, :HALO], 'table', to_last)]
    all_to_all x2, waiting for transfers between devices: 0.01 us -> 4.98 us  [the longest x1 4.98 us: shards(): rest = lax.all_to_all(packed[1], 'table', 0, 0, tiled=True)]
    ppermute x1, waiting for transfers between devices: 4.72 us -> 0.01 us  [shards(): x_before = lax.ppermute(x[:, length - HALO:], 'table', to_next)]
    squeeze x1 -> x0, local copies, waits for them, and re-layouts: 4.66 us -> none  [shards(): memory[0]]
  transfers between devices with their start and end apart: 20 -> 22, of which waited for: 9 -> 9; matrix products, arithmetic and copies ran while one was open for 5% -> 6% of each run, Pallas kernels for 24% -> 31%
where the time goes in v4:
time: 296 us; the launch traced here: 291 us
  Pallas kernels  117 us (40%)
  waiting for transfers between devices  72.9 us (25%)
  starting transfers between devices  69.9 us (24%)
  local copies, waits for them, and re-layouts  16.4 us (6%)
  other arithmetic  12.6 us (4%)
    ppermute x6, waiting for transfers between devices, shards(): near_halo = lax.ppermute(halo_send, ('section', 'table'), down_halo)  51.2 us
    pallas_call x7, Pallas kernels, backward_map(): pl.pallas_call(functools.partial(backward_kernel, (first, len(saved), pre...  42.8 us
    pallas_call x2, Pallas kernels, owner_add(): pl.pallas_call(functools.partial(owner_kernel, first, count, table is not...  30.1 us
    pallas_call x4, Pallas kernels, forward_map(): pl.pallas_call(functools.partial(forward_kernel, batch, v_halo), out_shap...  26.2 us
    ppermute x6, waiting for transfers between devices, shards(): near = lax.ppermute(grad_send, 'section', down)  16.6 us
    all_to_all x1, starting transfers between devices, shards(): got = lax.all_to_all(packed[0], 'table', 0, 0, tiled=True)  12.5 us
    all_to_all x1, starting transfers between devices, shards(): holds = lax.all_to_all(holds + order, 'table', 0, 0, tiled=True)  12.4 us
    pallas_call x3, Pallas kernels, pack_values(): pl.pallas_call(pack_kernel, out_shape=jax.ShapeDtypeStruct((slots, total...  9.75 us
  transfers between devices with their start and end apart: 22, of which 9 were waited for; matrix products, arithmetic and copies ran while one was open for 6% of the time, Pallas kernels for 31%

profile of v4, /device:TPU:1, one launch (start us, length us, event | category | flops | bytes accessed | tf_op | source)
XLA Modules:
  0.0 291.2 jit_solution(10262206174165930316)
XLA Ops:
  0.6 2.3 fusion.36
  2.9 4.6 %collective-permute-start.1 = (bf16[4,16,4096]{2,1,0:T(8,128)(2,1)}, bf16[4,16,4096]{2,1,0:T(8,128)(2,1)S(1)}, u32[]{:S(2)}, u32[]{:S(2)}) collective-permute-start(bf16[4,16,4096]{2,1,0:T(8,128)(2,1)} %get-tuple-element.105), channel_id=1, source_target_pairs={{0,1},{1,2},{2,3},{3,4},{4,5},{5,6},{6,7},{7,8},{8,9},{9,10},{10,1... | collective-permute-start | bytes 1572872 | tf_op jit(solution)/shard_map/ppermute | solution.py:764
  7.5 1.9 collective-permute-start.2
  9.5 8.1 %all_values.1 = (f32[256,4096]{1,0:T(8,128)}, f32[1,16,4096]{2,1,0:T(8,128)}, f32[1,16,4096]{2,1,0:T(8,128)}, f32[3,16,4096]{2,1,0:T(8,128)}, f32[3,16,4096]{2,1,0:T(8,128)}) custom-call(bf16[4,512,1024]{2,1,0:T(8,128)(2,1)} %bitcast.89, bf16[8,1024,512]{2,1,0:T(8,128)(2,1)} %bitcast.86), custom_call_target="tpu_custom_call" | custom-call | flops 2147483648 | bytes 18874368 | tf_op jit(solution)/shard_map/all_values/pallas_call | solution.py:91
  17.6 3.7 %collective-permute-start.3 = (f32[1,16,4096]{2,1,0:T(8,128)}, f32[1,16,4096]{2,1,0:T(8,128)S(1)}, u32[]{:S(2)}, u32[]{:S(2)}) collective-permute-start(f32[1,16,4096]{2,1,0:T(8,128)} %get-tuple-element.53), channel_id=1, source_target_pairs={{0,1},{1,2},{2,3},{3,4},{4,5},{5,6},{6,7},{7,8},{8,9},{9,10},{10,1... | collective-permute-start | bytes 786440 | tf_op jit(solution)/shard_map/ppermute | solution.py:767
  21.2 1.9 collective-permute-start.4
  23.2 1.9 slice.21
  25.0 1.9 collective-permute-start
  27.0 3.6 %collective-permute-start.7 = (f32[3,16,4096]{2,1,0:T(8,128)}, f32[3,16,4096]{2,1,0:T(8,128)S(1)}, u32[]{:S(2)}, u32[]{:S(2)}) collective-permute-start(f32[3,16,4096]{2,1,0:T(8,128)} %get-tuple-element.60), channel_id=1, source_target_pairs={{0,1},{1,2},{2,3},{3,4},{4,5},{5,6},{6,7},{7,8},{8,9},{9,10},{10,1... | collective-permute-start | bytes 2359304 | tf_op jit(solution)/shard_map/ppermute | solution.py:770
  31.4 1.9 collective-permute-start.8
  36.5 6.1 %forward_map.4 = (f32[4,80,4096]{2,1,0:T(8,128)}, f32[4,80,4096]{2,1,0:T(8,128)}, f32[8,80,128]{2,1,0:T(8,128)}) custom-call(s32[1]{0:T(128)S(6)} %copy.46.live_ref, bf16[4,16,4096]{2,1,0:T(8,128)(2,1)} %copy-done.1, bf16[4,64,4096]{2,1,0:T(8,128)(2,1)} %bitcast.72, bf16[4,16,4096]{2,1,0:T(8,128)(2,1)} %copy-done.2, f32[1,16,4096]{2,1,0:T(8,128)} %copy-done.13, ...), custom_call_target="tpu_custom_call" | custom-call | flops 47185920 | bytes 16777216 | tf_op jit(solution)/shard_map/forward_map/pallas_call | solution.py:226
  44.2 2.2 backward_map.7
  46.4 1.3 collective-permute-start.5
  52.2 6.7 %forward_map.5 = (f32[4,80,4096]{2,1,0:T(8,128)}, f32[4,80,4096]{2,1,0:T(8,128)}, f32[8,80,128]{2,1,0:T(8,128)}) custom-call(s32[1]{0:T(128)S(6)} %copy.46.live_ref, bf16[4,16,4096]{2,1,0:T(8,128)(2,1)} %copy-done.1, bf16[4,64,4096]{2,1,0:T(8,128)(2,1)} %bitcast.74, bf16[4,16,4096]{2,1,0:T(8,128)(2,1)} %copy-done.2, f32[3,16,4096]{2,1,0:T(8,128)} %copy-done.3, ...), custom_call_target="tpu_custom_call" | custom-call | flops 47185920 | bytes 16777216 | tf_op jit(solution)/shard_map/forward_map/pallas_call | solution.py:226
  58.9 2.9 %collective-permute-done.6.near_halo = bf16[16,4096]{1,0:T(8,128)(2,1)S(1)} collective-permute-done((bf16[16,4096]{1,0:T(8,128)(2,1)}, bf16[16,4096]{1,0:T(8,128)(2,1)S(1)}, u32[]{:S(2)}, u32[]{:S(2)}) %collective-permute-start.6) | collective-permute-done | bytes 131104 | tf_op jit(solution)/shard_map/ppermute | solution.py:804
  61.8 4.6 %collective-permute-done.5.near = bf16[64,4096]{1,0:T(8,128)(2,1)S(1)} collective-permute-done((bf16[64,4096]{1,0:T(8,128)(2,1)}, bf16[64,4096]{1,0:T(8,128)(2,1)S(1)}, u32[]{:S(2)}, u32[]{:S(2)}) %collective-permute-start.5) | collective-permute-done | bytes 524320 | tf_op jit(solution)/shard_map/ppermute | solution.py:803
  67.2 2.2 backward_map.8
  69.4 1.3 collective-permute-start.9
  73.4 6.6 %forward_map.6 = (f32[4,80,4096]{2,1,0:T(8,128)}, f32[4,80,4096]{2,1,0:T(8,128)}, f32[8,80,128]{2,1,0:T(8,128)}) custom-call(s32[1]{0:T(128)S(6)} %copy.46.live_ref, bf16[4,16,4096]{2,1,0:T(8,128)(2,1)} %copy-done.1, bf16[4,64,4096]{2,1,0:T(8,128)(2,1)} %bitcast.76, bf16[4,16,4096]{2,1,0:T(8,128)(2,1)} %copy-done.2, f32[3,16,4096]{2,1,0:T(8,128)} %copy-done.3, ...), custom_call_target="tpu_custom_call" | custom-call | flops 47185920 | bytes 16777216 | tf_op jit(solution)/shard_map/forward_map/pallas_call | solution.py:226
  80.1 3.9 %collective-permute-done.10.near_halo = bf16[16,4096]{1,0:T(8,128)(2,1)S(1)} collective-permute-done((bf16[16,4096]{1,0:T(8,128)(2,1)}, bf16[16,4096]{1,0:T(8,128)(2,1)S(1)}, u32[]{:S(2)}, u32[]{:S(2)}) %collective-permute-start.10) | collective-permute-done | bytes 131104 | tf_op jit(solution)/shard_map/ppermute | solution.py:804
  84.0 5.4 %collective-permute-done.9.near = bf16[64,4096]{1,0:T(8,128)(2,1)S(1)} collective-permute-done((bf16[64,4096]{1,0:T(8,128)(2,1)}, bf16[64,4096]{1,0:T(8,128)(2,1)S(1)}, u32[]{:S(2)}, u32[]{:S(2)}) %collective-permute-start.9) | collective-permute-done | bytes 524320 | tf_op jit(solution)/shard_map/ppermute | solution.py:803
  90.2 2.2 backward_map.9
  92.4 1.5 collective-permute-start.11
  95.2 1.3 collective-permute-start.12
  97.1 6.7 %forward_map.7 = (f32[4,80,4096]{2,1,0:T(8,128)}, f32[4,80,4096]{2,1,0:T(8,128)}, f32[8,80,128]{2,1,0:T(8,128)}) custom-call(s32[1]{0:T(128)S(6)} %copy.46.live_ref, bf16[4,16,4096]{2,1,0:T(8,128)(2,1)} %copy-done.1, bf16[4,64,4096]{2,1,0:T(8,128)(2,1)} %bitcast.78, bf16[4,16,4096]{2,1,0:T(8,128)(2,1)} %copy-done.2, f32[3,16,4096]{2,1,0:T(8,128)} %copy-done.3, ...), custom_call_target="tpu_custom_call" | custom-call | flops 47185920 | bytes 16777216 | tf_op jit(solution)/shard_map/forward_map/pallas_call | solution.py:226
  103.9 17.4 %collective-permute-done.12.near_halo = bf16[16,4096]{1,0:T(8,128)(2,1)S(1)} collective-permute-done((bf16[16,4096]{1,0:T(8,128)(2,1)}, bf16[16,4096]{1,0:T(8,128)(2,1)S(1)}, u32[]{:S(2)}, u32[]{:S(2)}) %collective-permute-start.12) | collective-permute-done | bytes 131104 | tf_op jit(solution)/shard_map/ppermute | solution.py:804
  122.2 6.3 %backward_map.10 = (bf16[64,4096]{1,0:T(8,128)(2,1)}, bf16[16,4096]{1,0:T(8,128)(2,1)}, bf16[4,64,4096]{2,1,0:T(8,128)(2,1)}, bf16[4,64,4096]{2,1,0:T(8,128)(2,1)}, s32[1]{0:T(128)}) custom-call(s32[4]{0:T(128)} %add_add_fusion.5.info, bf16[64,4096]{1,0:T(8,128)(2,1)} %copy-done.8, ...), custom_call_target="tpu_custom_call", output_to_operand_aliasing={{2}: (20, {}), {3}: (21, {})} | custom-call | flops 32768000 | bytes 14680064 | tf_op jit(solution)/shard_map/backward_map/pallas_call | solution.py:516
  128.5 1.3 collective-permute-start.13
  130.6 1.3 collective-permute-start.14
  133.5 12.4 %all-to-all-start.1 = ((s32[32,1,96]{2,1,0:T(1,128)}), s32[32,1,96]{2,1,0:T(1,128)S(1)}, u32[]{:S(2)}, u32[]{:S(2)}) async-start(s32[32,1,96]{2,1,0:T(1,128)} %bitcast.29), calls=%async_computation.1 | async-start | bytes 32768 | tf_op jit(solution)/shard_map/all_to_all | solution.py:810
  145.9 3.3 %pack_values.4.refs_0_ = bf16[768,1024]{1,0:T(8,128)(2,1)} custom-call(s32[1,512]{1,0:T(1,128)} %get-tuple-element.108.dest, bf16[4,64,4096]{2,1,0:T(8,128)(2,1)} %get-tuple-element.87.refs_10_.gv_all, s32[1]{0:T(128)} %get-tuple-element.99.order), custom_call_target="tpu_custom_call" | custom-call | flops 402653184 | bytes 2097152 | tf_op jit(solution)/shard_map/pack_values/pallas_call | solution.py:558
  150.0 6.3 %backward_map.11 = (bf16[64,4096]{1,0:T(8,128)(2,1)}, bf16[16,4096]{1,0:T(8,128)(2,1)}, bf16[4,64,4096]{2,1,0:T(8,128)(2,1)}, bf16[4,64,4096]{2,1,0:T(8,128)(2,1)}, s32[1]{0:T(128)}) custom-call(s32[4]{0:T(128)} %add_add_fusion.4.info, bf16[64,4096]{1,0:T(8,128)(2,1)} %copy-done.9, ...), custom_call_target="tpu_custom_call", output_to_operand_aliasing={{2}: (17, {}), {3}: (18, {})} | custom-call | flops 32768000 | bytes 14680064 | tf_op jit(solution)/shard_map/backward_map/pallas_call | solution.py:516
  156.4 3.3 %pack_values.5 = bf16[768,1024]{1,0:T(8,128)(2,1)} custom-call(s32[1,512]{1,0:T(1,128)} %get-tuple-element.109.dest, bf16[4,64,4096]{2,1,0:T(8,128)(2,1)} %get-tuple-element.91.refs_7_.gv_all, s32[1]{0:T(128)} %get-tuple-element.100.order, bf16[768,1024]{1,0:T(8,128)(2,1)} %pack_values.4.refs_0_), custom_call_target="tpu_custom_call", output_to_operand_aliasing={{}: (3, {})} | custom-call | flops 402653184 | bytes 2097152 | tf_op jit(solution)/shard_map/pack_values/pallas_call | solution.py:558
  159.7 12.5 %all-to-all-start.2 = ((bf16[32,24,1024]{2,1,0:T(8,128)(2,1)}), bf16[32,24,1024]{2,1,0:T(8,128)(2,1)S(1)}, u32[]{:S(2)}, u32[]{:S(2)}) async-start(bf16[32,24,1024]{2,1,0:T(8,128)(2,1)} %bitcast.85), calls=%async_computation.2 | async-start | bytes 3145728 | tf_op jit(solution)/shard_map/all_to_all | solution.py:822
  175.7 1.3 collective-permute-start.16
  177.2 21.8 %collective-permute-done.16.near_halo = bf16[16,4096]{1,0:T(8,128)(2,1)S(1)} collective-permute-done((bf16[16,4096]{1,0:T(8,128)(2,1)S(1)}, bf16[16,4096]{1,0:T(8,128)(2,1)S(1)}, u32[]{:S(2)}, u32[]{:S(2)}) %collective-permute-start.16) | collective-permute-done | bytes 131104 | tf_op jit(solution)/shard_map/ppermute | solution.py:804
  199.8 6.3 %backward_map.12 = (bf16[64,4096]{1,0:T(8,128)(2,1)}, bf16[16,4096]{1,0:T(8,128)(2,1)}, bf16[4,64,4096]{2,1,0:T(8,128)(2,1)}, bf16[4,64,4096]{2,1,0:T(8,128)(2,1)}, s32[1]{0:T(128)}) custom-call(s32[4]{0:T(128)} %add_add_fusion.3.info, bf16[64,4096]{1,0:T(8,128)(2,1)} %copy-done.10, ...), custom_call_target="tpu_custom_call", output_to_operand_aliasing={{2}: (14, {}), {3}: (15, {})} | custom-call | flops 32768000 | bytes 14680064 | tf_op jit(solution)/shard_map/backward_map/pallas_call | solution.py:516
  206.1 1.3 collective-permute-start.17
  207.9 1.3 collective-permute-start.18
  209.3 3.2 %pack_values.3.refs_6_ = bf16[768,1024]{1,0:T(8,128)(2,1)} custom-call(s32[1,512]{1,0:T(1,128)} %get-tuple-element.110.dest, bf16[4,64,4096]{2,1,0:T(8,128)(2,1)} %get-tuple-element.95.gv_all.refs_4_, s32[1]{0:T(128)} %get-tuple-element.96.order), custom_call_target="tpu_custom_call" | custom-call | flops 402653184 | bytes 2097152 | tf_op jit(solution)/shard_map/pack_values/pallas_call | solution.py:558
  212.5 5.2 %collective-permute-done.18.near_halo = bf16[16,4096]{1,0:T(8,128)(2,1)S(1)} collective-permute-done((bf16[16,4096]{1,0:T(8,128)(2,1)}, bf16[16,4096]{1,0:T(8,128)(2,1)S(1)}, u32[]{:S(2)}, u32[]{:S(2)}) %collective-permute-start.18) | collective-permute-done | bytes 131104 | tf_op jit(solution)/shard_map/ppermute | solution.py:804
  217.6 6.6 %collective-permute-done.17.near = bf16[64,4096]{1,0:T(8,128)(2,1)S(1)} collective-permute-done((bf16[64,4096]{1,0:T(8,128)(2,1)}, bf16[64,4096]{1,0:T(8,128)(2,1)S(1)}, u32[]{:S(2)}, u32[]{:S(2)}) %collective-permute-start.17) | collective-permute-done | bytes 524320 | tf_op jit(solution)/shard_map/ppermute | solution.py:803
  225.1 17.2 %backward_map.13 = (bf16[64,4096]{1,0:T(8,128)(2,1)}, bf16[16,4096]{1,0:T(8,128)(2,1)}, bf16[4,64,4096]{2,1,0:T(8,128)(2,1)}, bf16[4,64,4096]{2,1,0:T(8,128)(2,1)}, s32[1]{0:T(128)}, /*index=5*/bf16[768,1024]{1,0:T(8,128)(2,1)}) custom-call(s32[4]{0:T(128)} %add_add_fusion.2.info, ...), custom_call_target="tpu_custom_call", output_to_operand_aliasing={{2}: (11, {}), {3}: (12, {}), {5}: (14, {})} | custom-call | flops 32768000 | bytes 14680064 | tf_op jit(solution)/shard_map/backward_map/pallas_call | solution.py:516
  242.3 9.7 %all-to-all-start = ((bf16[32,24,1024]{2,1,0:T(8,128)(2,1)}), bf16[32,24,1024]{2,1,0:T(8,128)(2,1)S(1)}, u32[]{:S(2)}, u32[]{:S(2)}) async-start(bf16[32,24,1024]{2,1,0:T(8,128)(2,1)} %bitcast.84), calls=%async_computation | async-start | bytes 3145728 | tf_op jit(solution)/shard_map/all_to_all | solution.py:823
  252.7 1.4 select_reduce_fusion
  254.7 15.0 %owner_add.2.refs_0_ = f32[1024,1024]{1,0:T(8,128)} custom-call(bf16[768,1024]{1,0:T(8,128)(2,1)} %bitcast.90, s32[4,768]{1,0:T(4,128)} %copy-done.23, s32[4,896]{1,0:T(4,128)} %broadcast_add_fusion.row_of, s32[4,16]{1,0:T(4,128)} %pad_add_fusion.groups, s32[1]{0:T(128)} %get-tuple-element.101.order, bf16[8,1024,512]{2,1,0:T(8,128)(2,1)} %bitcast.87), custom_call_target="tpu_custom_call" | custom-call | flops 9663676416 | bytes 18874368 | tf_op jit(solution)/shard_map/owner_add/pallas_call | solution.py:678
  269.7 5.0 %all-to-all-done = bf16[32,24,1024]{2,1,0:T(8,128)(2,1)S(1)} async-done(((bf16[32,24,1024]{2,1,0:T(8,128)(2,1)}), bf16[32,24,1024]{2,1,0:T(8,128)(2,1)S(1)}, u32[]{:S(2)}, u32[]{:S(2)}) %all-to-all-start) | async-done | bytes 1572896 | tf_op jit(solution)/shard_map/all_to_all | solution.py:823
  275.9 15.1 %owner_add.3 = f32[1024,1024]{1,0:T(8,128)} custom-call(bf16[768,1024]{1,0:T(8,128)(2,1)} %bitcast.91, s32[4,768]{1,0:T(4,128)} %copy-done.23, s32[4,896]{1,0:T(4,128)} %broadcast_add_fusion.row_of, s32[4,16]{1,0:T(4,128)} %pad_add_fusion.groups, s32[1]{0:T(128)} %get-tuple-element.101.order, bf16[8,1024,512]{2,1,0:T(8,128)(2,1)} %bitcast.88, ...), custom_call_target="tpu_custom_call" | custom-call | flops 9663676416 | bytes 18874368 | tf_op jit(solution)/shard_map/owner_add/pallas_call | solution.py:678
  (107 shorter events, 27.7 us)
Async XLA Ops:
  2.9 32.5 %collective-permute-start.1 = (bf16[4,16,4096]{2,1,0:T(8,128)(2,1)}, bf16[4,16,4096]{2,1,0:T(8,128)(2,1)S(1)}, u32[]{:S(2)}, u32[]{:S(2)}) collective-permute-start(bf16[4,16,4096]{2,1,0:T(8,128)(2,1)} %get-tuple-element.105), channel_id=1, source_target_pairs={{0,1},{1,2},{2,3},{3,4},{4,5},{5,6},{6,7},{7,8},{8,9},{9,10},{10,1... | collective-permute-start | bytes 1572872 | tf_op jit(solution)/shard_map/ppermute | solution.py:764
  7.5 27.9 %collective-permute-start.2 = (bf16[4,16,4096]{2,1,0:T(8,128)(2,1)}, bf16[4,16,4096]{2,1,0:T(8,128)(2,1)S(1)}, u32[]{:S(2)}, u32[]{:S(2)}) collective-permute-start(bf16[4,16,4096]{2,1,0:T(8,128)(2,1)} %get-tuple-element.104), channel_id=1, source_target_pairs={{1,0},{2,1},{3,2},{4,3},{5,4},{6,5},{7,6},{8,7},{9,8},{10,9},{11,1... | collective-permute-start | bytes 1572872 | tf_op jit(solution)/shard_map/ppermute | solution.py:765
  9.4 17.5 %copy-start.22 = (f32[1,4,4096]{2,1,0:T(4,128)S(1)}, f32[1,4,4096]{2,1,0:T(4,128)}, u32[]{:S(2)}) copy-start(f32[1,4,4096]{2,1,0:T(4,128)} %param.12) | copy-start | bytes 196612
  9.5 23.8 %copy-start.15 = (f32[1,4,4,4096]{3,2,1,0:T(4,128)S(1)}, f32[1,4,4,4096]{3,2,1,0:T(4,128)}, u32[]{:S(2)}) copy-start(f32[1,4,4,4096]{3,2,1,0:T(4,128)} %param.11) | copy-start | bytes 786436
  17.6 9.4 %collective-permute-start.3 = (f32[1,16,4096]{2,1,0:T(8,128)}, f32[1,16,4096]{2,1,0:T(8,128)S(1)}, u32[]{:S(2)}, u32[]{:S(2)}) collective-permute-start(f32[1,16,4096]{2,1,0:T(8,128)} %get-tuple-element.53), channel_id=1, source_target_pairs={{0,1},{1,2},{2,3},{3,4},{4,5},{5,6},{6,7},{7,8},{8,9},{9,10},{10,1... | collective-permute-start | bytes 786440 | tf_op jit(solution)/shard_map/ppermute | solution.py:767
  21.2 9.4 %collective-permute-start.4 = (f32[1,16,4096]{2,1,0:T(8,128)}, f32[1,16,4096]{2,1,0:T(8,128)S(1)}, u32[]{:S(2)}, u32[]{:S(2)}) collective-permute-start(f32[1,16,4096]{2,1,0:T(8,128)} %get-tuple-element.54), channel_id=1, source_target_pairs={{1,0},{2,1},{3,2},{4,3},{5,4},{6,5},{7,6},{8,7},{9,8},{10,9},{11,1... | collective-permute-start | bytes 786440 | tf_op jit(solution)/shard_map/ppermute | solution.py:768
  25.0 17.6 %collective-permute-start = (bf16[4,16,4096]{2,1,0:T(8,128)(2,1)}, bf16[4,16,4096]{2,1,0:T(8,128)(2,1)S(1)}, u32[]{:S(2)}, u32[]{:S(2)}) collective-permute-start(bf16[4,16,4096]{2,1,0:T(8,128)(2,1)} %slice.21), channel_id=1, source_target_pairs={{1,0},{2,1},{3,2},{4,3},{5,4},{6,5},{7,6},{8,7},{9,8},{10,9},{11,1... | collective-permute-start | bytes 1572872 | tf_op jit(solution)/shard_map/ppermute | solution.py:769
  27.0 8.4 %copy-start.13 = (f32[1,16,4096]{2,1,0:T(8,128)}, f32[1,16,4096]{2,1,0:T(8,128)S(1)}, u32[]{:S(2)}) copy-start(f32[1,16,4096]{2,1,0:T(8,128)S(1)} %collective-permute-done.3.vb) | copy-start | bytes 786436
  27.0 24.0 %collective-permute-start.7 = (f32[3,16,4096]{2,1,0:T(8,128)}, f32[3,16,4096]{2,1,0:T(8,128)S(1)}, u32[]{:S(2)}, u32[]{:S(2)}) collective-permute-start(f32[3,16,4096]{2,1,0:T(8,128)} %get-tuple-element.60), channel_id=1, source_target_pairs={{0,1},{1,2},{2,3},{3,4},{4,5},{5,6},{6,7},{7,8},{8,9},{9,10},{10,1... | collective-permute-start | bytes 2359304 | tf_op jit(solution)/shard_map/ppermute | solution.py:770
  30.7 0.7 copy-start.14
  31.4 19.6 %collective-permute-start.8 = (f32[3,16,4096]{2,1,0:T(8,128)}, f32[3,16,4096]{2,1,0:T(8,128)S(1)}, u32[]{:S(2)}, u32[]{:S(2)}) collective-permute-start(f32[3,16,4096]{2,1,0:T(8,128)} %get-tuple-element.61), channel_id=1, source_target_pairs={{1,0},{2,1},{3,2},{4,3},{5,4},{6,5},{7,6},{8,7},{9,8},{10,9},{11,1... | collective-permute-start | bytes 2359304 | tf_op jit(solution)/shard_map/ppermute | solution.py:771
  35.4 0.8 copy-start.1
  35.4 1.0 copy-start.2
  42.6 1.6 copy-start
  46.4 20.0 %collective-permute-start.5 = (bf16[64,4096]{1,0:T(8,128)(2,1)}, bf16[64,4096]{1,0:T(8,128)(2,1)S(1)}, u32[]{:S(2)}, u32[]{:S(2)}) collective-permute-start(bf16[64,4096]{1,0:T(8,128)(2,1)} %get-tuple-element.58), channel_id=1, source_target_pairs={{32,0},{64,32},{96,64},{33,1},{65,33},{97,65},{34,2},{66,34},{98,6... | collective-permute-start | bytes 1572872 | tf_op jit(solution)/shard_map/ppermute | solution.py:803
  49.0 12.8 %collective-permute-start.6 = (bf16[16,4096]{1,0:T(8,128)(2,1)}, bf16[16,4096]{1,0:T(8,128)(2,1)S(1)}, u32[]{:S(2)}, u32[]{:S(2)}) collective-permute-start(bf16[16,4096]{1,0:T(8,128)(2,1)} %get-tuple-element.59), channel_id=1, source_target_pairs={{33,0},{34,1},{35,2},{36,3},{37,4},{38,5},{39,6},{40,7},{41,8},{42... | collective-permute-start | bytes 393224 | tf_op jit(solution)/shard_map/ppermute | solution.py:804
  51.0 0.9 copy-start.3
  51.0 1.1 copy-start.4
  61.8 4.6 %copy-start.16 = (bf16[16,4096]{1,0:T(8,128)(2,1)}, bf16[16,4096]{1,0:T(8,128)(2,1)S(1)}, u32[]{:S(2)}) copy-start(bf16[16,4096]{1,0:T(8,128)(2,1)S(1)} %collective-permute-done.6.near_halo) | copy-start | bytes 393220
  66.4 0.8 copy-start.7
  67.2 4.2 %copy-start.24 = (s32[1,4,64,8]{2,3,1,0:T(8,128)S(1)}, s32[1,4,64,8]{2,3,1,0:T(8,128)}, u32[]{:S(2)}) copy-start(s32[1,4,64,8]{2,3,1,0:T(8,128)} %param.14) | copy-start | bytes 24580
  69.4 20.0 %collective-permute-start.9 = (bf16[64,4096]{1,0:T(8,128)(2,1)}, bf16[64,4096]{1,0:T(8,128)(2,1)S(1)}, u32[]{:S(2)}, u32[]{:S(2)}) collective-permute-start(bf16[64,4096]{1,0:T(8,128)(2,1)} %get-tuple-element.68), channel_id=1, source_target_pairs={{32,0},{64,32},{96,64},{33,1},{65,33},{97,65},{34,2},{66,34},{98,6... | collective-permute-start | bytes 1572872 | tf_op jit(solution)/shard_map/ppermute | solution.py:803
  72.1 11.9 %collective-permute-start.10 = (bf16[16,4096]{1,0:T(8,128)(2,1)}, bf16[16,4096]{1,0:T(8,128)(2,1)S(1)}, u32[]{:S(2)}, u32[]{:S(2)}) collective-permute-start(bf16[16,4096]{1,0:T(8,128)(2,1)} %get-tuple-element.69), channel_id=1, source_target_pairs={{33,0},{34,1},{35,2},{36,3},{37,4},{38,5},{39,6},{40,7},{41,8},{42... | collective-permute-start | bytes 393224 | tf_op jit(solution)/shard_map/ppermute | solution.py:804
  84.0 5.4 %copy-start.20 = (bf16[16,4096]{1,0:T(8,128)(2,1)}, bf16[16,4096]{1,0:T(8,128)(2,1)S(1)}, u32[]{:S(2)}) copy-start(bf16[16,4096]{1,0:T(8,128)(2,1)S(1)} %collective-permute-done.10.near_halo) | copy-start | bytes 393220
  89.4 0.8 copy-start.11
  92.4 28.9 %collective-permute-start.11 = (bf16[64,4096]{1,0:T(8,128)(2,1)}, bf16[64,4096]{1,0:T(8,128)(2,1)S(1)}, u32[]{:S(2)}, u32[]{:S(2)}) collective-permute-start(bf16[64,4096]{1,0:T(8,128)(2,1)} %get-tuple-element.76), channel_id=1, source_target_pairs={{32,0},{64,32},{96,64},{33,1},{65,33},{97,65},{34,2},{66,34},{98,6... | collective-permute-start | bytes 1572872 | tf_op jit(solution)/shard_map/ppermute | solution.py:803
  95.2 26.1 %collective-permute-start.12 = (bf16[16,4096]{1,0:T(8,128)(2,1)}, bf16[16,4096]{1,0:T(8,128)(2,1)S(1)}, u32[]{:S(2)}, u32[]{:S(2)}) collective-permute-start(bf16[16,4096]{1,0:T(8,128)(2,1)} %get-tuple-element.77), channel_id=1, source_target_pairs={{33,0},{34,1},{35,2},{36,3},{37,4},{38,5},{39,6},{40,7},{41,8},{42... | collective-permute-start | bytes 393224 | tf_op jit(solution)/shard_map/ppermute | solution.py:804
  121.3 0.8 copy-start.8
  128.5 20.7 %collective-permute-start.13 = (bf16[64,4096]{1,0:T(8,128)(2,1)}, bf16[64,4096]{1,0:T(8,128)(2,1)S(1)}, u32[]{:S(2)}, u32[]{:S(2)}) collective-permute-start(bf16[64,4096]{1,0:T(8,128)(2,1)} %get-tuple-element.84), channel_id=1, source_target_pairs={{32,0},{64,32},{96,64},{33,1},{65,33},{97,65},{34,2},{66,34},{98,6... | collective-permute-start | bytes 1572872 | tf_op jit(solution)/shard_map/ppermute | solution.py:803
  130.6 18.6 %collective-permute-start.14 = (bf16[16,4096]{1,0:T(8,128)(2,1)}, bf16[16,4096]{1,0:T(8,128)(2,1)S(1)}, u32[]{:S(2)}, u32[]{:S(2)}) collective-permute-start(bf16[16,4096]{1,0:T(8,128)(2,1)} %get-tuple-element.85), channel_id=1, source_target_pairs={{33,0},{34,1},{35,2},{36,3},{37,4},{38,5},{39,6},{40,7},{41,8},{42... | collective-permute-start | bytes 393224 | tf_op jit(solution)/shard_map/ppermute | solution.py:804
  133.5 26.2 %all-to-all-start.1 = ((s32[32,1,96]{2,1,0:T(1,128)}), s32[32,1,96]{2,1,0:T(1,128)S(1)}, u32[]{:S(2)}, u32[]{:S(2)}) async-start(s32[32,1,96]{2,1,0:T(1,128)} %bitcast.29), calls=%async_computation.1 | async-start | bytes 32768 | tf_op jit(solution)/shard_map/all_to_all | solution.py:810
  149.2 0.6 copy-start.17
  149.2 0.8 copy-start.9
  159.6 13.2 %copy-start.25 = (bf16[64,4096]{1,0:T(8,128)(2,1)S(1)}, bf16[64,4096]{1,0:T(8,128)(2,1)}, u32[]{:S(2)}) copy-start(bf16[64,4096]{1,0:T(8,128)(2,1)} %get-tuple-element.88) | copy-start | bytes 1572868
  159.6 16.0 %copy-start.26 = (bf16[16,4096]{1,0:T(8,128)(2,1)S(1)}, bf16[16,4096]{1,0:T(8,128)(2,1)}, u32[]{:S(2)}) copy-start(bf16[16,4096]{1,0:T(8,128)(2,1)} %get-tuple-element.89) | copy-start | bytes 393220
  159.7 82.6 %all-to-all-start.2 = ((bf16[32,24,1024]{2,1,0:T(8,128)(2,1)}), bf16[32,24,1024]{2,1,0:T(8,128)(2,1)S(1)}, u32[]{:S(2)}, u32[]{:S(2)}) async-start(bf16[32,24,1024]{2,1,0:T(8,128)(2,1)} %bitcast.85), calls=%async_computation.2 | async-start | bytes 3145728 | tf_op jit(solution)/shard_map/all_to_all | solution.py:822
  172.8 26.1 %collective-permute-start.15 = (bf16[64,4096]{1,0:T(8,128)(2,1)S(1)}, bf16[64,4096]{1,0:T(8,128)(2,1)S(1)}, u32[]{:S(2)}, u32[]{:S(2)}) collective-permute-start(bf16[64,4096]{1,0:T(8,128)(2,1)S(1)} %copy-done.25), channel_id=1, source_target_pairs={{32,0},{64,32},{96,64},{33,1},{65,33},{97,65},{34,2},{66,34},{98,6... | collective-permute-start | bytes 1572872 | tf_op jit(solution)/shard_map/ppermute | solution.py:803
  175.7 23.2 %collective-permute-start.16 = (bf16[16,4096]{1,0:T(8,128)(2,1)S(1)}, bf16[16,4096]{1,0:T(8,128)(2,1)S(1)}, u32[]{:S(2)}, u32[]{:S(2)}) collective-permute-start(bf16[16,4096]{1,0:T(8,128)(2,1)S(1)} %copy-done.26), channel_id=1, source_target_pairs={{33,0},{34,1},{35,2},{36,3},{37,4},{38,5},{39,6},{40,7},{41,8},{42... | collective-permute-start | bytes 393224 | tf_op jit(solution)/shard_map/ppermute | solution.py:804
  198.9 0.7 copy-start.21
  198.9 0.8 copy-start.10
  206.1 18.2 %collective-permute-start.17 = (bf16[64,4096]{1,0:T(8,128)(2,1)}, bf16[64,4096]{1,0:T(8,128)(2,1)S(1)}, u32[]{:S(2)}, u32[]{:S(2)}) collective-permute-start(bf16[64,4096]{1,0:T(8,128)(2,1)} %get-tuple-element.92), channel_id=1, source_target_pairs={{32,0},{64,32},{96,64},{33,1},{65,33},{97,65},{34,2},{66,34},{98,6... | collective-permute-start | bytes 1572872 | tf_op jit(solution)/shard_map/ppermute | solution.py:803
  207.9 9.7 %collective-permute-start.18 = (bf16[16,4096]{1,0:T(8,128)(2,1)}, bf16[16,4096]{1,0:T(8,128)(2,1)S(1)}, u32[]{:S(2)}, u32[]{:S(2)}) collective-permute-start(bf16[16,4096]{1,0:T(8,128)(2,1)} %get-tuple-element.93), channel_id=1, source_target_pairs={{33,0},{34,1},{35,2},{36,3},{37,4},{38,5},{39,6},{40,7},{41,8},{42... | collective-permute-start | bytes 393224 | tf_op jit(solution)/shard_map/ppermute | solution.py:804
  209.3 43.4 %copy-start.23 = (s32[4,768]{1,0:T(4,128)}, s32[4,768]{1,0:T(4,128)S(1)}, u32[]{:S(2)}) copy-start(s32[4,768]{1,0:T(4,128)S(1)} %broadcast_add_fusion.1.place_of) | copy-start | bytes 36868
  217.6 6.6 %copy-start.19 = (bf16[16,4096]{1,0:T(8,128)(2,1)}, bf16[16,4096]{1,0:T(8,128)(2,1)S(1)}, u32[]{:S(2)}) copy-start(bf16[16,4096]{1,0:T(8,128)(2,1)S(1)} %collective-permute-done.18.near_halo) | copy-start | bytes 393220
  224.3 0.8 copy-start.12
  242.3 12.4 %copy-start.5 = (bf16[32,24,1024]{2,1,0:T(8,128)(2,1)}, bf16[32,24,1024]{2,1,0:T(8,128)(2,1)S(1)}, u32[]{:S(2)}) copy-start(bf16[32,24,1024]{2,1,0:T(8,128)(2,1)S(1)} %all-to-all-done.2) | copy-start | bytes 4718596
  242.3 32.4 %all-to-all-start = ((bf16[32,24,1024]{2,1,0:T(8,128)(2,1)}), bf16[32,24,1024]{2,1,0:T(8,128)(2,1)S(1)}, u32[]{:S(2)}, u32[]{:S(2)}) async-start(bf16[32,24,1024]{2,1,0:T(8,128)(2,1)} %bitcast.84), calls=%async_computation | async-start | bytes 3145728 | tf_op jit(solution)/shard_map/all_to_all | solution.py:823
  274.7 1.2 copy-start.6
  (1 other events, 0.6 us)

commit v5 on v4

--- a/solution.py
+++ b/solution.py
@@ -15,7 +15,7 @@
 STEP = 512
 SPLIT = 4
 MIB = 1 << 20
-VMEM_LIMIT = 60 * MIB
+VMEM_LIMIT = 51 * MIB
 
 f32 = jnp.float32
 bf16 = jnp.bfloat16
@@ -37,7 +37,41 @@
     return sum(chunk[:, i : i + LANES] for i in range(0, STEP, LANES))
 
 
-def values_kernel(memory, weight, v_out, low_one, high_one, low_rest, high_rest, held, wide_held, flat, v, sems):
+def edges_kernel(x, top, for_next, for_last, sems):
+    length = x.shape[1]
+    copies = (
+        pltpu.make_async_copy(x.at[:, pl.ds(length - HALO, HALO)], for_next, sems.at[0]),
+        pltpu.make_async_copy(x.at[:, pl.ds(0, HALO)], for_last.at[:, pl.ds(0, HALO)], sems.at[1]),
+        pltpu.make_async_copy(top.at[:, pl.ds(0, HALO)], for_last.at[:, pl.ds(HALO, HALO)], sems.at[2]),
+    )
+    for copy in copies:
+        copy.start()
+    for copy in copies:
+        copy.wait()
+
+
+def edges(x, top):
+    batches, length, width = x.shape
+    hbm = pl.BlockSpec(memory_space=pltpu.HBM)
+    return pl.pallas_call(
+        edges_kernel,
+        out_shape=(
+            jax.ShapeDtypeStruct((batches, HALO, width), bf16),
+            jax.ShapeDtypeStruct((batches, 2 * HALO, width), bf16),
+        ),
+        in_specs=[hbm] * 2,
+        out_specs=[hbm] * 2,
+        scratch_shapes=[pltpu.SemaphoreType.DMA((3,))],
+        compiler_params=pltpu.CompilerParams(vmem_limit_bytes=VMEM_LIMIT),
+        cost_estimate=pl.CostEstimate(flops=0, bytes_accessed=4 * MIB, transcendentals=0),
+        name="edges",
+    )(x, top)
+
+
+def values_kernel(
+    memory, weight, convs, gains, v_out, low_one, high_one, low_rest, high_rest, taps,
+    held, wide_held, flat, v, sems,
+):
     batches, rows = held.shape[:2]
     heads, _, feature = weight.shape
     length = rows // heads
@@ -45,6 +79,8 @@
     copies = [pltpu.make_async_copy(weight.at[h], flat.at[h], sems.at[1, h]) for h in range(heads)]
     for copy in loads + copies:
         copy.start()
+    for layer in range(taps.shape[0]):
+        taps[layer] = 0.5 * convs[layer] * gains[layer : layer + 1, :]
     step = 64
     for b in range(batches):
         loads[b].wait()
@@ -82,19 +118,21 @@
         copy.wait()
 
 
-def all_values(memory, weight):
+def all_values(memory, weight, convs, gains):
     batches, length, heads, row_width = memory.shape
     feature = weight.shape[2]
     hbm = pl.BlockSpec(memory_space=pltpu.HBM)
     one = jax.ShapeDtypeStruct((1, HALO, heads * feature), f32)
     rest = jax.ShapeDtypeStruct((batches - 1, HALO, heads * feature), f32)
-    v, *halos = pl.pallas_call(
+    vmem = pl.BlockSpec(memory_space=pltpu.VMEM)
+    v, *halos, taps = pl.pallas_call(
         values_kernel,
         out_shape=(
-            jax.ShapeDtypeStruct((batches * length, heads * feature), f32), one, one, rest, rest
+            jax.ShapeDtypeStruct((batches * length, heads * feature), f32), one, one, rest, rest,
+            jax.ShapeDtypeStruct(convs.shape, f32),
         ),
-        in_specs=[hbm] * 2,
-        out_specs=[hbm] * 5,
+        in_specs=[hbm] * 2 + [vmem] * 2,
+        out_specs=[hbm] * 5 + [vmem],
         scratch_shapes=[
             pltpu.VMEM((batches, length * heads, row_width), bf16),
             pltpu.VMEM((row_width // LANES, batches * length * heads, LANES), f32),
@@ -109,14 +147,15 @@
             transcendentals=0,
         ),
         name="all_values",
-    )(memory.reshape(batches, length * heads, row_width), weight)
-    return v.reshape(batches, length, heads * feature), halos
+    )(memory.reshape(batches, length * heads, row_width), weight, convs, gains)
+    return v.reshape(batches, length, heads * feature), halos, taps
 
 
 def forward_kernel(
-    batch, v_halo, live_ref, xb, xm, xa, vb, vm, va, taps, order, hid_out, der_out, scal_out,
-    x_win, v_win, hid, der, scal, rms_now, sems,
+    batch, v_halo, carried, live_ref, xb, xm, xa, vb, vm, va, taps, order, *refs,
 ):
+    hid_out, der_out, scal_out = refs[carried : carried + 3]
+    x_win, v_win, hid, der, scal, rms_now, sems = refs[2 * carried + 3 :]
     width = xm.shape[-1]
     rows = x_win.shape[0]
     keep = rows - HALO
@@ -133,7 +172,7 @@
             for j, (part, window, b) in enumerate(((x_part, x_win, batch), (v_part, v_win, here))):
                 loads[q].append(
                     pltpu.make_async_copy(
-                        part.at[b, :, cols],
+                        part.at[b, pl.ds(0, size), cols],
                         window.at[pl.ds(at, size), cols],
                         sems.at[2 + 3 * j + i, q],
                     )
@@ -217,23 +256,26 @@
     out.wait()
 
 
-def forward_map(batch, v_halo, live, x, x_before, x_after, v, v_before, v_after, taps, order):
+def forward_map(batch, v_halo, live, x, x_before, x_after, v, v_before, v_after, taps, order, carry):
     length, width = x.shape[1:]
     keep = length + HALO
     rows = keep + HALO
     layers = taps.shape[0]
     hbm = pl.BlockSpec(memory_space=pltpu.HBM)
     return pl.pallas_call(
-        functools.partial(forward_kernel, batch, v_halo),
+        functools.partial(forward_kernel, batch, v_halo, len(carry)),
         out_shape=(
             jax.ShapeDtypeStruct((layers, keep, width), f32),
             jax.ShapeDtypeStruct((layers, keep, width), f32),
             jax.ShapeDtypeStruct((8, keep, LANES), f32),
+            *(jax.ShapeDtypeStruct(array.shape, array.dtype) for array in carry),
         ),
         in_specs=[pl.BlockSpec(memory_space=pltpu.SMEM)]
         + [hbm] * 6
-        + [pl.BlockSpec(memory_space=pltpu.VMEM), pl.BlockSpec(memory_space=pltpu.SMEM)],
-        out_specs=[hbm] * 3,
+        + [pl.BlockSpec(memory_space=pltpu.VMEM), pl.BlockSpec(memory_space=pltpu.SMEM)]
+        + [hbm] * len(carry),
+        out_specs=[hbm] * (3 + len(carry)),
+        input_output_aliases={9 + i: 3 + i for i in range(len(carry))},
         scratch_shapes=[
             pltpu.VMEM((rows, width), bf16),
             pltpu.VMEM((rows, width), f32),
@@ -250,7 +292,7 @@
             transcendentals=layers * rows * width,
         ),
         name="forward_map",
-    )(live, x_before, x, x_after, v_before, v, v_after, taps, order)
+    )(live, x_before, x, x_after, v_before, v, v_after, taps, order, *carry)
 
 
 def backward_kernel(
@@ -260,6 +302,8 @@
     refs = refs[3 * held[1] :]
     if held[2]:
         gv_held, refs = refs[1], refs[2:]
+    if held[4]:
+        refs = refs[1:6] + refs[7:]
     if held[3]:
         dest, refs = refs[0], refs[2:]
         packed, stacked, slots_now = refs[5], refs[-2], refs[-1]
@@ -321,13 +365,14 @@
     def _():
         @pl.when(is_top == 1)
         def _():
-            for copy in grad_copies(top.at[which], top_halo.at[which]):
+            for copy in grad_copies(top.at[which], top_halo.at[which, pl.ds(HALO, HALO)]):
                 copy.start()
 
-        @pl.when(is_top == 0)
-        def _():
-            for copy in grad_copies(near, near_halo):
-                copy.start()
+        if held[5]:
+            @pl.when(is_top == 0)
+            def _():
+                for copy in grad_copies(near, near_halo):
+                    copy.start()
 
         for i in range(count):
             @pl.when(which == first + i)
@@ -346,7 +391,7 @@
         for copy in input_copies():
             copy.start()
 
-        for copy in grad_copies(near, near_halo):
+        for copy in grad_copies(top.at[which], top_halo.at[which, pl.ds(HALO, HALO)]):
             copy.wait()
 
         def into_taps(layer, cols, grad):
@@ -464,7 +509,7 @@
             pack()
 
 
-def backward_map(info, near, near_halo, top, top_halo, x, v, taps, first, saved, previous, packing=None):
+def backward_map(info, near, near_halo, top, top_halo, x, v, taps, first, saved, previous, packing=None, carry=None):
     batches, length, width = x.shape
     rows = length + HALO
     layers = taps.shape[0]
@@ -512,9 +557,18 @@
         out_specs.append(hbm)
         feature = width // 8
         scratch += [pltpu.VMEM((8 * length, feature), bf16), pltpu.VMEM((packed.shape[0], feature), bf16)]
+    if carry is not None:
+        aliases[len(operands)] = 5
+        operands.append(carry)
+        specs.append(hbm)
+        shapes.append(jax.ShapeDtypeStruct(carry.shape, carry.dtype))
+        out_specs.append(hbm)
     pack_flag = 0 if packing is None else packing[0] + 1
     return pl.pallas_call(
-        functools.partial(backward_kernel, (first, len(saved), previous is not None, pack_flag)),
+        functools.partial(
+            backward_kernel,
+            (first, len(saved), previous is not None, pack_flag, carry is not None, near.ndim == 2),
+        ),
         out_shape=shapes,
         in_specs=specs,
         out_specs=out_specs,
@@ -565,7 +619,7 @@
         input_output_aliases={} if into is None else {3: 0},
         compiler_params=pltpu.CompilerParams(vmem_limit_bytes=VMEM_LIMIT),
         cost_estimate=pl.CostEstimate(
-            flops=2 * slots * 8 * length * feature, bytes_accessed=2 * MIB, transcendentals=0
+            flops=MIB, bytes_accessed=MIB // 16, transcendentals=0
         ),
         name="pack_values",
     )(*operands)
@@ -749,7 +803,6 @@
     slots = owners * capacity
     weight = value_weight[0]
     live = layer_counts[0]
-    taps = 0.5 * conv_weight[0] * norm_gain[0][:, None, :]
     x = saved_inputs[0]
     is_top = section == sections - 1
 
@@ -761,31 +814,32 @@
         for i in range(sections - 1)
         for t in range(owners - 1)
     ]
-    x_before = lax.ppermute(x[:, length - HALO :], "table", to_next)
-    x_after = lax.ppermute(x[:, :HALO], "table", to_last)
-    v, (low_one, high_one, low_rest, high_rest) = all_values(memory[0], weight)
-    v_before = [lax.ppermute(high_one, "table", to_next)]
-    v_after = [lax.ppermute(low_one, "table", to_last)]
-    top_halo = lax.ppermute(out_grad[:, :HALO], "table", to_last)
-    v_before.append(lax.ppermute(high_rest, "table", to_next))
-    v_after.append(lax.ppermute(low_rest, "table", to_last))
+    for_next, for_last = edges(x, out_grad)
+    x_before = lax.ppermute(for_next, "table", to_next)
+    x_after = lax.ppermute(for_last, "table", to_last)
+    v, (low_one, high_one, low_rest, high_rest), taps = all_values(
+        memory[0], weight, conv_weight[0], norm_gain[0]
+    )
+    v_before = lax.ppermute(high_one, "table", to_next)
+    v_after = lax.ppermute(low_one, "table", to_last)
 
     saved = []
-    near = jnp.zeros((length, width), bf16)
-    near_halo = jnp.zeros((HALO, width), bf16)
     outputs = table = dest = holds = place_of = row_of = groups = got = None
     packed = [None, None]
     order = jnp.zeros((1,), jnp.int32)
+    near = near_halo = order
     ticks = batches + sections - 1
     for tick in range(ticks):
         if tick < batches:
-            which_halo = min(tick, 1)
-            saved.append(
-                forward_map(
-                    tick, max(tick - 1, 0), live.reshape(1), x, x_before, x_after,
-                    v, v_before[which_halo], v_after[which_halo], taps, order,
-                )
+            carry = (high_rest, low_rest) if tick == 0 else ()
+            *state, = forward_map(
+                tick, max(tick - 1, 0), live.reshape(1), x, x_before, x_after,
+                v, v_before, v_after, taps, order, carry,
             )
+            saved.append(state[:3])
+            if tick == 0:
+                v_before = lax.ppermute(state[3], "table", to_next)
+                v_after = lax.ppermute(state[4], "table", to_last)
         position = tick - (sections - 1 - section)
         which = jnp.clip(position, 0, batches - 1)
         active = (position >= 0) & (position < batches)
@@ -793,9 +847,12 @@
         first = max(0, tick - (sections - 1))
         packing = (batches - 1, dest[batches - 1][None, :], packed[1]) if tick == ticks - 1 else None
         grad_send, halo_send, *outputs = backward_map(
-            info, near, near_halo, out_grad, top_halo, x, v, taps,
-            first, saved[first : tick + 1], outputs, packing,
+            info, near, near_halo, out_grad, x_after, x, v, taps,
+            first, saved[first : tick + 1], outputs, packing, packed[0] if tick == ticks - 2 else None,
         )
+        if tick == ticks - 2:
+            packed[0] = outputs.pop()
+            got = lax.all_to_all(packed[0], "table", 0, 0, tiled=True)
         if packing is not None:
             packed[1] = outputs.pop()
         order = outputs.pop()
@@ -806,11 +863,11 @@
             dest, holds = slots_of(row_ids[0] + order, owners, capacity)
             holds = holds.reshape(batches, owners, capacity).transpose(1, 0, 2)
             holds = holds.reshape(owners, batches * capacity)
-        if tick == sections - 1:
+        if tick == sections:
             holds = lax.all_to_all(holds + order, "table", 0, 0, tiled=True)
             holds = holds.reshape(owners, batches, capacity).transpose(1, 0, 2)
             holds = holds.reshape(batches, slots)
-        if tick == sections:
+        if tick == sections + 1:
             place_of, row_of, groups = groups_of(holds + order, heads)
         batch = tick - (sections - 1)
         if 0 <= batch < batches - 1:
@@ -818,8 +875,6 @@
             packed[pair] = pack_values(
                 batch, dest[batch][None, :], outputs[1], slots, order, packed[pair], at, 2
             )
-        if batch == 2:
-            got = lax.all_to_all(packed[0], "table", 0, 0, tiled=True)
     rest = lax.all_to_all(packed[1], "table", 0, 0, tiled=True)
     table = owner_add(0, 2, None, got, place_of, row_of, groups, weight, order)
     table = owner_add(2, 2, table, rest, place_of, row_of, groups, weight, order)

time: 296 us -> 278 us (0.939)
  local copies, waits for them, and re-layouts: 16.4 us -> 7.94 us
  starting transfers between devices: 69.9 us -> 62.7 us
  other arithmetic: 12.6 us -> 7.19 us
  waiting for transfers between devices: 72.9 us -> 76.6 us
    ppermute x7 -> x6, waiting for transfers between devices: 0.02 us -> 10.8 us  [the longest x1 4.69 us: shards(): v_after = lax.ppermute(state[4], 'table', to_last)]
    ppermute x6, waiting for transfers between devices: 16.6 us -> 6.98 us  [shards(): near = lax.ppermute(grad_send, 'section', down)]
    ppermute x7 -> x6, starting transfers between devices: 19.5 us -> 15.2 us  [the longest x1 3.33 us: shards(): x_after = lax.ppermute(for_last, 'table', to_last)]
    slice x2 -> x0, local copies, waits for them, and re-layouts: 4.18 us -> none  [the longest x1 2.3 us: shards(): x_after = lax.ppermute(x[:, :HALO], 'table', to_last)]
    another operation x7, other arithmetic: 4.56 us -> 0.56 us  [shards(): info = jnp.stack([which, active, is_top, live]).astype(jnp.int32)]
    pallas_call x3, Pallas kernels: 9.75 us -> 6.67 us  [pack_values(): pl.pallas_call(pack_kernel, out_shape=jax.ShapeDtypeStruct((slots, total...]
    pallas_call x4 -> x5, Pallas kernels: 26.2 us -> 29.2 us  [the longest x4 27.8 us: forward_map(): pl.pallas_call(functools.partial(forward_kernel, batch, v_halo, len(carry...]
    unnamed x54 -> x30, local copies, waits for them, and re-layouts: 8.97 us -> 6.82 us
  transfers between devices with their start and end apart: 22 -> 21, of which waited for: 9 -> 11; matrix products, arithmetic and copies ran while one was open for 6% -> 3% of each run, Pallas kernels for 31% -> 28%
where the time goes in v5:
time: 278 us; the launch traced here: 275 us
  Pallas kernels  118 us (42%)
  waiting for transfers between devices  76.6 us (28%)
  starting transfers between devices  62.7 us (23%)
  local copies, waits for them, and re-layouts  7.94 us (3%)
  other arithmetic  7.19 us (3%)
    ppermute x6, waiting for transfers between devices, shards(): near_halo = lax.ppermute(halo_send, ('section', 'table'), down_halo)  52.7 us
    pallas_call x7, Pallas kernels, backward_map(): pl.pallas_call(functools.partial(backward_kernel, (first, len(saved), pre...  45.6 us
    pallas_call x2, Pallas kernels, owner_add(): pl.pallas_call(functools.partial(owner_kernel, first, count, table is not...  29.3 us
    pallas_call x4, Pallas kernels, forward_map(): pl.pallas_call(functools.partial(forward_kernel, batch, v_halo, len(carry...  27.8 us
    all_to_all x1, starting transfers between devices, shards(): holds = lax.all_to_all(holds + order, 'table', 0, 0, tiled=True)  14.7 us
    all_to_all x1, starting transfers between devices, shards(): got = lax.all_to_all(packed[0], 'table', 0, 0, tiled=True)  10.2 us
    ppermute x6, starting transfers between devices, shards(): near = lax.ppermute(grad_send, 'section', down)  7.74 us
    ppermute x6, starting transfers between devices, shards(): near_halo = lax.ppermute(halo_send, ('section', 'table'), down_halo)  7.73 us
  transfers between devices with their start and end apart: 21, of which 11 were waited for; matrix products, arithmetic and copies ran while one was open for 3% of the time, Pallas kernels for 28%

profile of v5, /device:TPU:1, one launch (start us, length us, event | category | flops | bytes accessed | tf_op | source)
XLA Modules:
  0.0 275.4 jit_solution(3347621481129453638)
XLA Ops:
  0.6 1.4 edges.1
  2.1 3.3 %collective-permute-start = (bf16[4,32,4096]{2,1,0:T(8,128)(2,1)S(1)}, bf16[4,32,4096]{2,1,0:T(8,128)(2,1)S(1)}, u32[]{:S(2)}, u32[]{:S(2)}) collective-permute-start(bf16[4,32,4096]{2,1,0:T(8,128)(2,1)S(1)} %get-tuple-element.58), channel_id=1, source_target_pairs={{1,0},{2,1},{3,2},{4,3},{5,4},{6,5},{7,6},{8,7},{9,8},{10,9},{11,1... | collective-permute-start | bytes 3145736 | tf_op jit(solution)/shard_map/ppermute | solution.py:819
  5.4 3.2 %collective-permute-start.1 = (bf16[4,16,4096]{2,1,0:T(8,128)(2,1)S(1)}, bf16[4,16,4096]{2,1,0:T(8,128)(2,1)S(1)}, u32[]{:S(2)}, u32[]{:S(2)}) collective-permute-start(bf16[4,16,4096]{2,1,0:T(8,128)(2,1)S(1)} %get-tuple-element.61), channel_id=1, source_target_pairs={{0,1},{1,2},{2,3},{3,4},{4,5},{5,6},{6,7},{7,8},{8,9},{9,10},{10,1... | collective-permute-start | bytes 1572872 | tf_op jit(solution)/shard_map/ppermute | solution.py:818
  8.6 7.6 %all_values.1 = (f32[256,4096]{1,0:T(8,128)}, f32[1,16,4096]{2,1,0:T(8,128)S(1)}, f32[1,16,4096]{2,1,0:T(8,128)S(1)}, f32[3,16,4096]{2,1,0:T(8,128)S(1)}, f32[3,...) custom-call(bf16[4,512,1024]{2,1,0:T(8,128)(2,1)} %bitcast.90, bf16[8,1024,512]{2,1,0:T(8,128)(2,1)} %bitcast.87, ...), custom_call_target="tpu_custom_call" | custom-call | flops 2147483648 | bytes 18874368 | tf_op jit(solution)/shard_map/all_values/pallas_call | solution.py:128
  17.2 2.4 collective-permute-start.2
  19.6 1.9 collective-permute-start.3
  22.9 4.4 %collective-permute-done.3.va = f32[1,16,4096]{2,1,0:T(8,128)S(1)} collective-permute-done((f32[1,16,4096]{2,1,0:T(8,128)S(1)}, f32[1,16,4096]{2,1,0:T(8,128)S(1)}, u32[]{:S(2)}, u32[]{:S(2)}) %collective-permute-start.3) | collective-permute-done | bytes 262176 | tf_op jit(solution)/shard_map/ppermute | solution.py:824
  28.2 6.5 %forward_map.4 = (f32[4,80,4096]{2,1,0:T(8,128)}, f32[4,80,4096]{2,1,0:T(8,128)}, f32[8,80,128]{2,1,0:T(8,128)S(1)}, f32[3,16,4096]{2,1,0:T(8,128)}, f32[3,16,4096]{2,1,0:T(8,128)}) custom-call(s32[1]{0:T(128)S(6)} %copy.52.live_ref, bf16[4,16,4096]{2,1,0:T(8,128)(2,1)S(1)} %collective-permute-done.1.xb, ...), custom_call_target="tpu_custom_call", output_to_operand_aliasing={{3}: (9, {}), {4}: (10, {})} | custom-call | flops 47185920 | bytes 16777216 | tf_op jit(solution)/shard_map/forward_map/pallas_call | solution.py:265
  34.7 1.9 collective-permute-start.6
  36.6 2.5 collective-permute-start.7
  40.4 1.8 backward_map.7
  42.2 1.3 collective-permute-start.4
  43.5 1.3 collective-permute-start.5
  45.9 4.7 %collective-permute-done.7.va = f32[3,16,4096]{2,1,0:T(8,128)S(1)} collective-permute-done((f32[3,16,4096]{2,1,0:T(8,128)}, f32[3,16,4096]{2,1,0:T(8,128)S(1)}, u32[]{:S(2)}, u32[]{:S(2)}) %collective-permute-start.7) | collective-permute-done | bytes 786464 | tf_op jit(solution)/shard_map/ppermute | solution.py:842
  50.6 7.1 %forward_map.5 = (f32[4,80,4096]{2,1,0:T(8,128)}, f32[4,80,4096]{2,1,0:T(8,128)}, f32[8,80,128]{2,1,0:T(8,128)S(1)}) custom-call(s32[1]{0:T(128)S(6)} %copy.52.live_ref, bf16[4,16,4096]{2,1,0:T(8,128)(2,1)S(1)} %collective-permute-done.1.xb, bf16[4,64,4096]{2,1,0:T(8,128)(2,1)} %bitcast.77, bf16[4,32,4096]{2,1,0:T(8,128)(2,1)} %copy-done, ...), custom_call_target="tpu_custom_call" | custom-call | flops 47185920 | bytes 16777216 | tf_op jit(solution)/shard_map/forward_map/pallas_call | solution.py:265
  57.7 3.0 %collective-permute-done.4.near = bf16[64,4096]{1,0:T(8,128)(2,1)} collective-permute-done((bf16[64,4096]{1,0:T(8,128)(2,1)}, bf16[64,4096]{1,0:T(8,128)(2,1)}, u32[]{:S(2)}, u32[]{:S(2)}) %collective-permute-start.4) | collective-permute-done | bytes 524320 | tf_op jit(solution)/shard_map/ppermute | solution.py:860
  60.7 1.8 backward_map.8
  62.5 1.3 collective-permute-start.8
  63.9 1.3 collective-permute-start.9
  66.0 7.2 %forward_map.6 = (f32[4,80,4096]{2,1,0:T(8,128)}, f32[4,80,4096]{2,1,0:T(8,128)}, f32[8,80,128]{2,1,0:T(8,128)S(1)}) custom-call(s32[1]{0:T(128)S(6)} %copy.52.live_ref, bf16[4,16,4096]{2,1,0:T(8,128)(2,1)S(1)} %collective-permute-done.1.xb, bf16[4,64,4096]{2,1,0:T(8,128)(2,1)} %bitcast.79, bf16[4,32,4096]{2,1,0:T(8,128)(2,1)} %copy-done, ...), custom_call_target="tpu_custom_call" | custom-call | flops 47185920 | bytes 16777216 | tf_op jit(solution)/shard_map/forward_map/pallas_call | solution.py:265
  74.4 3.9 %collective-permute-done.8.near = bf16[64,4096]{1,0:T(8,128)(2,1)} collective-permute-done((bf16[64,4096]{1,0:T(8,128)(2,1)}, bf16[64,4096]{1,0:T(8,128)(2,1)}, u32[]{:S(2)}, u32[]{:S(2)}) %collective-permute-start.8) | collective-permute-done | bytes 524320 | tf_op jit(solution)/shard_map/ppermute | solution.py:860
  78.4 2.0 backward_map.9
  81.1 1.3 collective-permute-start.10
  83.2 1.3 collective-permute-start.11
  84.5 7.1 %forward_map.7 = (f32[4,80,4096]{2,1,0:T(8,128)}, f32[4,80,4096]{2,1,0:T(8,128)}, f32[8,80,128]{2,1,0:T(8,128)S(1)}) custom-call(s32[1]{0:T(128)S(6)} %copy.52.live_ref, bf16[4,16,4096]{2,1,0:T(8,128)(2,1)S(1)} %collective-permute-done.1.xb, bf16[4,64,4096]{2,1,0:T(8,128)(2,1)} %bitcast.81, bf16[4,32,4096]{2,1,0:T(8,128)(2,1)} %copy-done, ...), custom_call_target="tpu_custom_call" | custom-call | flops 47185920 | bytes 16777216 | tf_op jit(solution)/shard_map/forward_map/pallas_call | solution.py:265
  91.6 22.3 %collective-permute-done.11.near_halo = bf16[16,4096]{1,0:T(8,128)(2,1)S(1)} collective-permute-done((bf16[16,4096]{1,0:T(8,128)(2,1)}, bf16[16,4096]{1,0:T(8,128)(2,1)S(1)}, u32[]{:S(2)}, u32[]{:S(2)}) %collective-permute-start.11) | collective-permute-done | bytes 131104 | tf_op jit(solution)/shard_map/ppermute | solution.py:861
  113.8 7.4 %backward_map.10 = (bf16[64,4096]{1,0:T(8,128)(2,1)S(1)}, bf16[16,4096]{1,0:T(8,128)(2,1)S(1)}, bf16[4,64,4096]{2,1,0:T(8,128)(2,1)}, bf16[4,64,4096]{2,1,0:T(8,128)(2,1)}, s32[1]{0:T(128)}) custom-call(s32[4]{0:T(128)S(1)} %add_add_fusion.5.info, bf16[64,4096]{1,0:T(8,128)(2,1)} %collective-permute-done.10.near, ...), custom_call_target="tpu_custom_call", output_to_operand_aliasing={{2}: (20, {}), {3}: (21, {})} | custom-call | flops 32768000 | bytes 14680064 | tf_op jit(solution)/shard_map/backward_map/pallas_call | solution.py:567
  121.2 1.3 collective-permute-start.12
  123.8 1.3 collective-permute-start.13
  125.1 2.3 pack_values.3.refs_0_
  127.4 12.3 %collective-permute-done.13.near_halo = bf16[16,4096]{1,0:T(8,128)(2,1)S(1)} collective-permute-done((bf16[16,4096]{1,0:T(8,128)(2,1)S(1)}, bf16[16,4096]{1,0:T(8,128)(2,1)S(1)}, u32[]{:S(2)}, u32[]{:S(2)}) %collective-permute-start.13) | collective-permute-done | bytes 131104 | tf_op jit(solution)/shard_map/ppermute | solution.py:861
  139.7 7.3 %backward_map.11 = (bf16[64,4096]{1,0:T(8,128)(2,1)}, bf16[16,4096]{1,0:T(8,128)(2,1)S(1)}, bf16[4,64,4096]{2,1,0:T(8,128)(2,1)}, bf16[4,64,4096]{2,1,0:T(8,128)(2,1)}, s32[1]{0:T(128)}) custom-call(s32[4]{0:T(128)S(1)} %add_add_fusion.4.info, bf16[64,4096]{1,0:T(8,128)(2,1)S(1)} %collective-permute-done.12.near, ...), custom_call_target="tpu_custom_call", output_to_operand_aliasing={{2}: (17, {}), {3}: (18, {})} | custom-call | flops 32768000 | bytes 14680064 | tf_op jit(solution)/shard_map/backward_map/pallas_call | solution.py:567
  147.0 1.3 collective-permute-start.14
  149.1 1.3 collective-permute-start.15
  151.9 14.7 %all-to-all-start.1 = ((s32[32,1,96]{2,1,0:T(1,128)}), s32[32,1,96]{2,1,0:T(1,128)S(1)}, u32[]{:S(2)}, u32[]{:S(2)}) async-start(s32[32,1,96]{2,1,0:T(1,128)} %bitcast.29), calls=%async_computation.1 | async-start | bytes 32768 | tf_op jit(solution)/shard_map/all_to_all | solution.py:867
  166.7 2.2 pack_values.4.refs_8_
  170.1 7.4 %backward_map.12 = (bf16[64,4096]{1,0:T(8,128)(2,1)S(1)}, bf16[16,4096]{1,0:T(8,128)(2,1)S(1)}, bf16[4,64,4096]{2,1,0:T(8,128)(2,1)}, bf16[4,64,4096]{2,1,0:T(8,...) custom-call(s32[4]{0:T(128)S(1)} %add_add_fusion.3.info, ...), custom_call_target="tpu_custom_call", output_to_operand_aliasing={{2}: (14, {}), {3}: (15, {}), {5}: (16, {})} | custom-call | flops 32768000 | bytes 14680064 | tf_op jit(solution)/shard_map/backward_map/pallas_call | solution.py:567
  178.3 10.2 %all-to-all-start.2 = ((bf16[32,24,1024]{2,1,0:T(8,128)(2,1)}), bf16[32,24,1024]{2,1,0:T(8,128)(2,1)}, u32[]{:S(2)}, u32[]{:S(2)}) async-start(bf16[32,24,1024]{2,1,0:T(8,128)(2,1)} %bitcast.58), calls=%async_computation.2 | async-start | bytes 3145728 | tf_op jit(solution)/shard_map/all_to_all | solution.py:855
  189.5 1.3 collective-permute-start.16
  191.0 1.3 collective-permute-start.17
  192.3 2.2 pack_values.5.refs_6_
  196.2 16.9 %collective-permute-done.17.near_halo = bf16[16,4096]{1,0:T(8,128)(2,1)S(1)} collective-permute-done((bf16[16,4096]{1,0:T(8,128)(2,1)S(1)}, bf16[16,4096]{1,0:T(8,128)(2,1)S(1)}, u32[]{:S(2)}, u32[]{:S(2)}) %collective-permute-start.17) | collective-permute-done | bytes 131104 | tf_op jit(solution)/shard_map/ppermute | solution.py:861
  213.1 18.0 %backward_map.13 = (bf16[64,4096]{1,0:T(8,128)(2,1)}, bf16[16,4096]{1,0:T(8,128)(2,1)}, bf16[4,64,4096]{2,1,0:T(8,128)(2,1)}, bf16[4,64,4096]{2,1,0:T(8,128)(2,1)}, s32[1]{0:T(128)}, /*index=5*/bf16[768,1024]{1,0:T(8,128)(2,1)}) custom-call(s32[4]{0:T(128)S(1)} %add_add_fusion.2.info, ...), custom_call_target="tpu_custom_call", output_to_operand_aliasing={{2}: (11, {}), {3}: (12, {}), {5}: (14, {})} | custom-call | flops 32768000 | bytes 14680064 | tf_op jit(solution)/shard_map/backward_map/pallas_call | solution.py:567
  231.2 7.1 %all-to-all-start = ((bf16[32,24,1024]{2,1,0:T(8,128)(2,1)}), bf16[32,24,1024]{2,1,0:T(8,128)(2,1)S(1)}, u32[]{:S(2)}, u32[]{:S(2)}) async-start(bf16[32,24,1024]{2,1,0:T(8,128)(2,1)} %bitcast.59), calls=%async_computation | async-start | bytes 3145728 | tf_op jit(solution)/shard_map/all_to_all | solution.py:878
  238.3 1.4 select_reduce_fusion
  239.8 15.1 %owner_add.2.refs_0_ = f32[1024,1024]{1,0:T(8,128)} custom-call(bf16[768,1024]{1,0:T(8,128)(2,1)} %bitcast.35.got, s32[4,768]{1,0:T(4,128)S(1)} %broadcast_add_fusion.1.place_of, s32[4,896]{1,0:T(4,128)S(1)} %broadcast_add_fusion.row_of, s32[4,16]{1,0:T(4,128)S(1)} %pad_add_fusion.groups, s32[1]{0:T(128)} %get-tuple-element.112.order, ...), custom_call_target="tpu_custom_call" | custom-call | flops 9663676416 | bytes 18874368 | tf_op jit(solution)/shard_map/owner_add/pallas_call | solution.py:732
  254.9 6.1 %all-to-all-done = bf16[32,24,1024]{2,1,0:T(8,128)(2,1)S(1)} async-done(((bf16[32,24,1024]{2,1,0:T(8,128)(2,1)}), bf16[32,24,1024]{2,1,0:T(8,128)(2,1)S(1)}, u32[]{:S(2)}, u32[]{:S(2)}) %all-to-all-start) | async-done | bytes 1572896 | tf_op jit(solution)/shard_map/all_to_all | solution.py:878
  261.0 14.2 %owner_add.3 = f32[1024,1024]{1,0:T(8,128)} custom-call(bf16[768,1024]{1,0:T(8,128)(2,1)S(1)} %bitcast.60, s32[4,768]{1,0:T(4,128)S(1)} %broadcast_add_fusion.1.place_of, s32[4,896]{1,0:T(4,128)S(1)} %broadcast_add_fusion.row_of, s32[4,16]{1,0:T(4,128)S(1)} %pad_add_fusion.groups, s32[1]{0:T(128)} %get-tuple-element.112.order, ...), custom_call_target="tpu_custom_call" | custom-call | flops 9663676416 | bytes 18874368 | tf_op jit(solution)/shard_map/owner_add/pallas_call | solution.py:732
  (76 shorter events, 17.0 us)
Async XLA Ops:
  0.6 8.0 %copy-start.8 = (f32[1,4,4,4096]{3,2,1,0:T(4,128)S(1)}, f32[1,4,4,4096]{3,2,1,0:T(4,128)}, u32[]{:S(2)}) copy-start(f32[1,4,4,4096]{3,2,1,0:T(4,128)} %param.11) | copy-start | bytes 786436
  0.6 8.0 %copy-start.9 = (f32[1,4,4096]{2,1,0:T(4,128)S(1)}, f32[1,4,4096]{2,1,0:T(4,128)}, u32[]{:S(2)}) copy-start(f32[1,4,4096]{2,1,0:T(4,128)} %param.12) | copy-start | bytes 196612
  2.1 25.2 %collective-permute-start = (bf16[4,32,4096]{2,1,0:T(8,128)(2,1)S(1)}, bf16[4,32,4096]{2,1,0:T(8,128)(2,1)S(1)}, u32[]{:S(2)}, u32[]{:S(2)}) collective-permute-start(bf16[4,32,4096]{2,1,0:T(8,128)(2,1)S(1)} %get-tuple-element.58), channel_id=1, source_target_pairs={{1,0},{2,1},{3,2},{4,3},{5,4},{6,5},{7,6},{8,7},{9,8},{10,9},{11,1... | collective-permute-start | bytes 3145736 | tf_op jit(solution)/shard_map/ppermute | solution.py:819
  5.4 21.9 %collective-permute-start.1 = (bf16[4,16,4096]{2,1,0:T(8,128)(2,1)S(1)}, bf16[4,16,4096]{2,1,0:T(8,128)(2,1)S(1)}, u32[]{:S(2)}, u32[]{:S(2)}) collective-permute-start(bf16[4,16,4096]{2,1,0:T(8,128)(2,1)S(1)} %get-tuple-element.61), channel_id=1, source_target_pairs={{0,1},{1,2},{2,3},{3,4},{4,5},{5,6},{6,7},{7,8},{8,9},{9,10},{10,1... | collective-permute-start | bytes 1572872 | tf_op jit(solution)/shard_map/ppermute | solution.py:818
  16.3 0.9 copy-start.7
  17.2 5.7 %collective-permute-start.2 = (f32[1,16,4096]{2,1,0:T(8,128)S(1)}, f32[1,16,4096]{2,1,0:T(8,128)S(1)}, u32[]{:S(2)}, u32[]{:S(2)}) collective-permute-start(f32[1,16,4096]{2,1,0:T(8,128)S(1)} %get-tuple-element.62), channel_id=1, source_target_pairs={{0,1},{1,2},{2,3},{3,4},{4,5},{5,6},{6,7},{7,8},{8,9},{9,10},{10,1... | collective-permute-start | bytes 786440 | tf_op jit(solution)/shard_map/ppermute | solution.py:823
  19.6 7.7 %collective-permute-start.3 = (f32[1,16,4096]{2,1,0:T(8,128)S(1)}, f32[1,16,4096]{2,1,0:T(8,128)S(1)}, u32[]{:S(2)}, u32[]{:S(2)}) collective-permute-start(f32[1,16,4096]{2,1,0:T(8,128)S(1)} %get-tuple-element.63), channel_id=1, source_target_pairs={{1,0},{2,1},{3,2},{4,3},{5,4},{6,5},{7,6},{8,7},{9,8},{10,9},{11,1... | collective-permute-start | bytes 786440 | tf_op jit(solution)/shard_map/ppermute | solution.py:824
  27.3 0.9 copy-start
  34.7 11.2 %collective-permute-start.6 = (f32[3,16,4096]{2,1,0:T(8,128)}, f32[3,16,4096]{2,1,0:T(8,128)S(1)}, u32[]{:S(2)}, u32[]{:S(2)}) collective-permute-start(f32[3,16,4096]{2,1,0:T(8,128)} %get-tuple-element.71), channel_id=1, source_target_pairs={{0,1},{1,2},{2,3},{3,4},{4,5},{5,6},{6,7},{7,8},{8,9},{9,10},{10,1... | collective-permute-start | bytes 2359304 | tf_op jit(solution)/shard_map/ppermute | solution.py:841
  36.6 13.9 %collective-permute-start.7 = (f32[3,16,4096]{2,1,0:T(8,128)}, f32[3,16,4096]{2,1,0:T(8,128)S(1)}, u32[]{:S(2)}, u32[]{:S(2)}) collective-permute-start(f32[3,16,4096]{2,1,0:T(8,128)} %get-tuple-element.72), channel_id=1, source_target_pairs={{1,0},{2,1},{3,2},{4,3},{5,4},{6,5},{7,6},{8,7},{9,8},{10,9},{11,1... | collective-permute-start | bytes 2359304 | tf_op jit(solution)/shard_map/ppermute | solution.py:842
  39.2 1.2 copy-start.1
  42.2 18.5 %collective-permute-start.4 = (bf16[64,4096]{1,0:T(8,128)(2,1)}, bf16[64,4096]{1,0:T(8,128)(2,1)}, u32[]{:S(2)}, u32[]{:S(2)}) collective-permute-start(bf16[64,4096]{1,0:T(8,128)(2,1)} %get-tuple-element.69), channel_id=1, source_target_pairs={{32,0},{64,32},{96,64},{33,1},{65,33},{97,65},{34,2},{66,34},{98,6... | collective-permute-start | bytes 1572872 | tf_op jit(solution)/shard_map/ppermute | solution.py:860
  43.5 14.2 %collective-permute-start.5 = (bf16[16,4096]{1,0:T(8,128)(2,1)S(1)}, bf16[16,4096]{1,0:T(8,128)(2,1)S(1)}, u32[]{:S(2)}, u32[]{:S(2)}) collective-permute-start(bf16[16,4096]{1,0:T(8,128)(2,1)S(1)} %get-tuple-element.70), channel_id=1, source_target_pairs={{33,0},{34,1},{35,2},{36,3},{37,4},{38,5},{39,6},{40,7},{41,8},{42... | collective-permute-start | bytes 393224 | tf_op jit(solution)/shard_map/ppermute | solution.py:861
  62.5 15.9 %collective-permute-start.8 = (bf16[64,4096]{1,0:T(8,128)(2,1)}, bf16[64,4096]{1,0:T(8,128)(2,1)}, u32[]{:S(2)}, u32[]{:S(2)}) collective-permute-start(bf16[64,4096]{1,0:T(8,128)(2,1)} %get-tuple-element.79), channel_id=1, source_target_pairs={{32,0},{64,32},{96,64},{33,1},{65,33},{97,65},{34,2},{66,34},{98,6... | collective-permute-start | bytes 1572872 | tf_op jit(solution)/shard_map/ppermute | solution.py:860
  63.9 10.5 %collective-permute-start.9 = (bf16[16,4096]{1,0:T(8,128)(2,1)}, bf16[16,4096]{1,0:T(8,128)(2,1)S(1)}, u32[]{:S(2)}, u32[]{:S(2)}) collective-permute-start(bf16[16,4096]{1,0:T(8,128)(2,1)} %get-tuple-element.80), channel_id=1, source_target_pairs={{33,0},{34,1},{35,2},{36,3},{37,4},{38,5},{39,6},{40,7},{41,8},{42... | collective-permute-start | bytes 393224 | tf_op jit(solution)/shard_map/ppermute | solution.py:861
  78.4 4.1 %copy-start.14 = (s32[1,4,64,8]{2,3,1,0:T(8,128)S(1)}, s32[1,4,64,8]{2,3,1,0:T(8,128)}, u32[]{:S(2)}) copy-start(s32[1,4,64,8]{2,3,1,0:T(8,128)} %param.14) | copy-start | bytes 24580
  80.4 0.6 copy-start.12
  81.1 32.8 %collective-permute-start.10 = (bf16[64,4096]{1,0:T(8,128)(2,1)}, bf16[64,4096]{1,0:T(8,128)(2,1)}, u32[]{:S(2)}, u32[]{:S(2)}) collective-permute-start(bf16[64,4096]{1,0:T(8,128)(2,1)} %get-tuple-element.87), channel_id=1, source_target_pairs={{32,0},{64,32},{96,64},{33,1},{65,33},{97,65},{34,2},{66,34},{98,6... | collective-permute-start | bytes 1572872 | tf_op jit(solution)/shard_map/ppermute | solution.py:860
  83.2 30.7 %collective-permute-start.11 = (bf16[16,4096]{1,0:T(8,128)(2,1)}, bf16[16,4096]{1,0:T(8,128)(2,1)S(1)}, u32[]{:S(2)}, u32[]{:S(2)}) collective-permute-start(bf16[16,4096]{1,0:T(8,128)(2,1)} %copy-done.12), channel_id=1, source_target_pairs={{33,0},{34,1},{35,2},{36,3},{37,4},{38,5},{39,6},{40,7},{41,8},{42... | collective-permute-start | bytes 393224 | tf_op jit(solution)/shard_map/ppermute | solution.py:861
  91.6 48.1 %copy-start.5 = (f32[8,80,128]{2,1,0:T(8,128)}, f32[8,80,128]{2,1,0:T(8,128)S(1)}, u32[]{:S(2)}) copy-start(f32[8,80,128]{2,1,0:T(8,128)S(1)} %get-tuple-element.92.refs_11_.refs_8_.refs_5_.refs_2_) | copy-start | bytes 983044
  113.8 8.7 %copy-start.13 = (pred[512,512]{1,0:T(8,128)(4,1)S(1)}, pred[512,512]{1,0:T(8,128)(4,1)}, u32[]{:S(2)}) copy-start(pred[512,512]{1,0:T(8,128)(4,1)} %iota_compare_fusion.3) | copy-start | bytes 786436
  121.2 18.5 %collective-permute-start.12 = (bf16[64,4096]{1,0:T(8,128)(2,1)S(1)}, bf16[64,4096]{1,0:T(8,128)(2,1)S(1)}, u32[]{:S(2)}, u32[]{:S(2)}) collective-permute-start(bf16[64,4096]{1,0:T(8,128)(2,1)S(1)} %get-tuple-element.95), channel_id=1, source_target_pairs={{32,0},{64,32},{96,64},{33,1},{65,33},{97,65},{34,2},{66,34},{98,6... | collective-permute-start | bytes 1572872 | tf_op jit(solution)/shard_map/ppermute | solution.py:860
  123.8 15.9 %collective-permute-start.13 = (bf16[16,4096]{1,0:T(8,128)(2,1)S(1)}, bf16[16,4096]{1,0:T(8,128)(2,1)S(1)}, u32[]{:S(2)}, u32[]{:S(2)}) collective-permute-start(bf16[16,4096]{1,0:T(8,128)(2,1)S(1)} %get-tuple-element.96), channel_id=1, source_target_pairs={{33,0},{34,1},{35,2},{36,3},{37,4},{38,5},{39,6},{40,7},{41,8},{42... | collective-permute-start | bytes 393224 | tf_op jit(solution)/shard_map/ppermute | solution.py:861
  147.0 23.1 %collective-permute-start.14 = (bf16[64,4096]{1,0:T(8,128)(2,1)}, bf16[64,4096]{1,0:T(8,128)(2,1)S(1)}, u32[]{:S(2)}, u32[]{:S(2)}) collective-permute-start(bf16[64,4096]{1,0:T(8,128)(2,1)} %get-tuple-element.99), channel_id=1, source_target_pairs={{32,0},{64,32},{96,64},{33,1},{65,33},{97,65},{34,2},{66,34},{98,6... | collective-permute-start | bytes 1572872 | tf_op jit(solution)/shard_map/ppermute | solution.py:860
  149.1 21.0 %collective-permute-start.15 = (bf16[16,4096]{1,0:T(8,128)(2,1)S(1)}, bf16[16,4096]{1,0:T(8,128)(2,1)S(1)}, u32[]{:S(2)}, u32[]{:S(2)}) collective-permute-start(bf16[16,4096]{1,0:T(8,128)(2,1)S(1)} %get-tuple-element.100), channel_id=1, source_target_pairs={{33,0},{34,1},{35,2},{36,3},{37,4},{38,5},{39,6},{40,7},{41,8},{42... | collective-permute-start | bytes 393224 | tf_op jit(solution)/shard_map/ppermute | solution.py:861
  151.1 19.0 %copy-start.6 = (f32[8,80,128]{2,1,0:T(8,128)S(1)}, f32[8,80,128]{2,1,0:T(8,128)}, u32[]{:S(2)}) copy-start(f32[8,80,128]{2,1,0:T(8,128)} %copy-done.5) | copy-start | bytes 983044
  151.9 26.4 %all-to-all-start.1 = ((s32[32,1,96]{2,1,0:T(1,128)}), s32[32,1,96]{2,1,0:T(1,128)S(1)}, u32[]{:S(2)}, u32[]{:S(2)}) async-start(s32[32,1,96]{2,1,0:T(1,128)} %bitcast.29), calls=%async_computation.1 | async-start | bytes 32768 | tf_op jit(solution)/shard_map/all_to_all | solution.py:867
  168.9 1.2 copy-start.3
  177.5 0.8 copy-start.10
  178.3 11.2 %copy-start.11 = (bf16[64,4096]{1,0:T(8,128)(2,1)S(1)}, bf16[64,4096]{1,0:T(8,128)(2,1)}, u32[]{:S(2)}) copy-start(bf16[64,4096]{1,0:T(8,128)(2,1)} %copy-done.10) | copy-start | bytes 1572868
  178.3 52.9 %all-to-all-start.2 = ((bf16[32,24,1024]{2,1,0:T(8,128)(2,1)}), bf16[32,24,1024]{2,1,0:T(8,128)(2,1)}, u32[]{:S(2)}, u32[]{:S(2)}) async-start(bf16[32,24,1024]{2,1,0:T(8,128)(2,1)} %bitcast.58), calls=%async_computation.2 | async-start | bytes 3145728 | tf_op jit(solution)/shard_map/all_to_all | solution.py:855
  188.5 24.6 %copy-start.2 = (bf16[4,32,4096]{2,1,0:T(8,128)(2,1)S(1)}, bf16[4,32,4096]{2,1,0:T(8,128)(2,1)}, u32[]{:S(2)}) copy-start(bf16[4,32,4096]{2,1,0:T(8,128)(2,1)} %copy-done) | copy-start | bytes 3145732
  189.5 23.6 %collective-permute-start.16 = (bf16[64,4096]{1,0:T(8,128)(2,1)S(1)}, bf16[64,4096]{1,0:T(8,128)(2,1)S(1)}, u32[]{:S(2)}, u32[]{:S(2)}) collective-permute-start(bf16[64,4096]{1,0:T(8,128)(2,1)S(1)} %copy-done.11), channel_id=1, source_target_pairs={{32,0},{64,32},{96,64},{33,1},{65,33},{97,65},{34,2},{66,34},{98,6... | collective-permute-start | bytes 1572872 | tf_op jit(solution)/shard_map/ppermute | solution.py:860
  191.0 22.1 %collective-permute-start.17 = (bf16[16,4096]{1,0:T(8,128)(2,1)S(1)}, bf16[16,4096]{1,0:T(8,128)(2,1)S(1)}, u32[]{:S(2)}, u32[]{:S(2)}) collective-permute-start(bf16[16,4096]{1,0:T(8,128)(2,1)S(1)} %get-tuple-element.106), channel_id=1, source_target_pairs={{33,0},{34,1},{35,2},{36,3},{37,4},{38,5},{39,6},{40,7},{41,8},{42... | collective-permute-start | bytes 393224 | tf_op jit(solution)/shard_map/ppermute | solution.py:861
  194.5 1.1 copy-start.4
  231.2 29.8 %all-to-all-start = ((bf16[32,24,1024]{2,1,0:T(8,128)(2,1)}), bf16[32,24,1024]{2,1,0:T(8,128)(2,1)S(1)}, u32[]{:S(2)}, u32[]{:S(2)}) async-start(bf16[32,24,1024]{2,1,0:T(8,128)(2,1)} %bitcast.59), calls=%async_computation | async-start | bytes 3145728 | tf_op jit(solution)/shard_map/all_to_all | solution.py:878
